TPU v7x, 32 devices: a whole 2x2x4 slice. The times are simulated.
32 devices in a mesh: dp: 8 (over z, y), rep: 4 (over x, core).
Axes of the slice: x: 2, y: 2, z: 4, core: 2. Of those that a mesh axis runs over, the one named last changes fastest.
Arguments:
- slow_input: bfloat16 [256, 196, 1024], P(('dp', 'rep')), may hold values from -30 to 30
- fast_input: bfloat16 [1024, 196, 128], P(('dp', 'rep')), may hold values from -30 to 30
- clip_ids: int32 [32, 8], P(('dp', 'rep')), may hold values from 0 to 3, never falling along the last dimension, each value on 1 to 5 neighbouring positions
- fast_narrow: bfloat16 [3, 32, 128], replicated, may hold values from -0.3125 to 0.3125
- fast_spatial: bfloat16 [9, 32, 32], replicated, may hold values from -0.375 to 0.375
- fast_widen: bfloat16 [128, 32], replicated, may hold values from -1 to 1
- lateral_conv: bfloat16 [5, 256, 128], replicated, may hold values from -0.25 to 0.25
- slow_narrow: bfloat16 [3, 256, 1280], replicated, may hold values from -0.09375 to 0.09375
- slow_spatial: bfloat16 [9, 256, 256], replicated, may hold values from -0.125 to 0.125
- slow_widen: bfloat16 [1024, 256], replicated, may hold values from -0.375 to 0.375
- norm_gains: float32 [1984], replicated, may hold values from 0.5 to 1.5
- norm_biases: float32 [1984], replicated, may hold values from -2 to 2
- slow_cotangent: bfloat16 [256, 196, 1024], P(('dp', 'rep')), may hold values from -6 to 6
- fast_cotangent: bfloat16 [1024, 196, 128], P(('dp', 'rep')), may hold values from -6 to 6
Outputs:
- slow_output: bfloat16 [256, 196, 1024], P(('dp', 'rep'))
- fast_output: bfloat16 [1024, 196, 128], P(('dp', 'rep'))
- slow_ingrad: bfloat16 [256, 196, 1024], P(('dp', 'rep'))
- fast_ingrad: bfloat16 [1024, 196, 128], P(('dp', 'rep'))
- fnarrow_grad: float32 [3, 32, 128], replicated
- fspatial_grad: float32 [9, 32, 32], replicated
- fwiden_grad: float32 [128, 32], replicated
- lateral_grad: float32 [5, 256, 128], replicated
- snarrow_grad: float32 [3, 256, 1280], replicated
- sspatial_grad: float32 [9, 256, 256], replicated
- swiden_grad: float32 [1024, 256], replicated
- gains_grad: float32 [1984], replicated
- biases_grad: float32 [1984], replicated
Inputs may be any that keep to these rules, and one draw needn't show every extreme that they name: `clip_ids`: row r holds the clip numbers of slow frames r * 8 to r * 8 + 7: never falling, starting at 0, each clip 1 to 5 frames.
All inputs are finite; a program needn't handle non-finite values.
Results may differ from a plain program's by a relative error of at most 0.006.
Values sent between devices are 32-bit elements; how exact they have to be, the bound alone decides.
A program may use at most 256 MiB of HBM per device.

v0:
```python
import math

import jax
import jax.numpy as jnp
from jax import lax
from jax.sharding import PartitionSpec as P

EPS = 1e-05


def shifted(values, axis, offset):
    if offset == 0:
        return values
    size = values.shape[axis]
    widths = [(0, 0)] * values.ndim
    widths[axis] = (max(-offset, 0), max(offset, 0))
    padded = jnp.pad(values, widths)
    return lax.slice_in_dim(padded, max(offset, 0), max(offset, 0) + size, axis=axis)


def clip_mask(rows, offset):
    size = rows.shape[1]
    padded = jnp.pad(rows, ((0, 0), (max(-offset, 0), max(offset, 0))), constant_values=-1)
    moved = lax.slice_in_dim(padded, max(offset, 0), max(offset, 0) + size, axis=1)
    return (moved == rows).astype(jnp.float32)[:, :, None, None]


def column_mask(plane, side, step):
    column = jnp.arange(plane, dtype=jnp.int32) % side
    inside = (column + step >= 0) & (column + step < side)
    return inside.astype(jnp.float32)[None, None, :, None]


def temporal_specs(rows):
    return [(1, offset, clip_mask(rows, offset)) for offset in (-1, 0, 1)]


def spatial_specs(plane):
    side = math.isqrt(plane)
    return [
        (2, row_step * side + col_step, column_mask(plane, side, col_step))
        for row_step in (-1, 0, 1)
        for col_step in (-1, 0, 1)
    ]


def spread_taps(values, specs):
    return jnp.concatenate(
        [
            shifted(values, axis, offset) * valid.astype(values.dtype)
            for axis, offset, valid in specs
        ],
        axis=3,
    )


def fold_taps(pieces, specs):
    total = None
    for piece, (axis, offset, valid) in zip(pieces, specs):
        term = shifted(piece * valid, axis, -offset)
        total = term if total is None else total + term
    return total


def lateral_specs(rows, stride):
    return [
        (
            (tap_index - 2) % stride,
            (tap_index - 2) // stride,
            clip_mask(rows, (tap_index - 2) // stride),
        )
        for tap_index in range(5)
    ]


def lateral_spread(values, specs, frames):
    split = values.reshape(
        values.shape[0], frames, values.shape[1] // frames, values.shape[2], values.shape[3]
    )
    return jnp.concatenate(
        [
            shifted(split[:, :, phase], 1, step) * valid.astype(values.dtype)
            for phase, step, valid in specs
        ],
        axis=3,
    )


def lateral_fold(pieces, specs, stride):
    phases = [jnp.zeros_like(pieces[0]) for unused in range(stride)]
    for piece, (phase, step, valid) in zip(pieces, specs):
        phases[phase] = phases[phase] + shifted(piece * valid, 1, -step)
    joined = jnp.stack(phases, axis=2)
    return joined.reshape(
        joined.shape[0], joined.shape[1] * stride, joined.shape[3], joined.shape[4]
    )


def widen_weight(weight):
    return weight.transpose(0, 2, 1).reshape(weight.shape[0] * weight.shape[2], weight.shape[1])


def apply_conv(weight, stacked):
    return jnp.einsum(
        "gtpk,ko->gtpo", stacked, widen_weight(weight), preferred_element_type=jnp.float32
    )


def conv_back(weight, stacked, grad_out):
    wide = widen_weight(weight)
    grad_wide = jnp.einsum("gtpk,gtpo->ko", stacked, grad_out, preferred_element_type=jnp.float32)
    grad_weight = grad_wide.reshape(weight.shape[0], weight.shape[2], weight.shape[1]).transpose(
        0, 2, 1
    )
    back = jnp.einsum("gtpo,ko->gtpk", grad_out, wide, preferred_element_type=jnp.float32)
    pieces = back.reshape(
        back.shape[0], back.shape[1], back.shape[2], weight.shape[0], weight.shape[2]
    )
    return (grad_weight, [pieces[:, :, :, tap_index] for tap_index in range(weight.shape[0])])


def split_channels(vector, widths):
    pieces = []
    start = 0
    for width in widths:
        pieces.append(vector[start : start + width])
        start = start + width
    return pieces


def channel_row(vector):
    return vector[None, None, None, :]


def silu_slope(values):
    sigma = jax.nn.sigmoid(values)
    return sigma * (1.0 + values * (1.0 - sigma))


def moment_sums(sums, squares):
    return lax.psum((sums, squares), ("dp", "rep"))


def batch_moments(items):
    local_sums = [jnp.sum(values, axis=(0, 1, 2)) for values, count in items]
    local_squares = [jnp.sum(values * values, axis=(0, 1, 2)) for values, count in items]
    totals = [moment_sums(first, second) for first, second in zip(local_sums, local_squares)]
    result = []
    for (values, count), (sums, squares) in zip(items, totals):
        average = sums / count
        spread = squares / count - average * average
        scale = lax.rsqrt(spread + EPS)
        result.append(((values - channel_row(average)) * channel_row(scale), scale))
    return result


def grad_sums(bias_part, gain_part):
    return lax.psum((bias_part, gain_part), ("dp", "rep"))


def batch_back(items):
    local_bias = [jnp.sum(grad_y, axis=(0, 1, 2)) for grad_y, normed, gain, scale, count in items]
    local_gain = [
        jnp.sum(grad_y * normed, axis=(0, 1, 2)) for grad_y, normed, gain, scale, count in items
    ]
    totals = [grad_sums(first, second) for first, second in zip(local_bias, local_gain)]
    result = []
    for (grad_y, normed, gain, scale, count), (bias_total, gain_total) in zip(items, totals):
        grad_in = channel_row(gain * scale) * (
            grad_y - (channel_row(bias_total) + normed * channel_row(gain_total)) / count
        )
        result.append((grad_in, bias_total, gain_total))
    return result


def body(
    slow_input,
    fast_input,
    clip_ids,
    fast_narrow,
    fast_spatial,
    fast_widen,
    lateral_conv,
    slow_narrow,
    slow_spatial,
    slow_widen,
    norm_gains,
    norm_biases,
    slow_cotangent,
    fast_cotangent,
):
    devices = lax.axis_size(("dp", "rep"))
    slow_values = slow_input[None]
    fast_values = fast_input[None]
    frames = slow_values.shape[1]
    stride = fast_values.shape[1] // frames
    plane = slow_values.shape[2]
    slow_count = frames * plane * devices
    fast_count = stride * slow_count
    fast_rows = jnp.repeat(clip_ids, stride, axis=1)
    widths = [
        fast_narrow.shape[1],
        fast_spatial.shape[1],
        fast_widen.shape[0],
        lateral_conv.shape[1],
        slow_narrow.shape[1],
        slow_spatial.shape[1],
        slow_widen.shape[0],
    ]
    gains = split_channels(norm_gains, widths)
    biases = split_channels(norm_biases, widths)
    slow_temporal = temporal_specs(clip_ids)
    fast_temporal = temporal_specs(fast_rows)
    planar = spatial_specs(plane)
    lateral = lateral_specs(clip_ids, stride)
    stack_fa = spread_taps(fast_values, fast_temporal)
    section_fa = apply_conv(fast_narrow, stack_fa)
    stack_lat = lateral_spread(fast_values, lateral, frames)
    section_lat = apply_conv(lateral_conv, stack_lat)
    (normed_fa, scale_fa), (normed_lat, scale_lat) = batch_moments(
        [(section_fa, fast_count), (section_lat, slow_count)]
    )
    pre_fa = normed_fa * channel_row(gains[0]) + channel_row(biases[0])
    hidden_fa = jax.nn.silu(pre_fa).astype(jnp.bfloat16)
    pre_lat = normed_lat * channel_row(gains[3]) + channel_row(biases[3])
    lateral_act = jax.nn.silu(pre_lat).astype(jnp.bfloat16)
    joined = jnp.concatenate([slow_values, lateral_act], axis=3)
    stack_fb = spread_taps(hidden_fa, planar)
    section_fb = apply_conv(fast_spatial, stack_fb)
    stack_sa = spread_taps(joined, slow_temporal)
    section_sa = apply_conv(slow_narrow, stack_sa)
    (normed_fb, scale_fb), (normed_sa, scale_sa) = batch_moments(
        [(section_fb, fast_count), (section_sa, slow_count)]
    )
    pre_fb = normed_fb * channel_row(gains[1]) + channel_row(biases[1])
    hidden_fb = jax.nn.silu(pre_fb).astype(jnp.bfloat16)
    pre_sa = normed_sa * channel_row(gains[4]) + channel_row(biases[4])
    hidden_sa = jax.nn.silu(pre_sa).astype(jnp.bfloat16)
    section_fc = jnp.einsum(
        "gtpc,oc->gtpo", hidden_fb, fast_widen, preferred_element_type=jnp.float32
    )
    stack_sb = spread_taps(hidden_sa, planar)
    section_sb = apply_conv(slow_spatial, stack_sb)
    (normed_fc, scale_fc), (normed_sb, scale_sb) = batch_moments(
        [(section_fc, fast_count), (section_sb, slow_count)]
    )
    fast_sum = (
        fast_values.astype(jnp.float32) + normed_fc * channel_row(gains[2]) + channel_row(biases[2])
    )
    pre_sb = normed_sb * channel_row(gains[5]) + channel_row(biases[5])
    hidden_sb = jax.nn.silu(pre_sb).astype(jnp.bfloat16)
    section_sc = jnp.einsum(
        "gtpc,oc->gtpo", hidden_sb, slow_widen, preferred_element_type=jnp.float32
    )
    ((normed_sc, scale_sc),) = batch_moments([(section_sc, slow_count)])
    slow_sum = (
        slow_values.astype(jnp.float32) + normed_sc * channel_row(gains[6]) + channel_row(biases[6])
    )
    slow_output = jax.nn.silu(slow_sum).astype(jnp.bfloat16)[0]
    fast_output = jax.nn.silu(fast_sum).astype(jnp.bfloat16)[0]
    grad_fast_sum = fast_cotangent[None].astype(jnp.float32) * silu_slope(fast_sum)
    grad_slow_sum = slow_cotangent[None].astype(jnp.float32) * silu_slope(slow_sum)
    (grad_fc, bias_fc, gain_fc), (grad_sc, bias_sc, gain_sc) = batch_back(
        [
            (grad_fast_sum, normed_fc, gains[2], scale_fc, fast_count),
            (grad_slow_sum, normed_sc, gains[6], scale_sc, slow_count),
        ]
    )
    low_fc = grad_fc.astype(jnp.bfloat16)
    low_sc = grad_sc.astype(jnp.bfloat16)
    fwiden_local = jnp.einsum(
        "gtpo,gtpc->oc", low_fc, hidden_fb, preferred_element_type=jnp.float32
    )
    grad_hidden_fb = jnp.einsum(
        "gtpo,oc->gtpc", low_fc, fast_widen, preferred_element_type=jnp.float32
    )
    swiden_local = jnp.einsum(
        "gtpo,gtpc->oc", low_sc, hidden_sb, preferred_element_type=jnp.float32
    )
    grad_hidden_sb = jnp.einsum(
        "gtpo,oc->gtpc", low_sc, slow_widen, preferred_element_type=jnp.float32
    )
    (grad_fb, bias_fb, gain_fb), (grad_sb, bias_sb, gain_sb) = batch_back(
        [
            (grad_hidden_fb * silu_slope(pre_fb), normed_fb, gains[1], scale_fb, fast_count),
            (grad_hidden_sb * silu_slope(pre_sb), normed_sb, gains[5], scale_sb, slow_count),
        ]
    )
    fspatial_local, pieces = conv_back(fast_spatial, stack_fb, grad_fb.astype(jnp.bfloat16))
    grad_hidden_fa = fold_taps(pieces, planar)
    sspatial_local, pieces = conv_back(slow_spatial, stack_sb, grad_sb.astype(jnp.bfloat16))
    grad_hidden_sa = fold_taps(pieces, planar)
    (grad_fa, bias_fa, gain_fa), (grad_sa, bias_sa, gain_sa) = batch_back(
        [
            (grad_hidden_fa * silu_slope(pre_fa), normed_fa, gains[0], scale_fa, fast_count),
            (grad_hidden_sa * silu_slope(pre_sa), normed_sa, gains[4], scale_sa, slow_count),
        ]
    )
    fnarrow_local, pieces = conv_back(fast_narrow, stack_fa, grad_fa.astype(jnp.bfloat16))
    grad_fast_conv = fold_taps(pieces, fast_temporal)
    snarrow_local, pieces = conv_back(slow_narrow, stack_sa, grad_sa.astype(jnp.bfloat16))
    grad_joined = fold_taps(pieces, slow_temporal)
    channels = slow_values.shape[3]
    grad_slow = grad_slow_sum + grad_joined[:, :, :, :channels]
    grad_lateral_act = grad_joined[:, :, :, channels:]
    ((grad_lat, bias_lat, gain_lat),) = batch_back(
        [(grad_lateral_act * silu_slope(pre_lat), normed_lat, gains[3], scale_lat, slow_count)]
    )
    lateral_local, pieces = conv_back(lateral_conv, stack_lat, grad_lat.astype(jnp.bfloat16))
    grad_fast_lat = lateral_fold(pieces, lateral, stride)
    grad_fast = grad_fast_sum + grad_fast_conv + grad_fast_lat
    (
        fnarrow_total,
        fspatial_total,
        fwiden_total,
        lateral_total,
        snarrow_total,
        sspatial_total,
        swiden_total,
    ) = lax.psum(
        (
            fnarrow_local,
            fspatial_local,
            fwiden_local,
            lateral_local,
            snarrow_local,
            sspatial_local,
            swiden_local,
        ),
        ("dp", "rep"),
    )
    factor = 1.0 / math.sqrt(float(slow_count))
    gains_grad = (
        jnp.concatenate([gain_fa, gain_fb, gain_fc, gain_lat, gain_sa, gain_sb, gain_sc]) * factor
    )
    biases_grad = (
        jnp.concatenate([bias_fa, bias_fb, bias_fc, bias_lat, bias_sa, bias_sb, bias_sc]) * factor
    )
    return (
        slow_output,
        fast_output,
        grad_slow.astype(jnp.bfloat16)[0],
        grad_fast.astype(jnp.bfloat16)[0],
        fnarrow_total * factor,
        fspatial_total * factor,
        fwiden_total * factor,
        lateral_total * factor,
        snarrow_total * factor,
        sspatial_total * factor,
        swiden_total * factor,
        gains_grad,
        biases_grad,
    )


def solution(mesh):
    return jax.shard_map(
        body,
        mesh=mesh,
        in_specs=(
            P(("dp", "rep"), None, None),
            P(("dp", "rep"), None, None),
            P(("dp", "rep"), None),
            P(),
            P(),
            P(),
            P(),
            P(),
            P(),
            P(),
            P(),
            P(),
            P(("dp", "rep"), None, None),
            P(("dp", "rep"), None, None),
        ),
        out_specs=(
            P(("dp", "rep"), None, None),
            P(("dp", "rep"), None, None),
            P(("dp", "rep"), None, None),
            P(("dp", "rep"), None, None),
            P(),
            P(),
            P(),
            P(),
            P(),
            P(),
            P(),
            P(),
            P(),
        ),
        check_vma=False,
    )
```

profile of v0, /device:TPU:0, one launch (start us, length us, event | category | flops | bytes accessed | tf_op | source)
XLA Modules:
  0.0 822.5 jit_solution(17245794462391537622)
XLA Ops:
  42.7 42.2 %all-reduce.55 = (f32[256]{0:T(256)S(1)}, f32[256]{0:T(256)S(1)}) all-reduce(f32[256]{0:T(256)} %get-tuple-element.58, f32[256]{0:T(256)} %get-tuple-element.57), channel_id=1, replica_groups=mesh['dp'=8,'rep'=4] {'dp','rep'}, use_global_device_ids=true, to_apply=%region_3.4 | all-reduce | flops 512 | bytes 4096 | tf_op jit(solution)/shard_map/psum | solution.py:141
  94.7 6.8 fusion.160
  101.6 40.4 %all-reduce.54 = (f32[256]{0:T(256)S(1)}, f32[256]{0:T(256)S(1)}, f32[32]{0:T(128)S(1)}, f32[32]{0:T(128)S(1)}) all-reduce(f32[256]{0:T(256)S(1)} %get-tuple-element.56, f32[256]{0:T(256)S(1)} %get-tuple-element.55, f32[32]{0:T(128)S(1)} %copy-done.79, f32[32]{0:T(128)S(1)} %copy-done.78), channel_id=1, replica_groups=mesh['dp'=8,'rep'=4] {'dp','rep'}, use_global_device_ids=true, to_apply=%region_7.8 | all-reduce | flops 576 | bytes 4608 | tf_op jit(solution)/shard_map/psum | solution.py:141
  154.4 40.1 %all-reduce.53 = (f32[256]{0:T(256)S(1)}, f32[256]{0:T(256)S(1)}, f32[32]{0:T(128)S(1)}, f32[32]{0:T(128)S(1)}) all-reduce(f32[256]{0:T(256)S(1)} %get-tuple-element.54, f32[256]{0:T(256)S(1)} %get-tuple-element.53, f32[32]{0:T(128)S(1)} %get-tuple-element.64, f32[32]{0:T(128)S(1)} %get-tuple-element.63), channel_id=1, replica_groups=mesh['dp'=8,'rep'=4] {'dp','rep'}, use_global_device_ids=true, to_apply=%region_11.12 | all-reduce | flops 576 | bytes 4608 | tf_op jit(solution)/shard_map/psum | solution.py:141
  194.7 4.8 fusion.155
  203.6 40.4 %all-reduce.52 = (f32[1024]{0:T(1024)S(1)}, f32[1024]{0:T(1024)S(1)}, f32[128]{0:T(128)S(1)}, f32[128]{0:T(128)S(1)}) all-reduce(f32[1024]{0:T(1024)S(1)} %get-tuple-element.42, f32[1024]{0:T(1024)S(1)} %get-tuple-element.41, f32[128]{0:T(128)S(1)} %get-tuple-element.46, ...), channel_id=1, replica_groups=mesh['dp'=8,'rep'=4] {'dp','rep'}, use_global_device_ids=true, to_apply=%region_15.16 | all-reduce | flops 2304 | bytes 18432 | tf_op jit(solution)/shard_map/psum | solution.py:141
  244.1 5.8 fusion.154
  251.6 9.2 %fusion.152 = (f32[1024]{0:T(1024)S(1)}, f32[1024]{0:T(1024)S(1)}, f32[8,196,1024]{2,1,0:T(8,128)}, bf16[8,196,1024]{2,1,0:T(8,128)(2,1)}) fusion(f32[1024]{0:T(1024)S(1)} %get-tuple-element.170, f32[8,196,1024]{2,1,0:T(8,128)S(1)} %copy-done.6, f32[1024]{0:T(1024)S(1)} %get-tuple-element.178, f32[1024]{0:T(1024)S(1)} %copy-done.58, ...), kind=kLoop, calls=%fused_computation.312 | loop fusion | flops 32110592 | bytes 22503424 | tf_op jit(solution)/shard_map/reduce_sum | solution.py:162
  260.8 40.4 %all-reduce.51 = (f32[1024]{0:T(1024)S(1)}, f32[1024]{0:T(1024)S(1)}, f32[128]{0:T(128)S(1)}, f32[128]{0:T(128)S(1)}) all-reduce(f32[1024]{0:T(1024)S(1)} %get-tuple-element.40, f32[1024]{0:T(1024)S(1)} %get-tuple-element.39, f32[128]{0:T(128)S(1)} %get-tuple-element.44, ...), channel_id=1, replica_groups=mesh['dp'=8,'rep'=4] {'dp','rep'}, use_global_device_ids=true, to_apply=%region_31.32 | all-reduce | flops 2304 | bytes 18432 | tf_op jit(solution)/shard_map/psum | solution.py:158
  308.6 11.2 %reshape.1002 = bf16[3,128,196,32]{1,0,2,3:T(4,128)(2,1)} reshape(bf16[384,196,32]{0,1,2:T(8,128)(2,1)} %fusion.37) | data formatting | bytes 9633792 | tf_op jit(solution)/shard_map/gtpk,gtpo->ko/dot_general | solution.py:111
  319.8 6.7 multiply_convert_fusion
  329.3 40.5 %all-reduce.50 = (f32[256]{0:T(256)S(1)}, f32[256]{0:T(256)S(1)}, f32[32]{0:T(128)S(1)}, f32[32]{0:T(128)S(1)}) all-reduce(f32[256]{0:T(256)S(1)} %get-tuple-element.52, f32[256]{0:T(256)S(1)} %get-tuple-element.51, f32[32]{0:T(128)S(1)} %get-tuple-element.62, f32[32]{0:T(128)S(1)} %get-tuple-element.61), channel_id=1, replica_groups=mesh['dp'=8,'rep'=4] {'dp','rep'}, use_global_device_ids=true, to_apply=%region_35.36 | all-reduce | flops 576 | bytes 4608 | tf_op jit(solution)/shard_map/psum | solution.py:158
  373.0 7.9 convolution_bitcast_fusion.6
  382.2 7.3 convolution_bitcast_fusion.1
  392.8 9.6 %fusion.61 = (f32[1,8,196,256]{3,2,1,0:T(8,128)}, f32[1,8,196,256]{3,2,1,0:T(8,128)}, f32[1,8,196,256]{3,2,1,0:T(8,128)}, f32[1,8,196,256]{3,2,1,0:T(8,128)}, f3...) fusion(f32[1,8,196,9,256]{4,2,1,3,0:T(8,128)} %convolution_bitc, ...), kind=kLoop, calls=%fused_computation.115 | loop fusion | flops 3211264 | bytes 25692464 | tf_op jit(solution)/shard_map/mul | solution.py:60
  402.5 6.0 fusion.162
  410.0 4.9 fusion.157
  414.9 40.0 %all-reduce.49 = (f32[256]{0:T(256)S(1)}, f32[256]{0:T(256)S(1)}, f32[32]{0:T(128)S(1)}, f32[32]{0:T(128)S(1)}) all-reduce(f32[256]{0:T(256)S(1)} %get-tuple-element.50, f32[256]{0:T(256)S(1)} %get-tuple-element.49, f32[32]{0:T(128)S(1)} %get-tuple-element.60, f32[32]{0:T(128)S(1)} %get-tuple-element.59), channel_id=1, replica_groups=mesh['dp'=8,'rep'=4] {'dp','rep'}, use_global_device_ids=true, to_apply=%region_39.40 | all-reduce | flops 576 | bytes 4608 | tf_op jit(solution)/shard_map/psum | solution.py:158
  456.9 9.9 %convolution_bitcast_fusion = f32[1,8,196,3,1280]{4,2,1,3,0:T(8,128)} fusion(bf16[8,196,256,1]{2,1,0,3:T(8,128)(2,1)S(1)} %fusion.110, bf16[3,256,1280]{1,2,0:T(8,128)(2,1)S(1)} %copy-done.20), kind=kOutput, calls=%fused_computation | convolution fusion | flops 3082813440 | bytes 26853376 | tf_op jit(solution)/shard_map/gtpo,ko->gtpk/dot_general | solution.py:115
  466.9 6.5 fusion.8
  473.4 6.4 fusion.7
  484.0 4.5 fusion.73
  488.6 11.1 %fusion.34 = bf16[3840,196,8]{0,1,2:T(8,128)(2,1)} fusion(bf16[1,8,196,1280]{3,2,1,0:T(8,128)(2,1)} %get-tuple-element.152, bf16[1,8,196,256]{3,2,1,0:T(8,128)(2,1)} %copy-done.21, bf16[1,8,196,1024]{3,2,1,0:T(8,128)(2,1)} %bitcast.450, bf16[1,8,196,1280]{3,2,1,0:T(8,128)(2,1)} %get-tuple-element.151), kind=kLoop, calls=%fused_computation.71 | loop fusion | flops 48168960 | bytes 24084480 | tf_op jit(solution)/shard_map/gtpk,gtpo->ko/dot_general | solution.py:111
  499.6 14.5 %reshape.1003 = bf16[3,1280,196,8]{1,0,2,3:T(4,128)(2,1)} reshape(bf16[3840,196,8]{0,1,2:T(8,128)(2,1)} %fusion.34) | data formatting | bytes 24084480 | tf_op jit(solution)/shard_map/gtpk,gtpo->ko/dot_general | solution.py:111
  514.2 13.2 %copy.93 = bf16[2304,196,8]{1,2,0:T(8,128)(2,1)} copy(bf16[2304,196,8]{0,1,2:T(8,128)(2,1)} %bitcast.455) | data formatting | bytes 14450688 | tf_op jit(solution)/shard_map/gtpk,gtpo->ko/dot_general | solution.py:111
  527.4 9.1 %fusion.39 = f32[9,256,256]{1,2,0:T(8,128)} fusion(bf16[8,196,256,1]{2,1,0,3:T(8,128)(2,1)} %copy-done.38, bf16[9,256,196,8]{2,3,1,0:T(8,128)(2,1)} %bitcast.454), kind=kOutput, calls=%fused_computation.83 | convolution fusion | flops 1849688064 | bytes 10387456 | tf_op jit(solution)/shard_map/gtpk,gtpo->ko/dot_general | solution.py:111
  536.5 5.9 fusion.21
  546.7 4.9 copy.89
  551.6 62.6 %all-reduce.60.cloned.1.call-done = (f32[256]{0:T(256)}, f32[256]{0:T(256)}, f32[3,32,128]{2,1,0:T(8,128)}, f32[9,32,32]{1,2,0:T(8,128)}, f32[128,32]{0,1:T(8,128)}) async-done(((f32[256]{0:T(256)}, f32[256]{0:T(256)}, f32[3,32,128]{2,1,0:T(8,128)}, f32[9,32,32]{1,2,0:T(8,128)}, f32[128,32]{0,1:T(8,128)}), (f32[256]{0:T(256)}, f32[256]{0:T(256)}, f32[3,32,128]{2,1,0:T(8,128)}, f32[9,32,32]{1,2,0:T(8,128)}, ...) | async-done | bytes 104464 | tf_op jit(solution)/shard_map/psum | solution.py:158
  619.1 6.1 fusion.29
  656.1 142.3 %all-reduce.62.cloned.1.call-done = (f32[5,256,128]{1,2,0:T(8,128)}, f32[3,256,1280]{1,2,0:T(8,128)}, f32[9,256,256]{1,2,0:T(8,128)}, f32[1024,256]{1,0:T(8,128)}) async-done(((f32[5,256,128]{1,2,0:T(8,128)}, f32[3,256,1280]{1,2,0:T(8,128)}, f32[9,256,256]{1,2,0:T(8,128)}, f32[1024,256]{1,0:T(8,128)}), (f32[5,256,128]{1,2,0:T(8,128)}, f32[3,256,1280]{1,2,0:T(8,128)}, f32[9,256,256]{1,2,0:T(8,128)}, ...) | async-done | bytes 7995408 | tf_op jit(solution)/shard_map/psum | solution.py:320
  810.0 5.4 copy.101
  (271 shorter events, 140.9 us)
Async XLA Ops:
  7.2 192.3 %copy-start = (bf16[1024,256]{1,0:T(8,128)(2,1)S(1)}, bf16[1024,256]{1,0:T(8,128)(2,1)}, u32[]{:S(2)}) copy-start(bf16[1024,256]{1,0:T(8,128)(2,1)} %param.23) | copy-start | bytes 1572868
  7.2 607.0 %all-reduce.60.cloned.1.call-start = ((), (), s32[]{:S(2)}) async-start(), calls=%async_computation | async-start | bytes 430080 | tf_op jit(solution)/shard_map/psum | solution.py:158
  16.6 14.3 %copy-start.63 = (bf16[8]{0:T(256)(128)(2,1)}, bf16[8]{0:T(256)(128)(2,1)S(1)}, u32[]{:S(2)}) copy-start(bf16[8]{0:T(256)(128)(2,1)S(1)} %get-tuple-element.193) | copy-start | bytes 52
  22.2 19.1 %copy-start.48 = (bf16[5,256,128]{1,2,0:T(8,128)(2,1)}, bf16[5,256,128]{1,2,0:T(8,128)(2,1)S(1)}, u32[]{:S(2)}) copy-start(bf16[5,256,128]{1,2,0:T(8,128)(2,1)S(1)} %copy.66) | copy-start | bytes 983044
  31.5 9.9 %copy-start.41 = (bf16[1,8,196,640]{3,2,1,0:T(8,128)(2,1)}, bf16[1,8,196,640]{3,2,1,0:T(8,128)(2,1)S(1)}, u32[]{:S(2)}) copy-start(bf16[1,8,196,640]{3,2,1,0:T(8,128)(2,1)S(1)} %constant_dynamic-update-slice_fusion) | copy-start | bytes 6021124
  42.7 47.0 %copy-start.9 = (f32[8,196,256]{2,1,0:T(8,128)}, f32[8,196,256]{2,1,0:T(8,128)S(1)}, u32[]{:S(2)}) copy-start(f32[8,196,256]{2,1,0:T(8,128)S(1)} %get-tuple-element.195) | copy-start | bytes 4816900
  86.9 7.2 copy-start.21
  94.7 47.2 %copy-start.65 = (f32[32]{0:T(128)S(1)}, f32[32]{0:T(128)}, u32[]{:S(2)}) copy-start(f32[32]{0:T(128)} %get-tuple-element.172) | copy-start | bytes 388
  94.7 47.3 %copy-start.67 = (f32[32]{0:T(128)S(1)}, f32[32]{0:T(128)}, u32[]{:S(2)}) copy-start(f32[32]{0:T(128)} %slice.324) | copy-start | bytes 388
  151.0 43.5 %copy-start.60 = (f32[1984]{0:T(1024)S(1)}, f32[1984]{0:T(1024)}, u32[]{:S(2)}) copy-start(f32[1984]{0:T(1024)} %param.24) | copy-start | bytes 23812
  151.0 43.6 %copy-start.77 = (f32[32]{0:T(128)S(1)}, f32[32]{0:T(128)}, u32[]{:S(2)}) copy-start(f32[32]{0:T(128)} %get-tuple-element.171) | copy-start | bytes 388
  151.1 43.6 %copy-start.80 = (bf16[128,32]{0,1:T(8,128)(2,1)S(1)}, bf16[128,32]{0,1:T(8,128)(2,1)}, u32[]{:S(2)}) copy-start(bf16[128,32]{0,1:T(8,128)(2,1)} %param.19) | copy-start | bytes 24580
  199.4 44.6 %copy-start.76 = (f32[128]{0:T(128)S(1)}, f32[128]{0:T(128)}, u32[]{:S(2)}) copy-start(f32[128]{0:T(128)} %slice.337) | copy-start | bytes 1540
  244.1 7.5 copy-start.15
  244.1 7.5 copy-start.58
  326.5 43.3 %copy-start.51 = (bf16[9,32,32]{2,1,0:T(8,128)(2,1)S(1)}, bf16[9,32,32]{2,1,0:T(8,128)(2,1)}, u32[]{:S(2)}) copy-start(bf16[9,32,32]{2,1,0:T(8,128)(2,1)} %param.18) | copy-start | bytes 55300
  373.0 16.5 %copy-start.3 = (f32[1,32,196,9,32]{2,4,1,3,0:T(8,128)}, f32[1,32,196,9,32]{2,4,1,3,0:T(8,128)S(1)}, u32[]{:S(2)}) copy-start(f32[1,32,196,9,32]{2,4,1,3,0:T(8,128)S(1)} %convolution_bitcast_fusion.3) | copy-start | bytes 21676036
  373.0 7.9 copy-start.45
  373.0 7.9 copy-start.47
  382.2 7.3 copy-start.38
  382.2 7.3 copy-start.61
  382.2 7.3 copy-start.68
  402.5 7.0 copy-start.28
  402.5 7.5 copy-start.29
  456.9 9.9 %copy-start.39 = (bf16[8,196,256,1]{2,1,0,3:T(8,128)(2,1)}, bf16[8,196,256,1]{2,1,0,3:T(8,128)(2,1)S(1)}, u32[]{:S(2)}) copy-start(bf16[8,196,256,1]{2,1,0,3:T(8,128)(2,1)S(1)} %fusion.110) | copy-start | bytes 2408452
  456.9 9.9 %copy-start.66 = (f32[8]{0:T(128)S(1)}, f32[8]{0:T(128)}, u32[]{:S(2)}) copy-start(f32[8]{0:T(128)} %get-tuple-element.194) | copy-start | bytes 100
  456.9 9.9 %copy-start.71 = (f32[8]{0:T(128)S(1)}, f32[8]{0:T(128)}, u32[]{:S(2)}) copy-start(f32[8]{0:T(128)} %get-tuple-element.112) | copy-start | bytes 100
  488.5 309.9 %all-reduce.62.cloned.1.call-start = ((), (), s32[]{:S(2)}) async-start(), calls=%async_computation.1 | async-start | bytes 15990784 | tf_op jit(solution)/shard_map/psum | solution.py:320
  527.4 9.1 %copy-start.8 = (bf16[3,1280,196,8]{1,0,2,3:T(4,128)(2,1)S(1)}, bf16[3,1280,196,8]{1,0,2,3:T(4,128)(2,1)}, u32[]{:S(2)}) copy-start(bf16[3,1280,196,8]{1,0,2,3:T(4,128)(2,1)} %reshape.1003) | copy-start | bytes 36126724
  527.4 9.1 %copy-start.40 = (bf16[8,196,256,1]{2,1,0,3:T(8,128)(2,1)S(1)}, bf16[8,196,256,1]{2,1,0,3:T(8,128)(2,1)}, u32[]{:S(2)}) copy-start(bf16[8,196,256,1]{2,1,0,3:T(8,128)(2,1)} %copy-done.39) | copy-start | bytes 2408452
  619.1 7.5 copy-start.11
  805.7 9.8 %copy-start.1 = (bf16[1024,256]{1,0:T(8,128)(2,1)S(1)}, bf16[1024,256]{1,0:T(8,128)(2,1)}, u32[]{:S(2)}) copy-start(bf16[1024,256]{1,0:T(8,128)(2,1)} %param.23) | copy-start | bytes 1572868
  (51 other events, 209.4 us)
Sparse Core Ops, SparseCore 0:
  488.6 125.5 all-reduce.59
  621.7 176.6 all-reduce.61
where the time goes:
time: 838 us; the launch traced here: 823 us
  blocking collectives  284 us (34%)
  waiting for transfers between devices  205 us (24%)
  other arithmetic  129 us (15%)
  local copies, waits for them, and re-layouts  101 us (12%)
  matrix products  89 us (11%)
  between operations  15.1 us (2%)
    psum x4, blocking collectives, moment_sums(): return lax.psum((sums, squares), ('dp', 'rep'))  163 us
    psum x1, waiting for transfers between devices, body(): lax.psum((fnarrow_local, fspatial_local, fwiden_local, lateral_local, sna...  142 us
    psum x3, blocking collectives, grad_sums(): return lax.psum((bias_part, gain_part), ('dp', 'rep'))  121 us
    psum x1, waiting for transfers between devices, grad_sums(): return lax.psum((bias_part, gain_part), ('dp', 'rep'))  62.6 us
    unnamed x177, local copies, waits for them, and re-layouts  45.8 us
    dot_general x4, local copies, waits for them, and re-layouts, conv_back(): jnp.einsum('gtpk,gtpo->ko', stacked, grad_out, preferred_element_type=jnp...  43.8 us
    reduce_sum x5, other arithmetic, batch_back(): jnp.sum(grad_y, axis=(0, 1, 2))  30 us
    dot_general x5, matrix products, conv_back(): jnp.einsum('gtpk,gtpo->ko', stacked, grad_out, preferred_element_type=jnp...  29.4 us
  transfers between devices with their start and end apart: 2, of which 2 were waited for; matrix products, arithmetic and copies ran while one was open for 11% of the time, Pallas kernels for 0%

commit v1 on v0

v1 whole, which is shorter than its diff:
```python
import functools
import math

import jax
import jax.numpy as jnp
from jax import lax
from jax.experimental import pallas as pl
from jax.experimental.pallas import tpu as pltpu
from jax.sharding import PartitionSpec as P

EPS = 1e-05
F32 = jnp.float32
BF16 = jnp.bfloat16
MESH = pl.DeviceIdType.MESH
NN = ((1,), (0,))
NT = ((1,), (1,))
TN = ((0,), (0,))
LANES = 128
ROWS = (8, 8, 8, 16, 24, 8, 8, 8)


def dot(left, right, dims):
    return lax.dot_general(left, right, (dims, ((), ())), preferred_element_type=F32)


def sigmoid(values):
    return 0.5 * jnp.tanh(0.5 * values) + 0.5


def column_sums(values):
    return jnp.sum(values.reshape(values.shape[0] // 8, 8, values.shape[1]), axis=0)


def squash(partial):
    return jnp.sum(partial, axis=0, keepdims=True)


def fold_lanes(values):
    half = values + pltpu.roll(values, 64, 1)
    return half + pltpu.roll(half, 32, 1)


def loop(count, body, init=None):
    if init is None:

        def plain(index, carry):
            body(index)
            return carry

        lax.fori_loop(0, count, plain, 0)
        return None
    return lax.fori_loop(0, count, body, init)


def rows_at(index, size):
    return pl.ds(pl.multiple_of(index * size, 16), size)


def kernel(
    dims,
    xs_h, xf_h, cs_h, cf_h, clip, wfa_h, wfb_h, wfc_h, wl_h, wsa_h, wsb_h, wsc_h, gains_in, biases_in,
    slow_h, fast_h, sgrad_h, fgrad_h, dsa_h, dsb, dsc, dl, dfa, dfb, dfc, dgains, dbiases,
    xs, cs, gsum, xf, cf, big, sec_fc, gsf, hcs, gcs, hcf, gcf,
    sec_lat, sec_sa, sec_sb, dbuf, sec_fa, sec_fb, dbuf_f, jl, hbs, hbf, vx, dsa2,
    wsa, wsb, wsc, wl, wfa_in, wfb_in, wfc_in, wlat, wfa, wfb, wfbk, wfc,
    stage_a, stage_b, gain_rows, bias_rows, near_s, near_l, far_s, far_l, near_send, near_recv, far_send, far_recv, io_sem,
):
    n_dp, n_rep, low, frames, side, slow_count, fast_count, factor = dims
    rows = xs.shape[0]
    half = rows // 2
    band = side * frames
    bands = side
    fband = 4 * band
    cs_n = xs.shape[1]
    bs = wsb.shape[1]

    dp_i, rep_i = lax.axis_index("dp"), lax.axis_index("rep")
    dp_lo, dp_hi = lax.rem(dp_i, low), lax.div(dp_i, low)
    high = n_dp // low
    near_rank = dp_lo * n_rep + rep_i
    near_peers = [
        (dp_hi * low + lax.rem(dp_lo + a, low), lax.rem(rep_i + b, n_rep))
        for a in range(low)
        for b in range(n_rep)
        if a or b
    ]
    far_rank = dp_hi
    far_peers = [(lax.rem(dp_hi + a, high) * low + dp_lo, rep_i) for a in range(1, high)]

    barrier = pltpu.get_barrier_semaphore()
    for peer in near_peers + far_peers:
        pl.semaphore_signal(barrier, inc=1, device_id=peer, device_id_type=MESH)

    loads = {}
    for slot, (name, src, dst) in enumerate([
        ("xf", xf_h, xf), ("wfa", wfa_h, wfa_in), ("wl", wl_h, wl), ("xs", xs_h, xs),
        ("wsa", wsa_h, wsa), ("wfb", wfb_h, wfb_in), ("wfc", wfc_h, wfc_in), ("wsb", wsb_h, wsb),
        ("wsc", wsc_h, wsc), ("cf", cf_h, cf), ("cs", cs_h, cs),
    ]):
        loads[name] = pltpu.make_async_copy(src, dst, io_sem.at[slot])
        loads[name].start()
    stores = []

    def store(src, dst, slot):
        copy = pltpu.make_async_copy(src, dst, io_sem.at[slot])
        copy.start()
        return copy

    slots, counts = [], {8: 0, 24: 0}
    for size in ROWS:
        wide = 8 if size == 8 else 24
        slots.append((near_s, far_s, counts[wide]) if wide == 8 else (near_l, far_l, counts[wide]))
        counts[wide] += 1

    def put(turn, at, vector):
        near, far, slot = slots[turn]
        for piece in range(vector.shape[1] // LANES):
            near[slot, near_rank, pl.ds(at + piece, 1), :] = vector[:, piece * LANES : (piece + 1) * LANES]

    def near_copy(turn, first, count, peer):
        near, far, slot = slots[turn]
        span = near.at[slot, pl.ds(first, count), pl.ds(0, ROWS[turn])]
        return pltpu.make_async_remote_copy(
            src_ref=span, dst_ref=span, send_sem=near_send.at[turn], recv_sem=near_recv.at[turn],
            device_id=peer, device_id_type=MESH,
        )

    def far_copy(turn, first, count, peer):
        near, far, slot = slots[turn]
        span = far.at[slot, pl.ds(first, count), pl.ds(0, ROWS[turn])]
        return pltpu.make_async_remote_copy(
            src_ref=span, dst_ref=span, send_sem=far_send.at[turn], recv_sem=far_recv.at[turn],
            device_id=peer, device_id_type=MESH,
        )

    def exchange_start(turn):
        for peer in near_peers:
            near_copy(turn, near_rank, 1, peer).start()

    def exchange_middle(turn):
        near, far, slot = slots[turn]
        size = ROWS[turn]
        near_copy(turn, 0, len(near_peers), near_peers[0]).wait_recv()
        far[slot, far_rank, pl.ds(0, size), :] = jnp.sum(near[slot, :, pl.ds(0, size), :], axis=0)
        for peer in far_peers:
            far_copy(turn, far_rank, 1, peer).start()

    def exchange_end(turn):
        near, far, slot = slots[turn]
        size = ROWS[turn]
        far_copy(turn, 0, len(far_peers), far_peers[0]).wait_recv()
        total = jnp.sum(far[slot, :, pl.ds(0, size), :], axis=0)
        near_copy(turn, 0, len(near_peers), near_peers[0]).wait_send()
        far_copy(turn, 0, len(far_peers), far_peers[0]).wait_send()
        return total

    def take(total, at, width):
        pieces = [total[at + piece : at + piece + 1, :] for piece in range(width // LANES)]
        return pieces[0] if len(pieces) == 1 else jnp.concatenate(pieces, axis=1)

    def repeat4(vector):
        return jnp.concatenate([vector] * 4, axis=1)

    spots = {"fc": 0, "lat": 1, "sa": 3, "sb": 5, "sc": 7, "fa": 16, "fb": 17}

    lane16 = lax.broadcasted_iota(jnp.int32, (16, LANES), 1)

    def unpack(packed):
        fa = fold_lanes(jnp.where(lane16 // 32 == 0, packed, 0.0))[0:1, :]
        fb = fold_lanes(jnp.where(lane16 // 32 == 1, packed, 0.0))[0:1, :]
        turned = pltpu.roll(packed, 64, 1)
        moved = jnp.where(lane16 < 64, turned, pltpu.roll(turned, 15, 0))
        vectors = {"fa": fa, "fb": fb}
        at = 0
        for name, count in (("fc", 1), ("lat", 2), ("sa", 2), ("sb", 2), ("sc", 8)):
            vectors[name] = take(moved, at, count * LANES)
            at += count
        return vectors

    gains, biases = unpack(gains_in[...]), unpack(biases_in[...])

    def gain(name):
        return gains[name]

    def bias(name):
        return biases[name]

    def moments(total, squares, count):
        mean = total * (1.0 / count)
        return mean, lax.rsqrt(squares * (1.0 / count) - mean * mean + EPS)

    def back_vectors(name, stats, bias_total, gain_total, count):
        mean, scale = stats
        lead = gain(name) * scale
        tilt = lead * scale * gain_total * (1.0 / count)
        level = lead * bias_total * (1.0 / count) - mean * tilt
        return lead, level, tilt

    def report(name, bias_total, gain_total):
        at = spots[name]
        for piece in range(bias_total.shape[1] // LANES):
            lanes = slice(piece * LANES, (piece + 1) * LANES)
            gain_rows[at + piece : at + piece + 1, :] = gain_total[:, lanes]
            bias_rows[at + piece : at + piece + 1, :] = bias_total[:, lanes]

    def before_act(values, stats, name):
        mean, scale = stats
        normed = (values - mean) * scale
        return normed, normed * gain(name) + bias(name)

    def clip_masks(width):
        frame = lax.broadcasted_iota(jnp.int32, (1, 8, width), 1)
        with_prev = jnp.zeros((1, 8, width), F32)
        with_next = jnp.zeros((1, 8, width), F32)
        for t in range(1, frames):
            same = jnp.where(clip[0, t] == clip[0, t - 1], 1.0, 0.0)
            with_prev = jnp.where(frame == t, same, with_prev)
            with_next = jnp.where(frame == t - 1, same, with_next)
        return with_prev, with_next

    def roll_frames(values, mask, step, mask_first):
        grouped = values.reshape(values.shape[0] // 8, 8, values.shape[1])
        if mask_first:
            grouped = grouped * mask
        grouped = pltpu.roll(grouped, step % 8, 1)
        if not mask_first:
            grouped = grouped * mask
        return grouped.reshape(values.shape)

    def spread_columns(target, index, values):
        width = values.shape[1]
        nothing = jnp.zeros((frames, width), F32)
        at = pl.ds(pl.multiple_of((index + 1) * band, 16), band)
        target[at, 0:width] = jnp.concatenate([nothing, values[: band - frames]], axis=0).astype(BF16)
        target[at, width : 2 * width] = values.astype(BF16)
        target[at, 2 * width :] = jnp.concatenate([values[frames:], nothing], axis=0).astype(BF16)

    gain_rows[...] = jnp.zeros(gain_rows.shape, F32)
    bias_rows[...] = jnp.zeros(bias_rows.shape, F32)
    for target in (hcs, gcs, hcf, gcf):
        edge = jnp.zeros((band, target.shape[1]), BF16)
        target[0:band, :] = edge
        target[band + rows : rows + 2 * band, :] = edge

    lane_group = lax.broadcasted_iota(jnp.int32, (LANES, LANES), 1) // 32
    row_group = lax.broadcasted_iota(jnp.int32, (LANES, LANES), 0) // 32
    block_mask = jnp.where(lane_group == row_group, 1.0, 0.0)
    repeat_lanes = jnp.where(
        lax.broadcasted_iota(jnp.int32, (32, LANES), 1) % 32 == lax.broadcasted_iota(jnp.int32, (32, LANES), 0),
        1.0, 0.0,
    ).astype(BF16)

    wfa[...] = jnp.zeros(wfa.shape, BF16)
    loads["wfa"].wait()
    for phase in range(4):
        for k in range(3):
            wfa[32 * phase : 32 * (phase + 1), LANES * (phase + k) : LANES * (phase + k + 1)] = wfa_in[
                32 * k : 32 * (k + 1), :
            ]
    prev128, next128 = clip_masks(128)
    loads["xf"].wait()

    def arrange(i):
        at = rows_at(i, band)
        stage_a[...] = xf[rows_at(i, fband), :].astype(F32)
        phases = [stage_a[pl.ds(phase, band, stride=4), :] for phase in range(4)]
        vx[at, 0:128] = roll_frames(phases[2], prev128, 1, False).astype(BF16)
        vx[at, 128:256] = roll_frames(phases[3], prev128, 1, False).astype(BF16)
        for phase in range(4):
            vx[at, 256 + 128 * phase : 384 + 128 * phase] = phases[phase].astype(BF16)
        vx[at, 768:896] = roll_frames(phases[0], next128, -1, False).astype(BF16)

    loop(bands, arrange)
    loads["wl"].wait()
    for k in range(5):
        wlat[:, LANES * k : LANES * (k + 1)] = wl[bs * k : bs * (k + 1), :]

    def zero2(width):
        return (jnp.zeros((8, width), F32), jnp.zeros((8, width), F32))

    def conv_fa(i, carry):
        at = rows_at(i, half)
        value = dot(vx[at, 128:896], wfa[...], NT)
        sec_fa[at, :] = value
        return carry[0] + column_sums(value), carry[1] + column_sums(value * value)

    def conv_lat(i, carry):
        at = rows_at(i, half)
        value = dot(vx[at, 0:640], wlat[...], NT)
        sec_lat[at, :] = value
        return carry[0] + column_sums(value), carry[1] + column_sums(value * value)

    sum_fa, sq_fa = loop(2, conv_fa, zero2(128))
    sum_lat, sq_lat = loop(2, conv_lat, zero2(256))
    put(0, 0, squash(sum_fa))
    put(0, 1, squash(sq_fa))
    put(0, 2, squash(sum_lat))
    put(0, 4, squash(sq_lat))
    pl.semaphore_wait(barrier, len(near_peers) + len(far_peers))
    exchange_start(0)

    loads["xs"].wait()
    loads["wsa"].wait()

    def narrow_main(i):
        at = rows_at(i, half)
        for k in range(3):
            big[at, bs * k : bs * (k + 1)] = dot(xs[at, :], wsa[bs * k : bs * (k + 1), 0:cs_n], NT)

    loop(2, narrow_main)
    exchange_middle(0)
    loads["wfb"].wait()
    loads["wfc"].wait()
    spread = dot(wfb_in[...], repeat_lanes, NN)
    for a in range(3):
        for b in range(3):
            piece = spread[32 * (3 * a + b) : 32 * (3 * a + b + 1), :]
            block = (jnp.concatenate([piece] * 4, axis=0) * block_mask).astype(BF16)
            wfb[a, :, LANES * b : LANES * (b + 1)] = block
            wfbk[a, LANES * (2 - b) : LANES * (3 - b), :] = block
    widen = dot(wfc_in[...], repeat_lanes, TN)
    for phase in range(4):
        wfc[LANES * phase : LANES * (phase + 1), :] = jnp.where(lane_group == phase, widen, 0.0).astype(BF16)
    total = exchange_end(0)

    fa_rows = fold_lanes(total[0:8, :])
    stats_fa = moments(fa_rows[0:1, :], fa_rows[1:2, :], fast_count)
    stats_lat = moments(take(total, 2, 256), take(total, 4, 256), slow_count)

    def act_fa(i):
        normed, pre = before_act(sec_fa[rows_at(i, band), :], stats_fa, "fa")
        spread_columns(hcf, i, pre * sigmoid(pre))

    def act_lat(i):
        at = rows_at(i, band)
        normed, pre = before_act(sec_lat[at, :], stats_lat, "lat")
        jl[at, :] = (pre * sigmoid(pre)).astype(BF16)

    loop(bands, act_fa)
    loop(bands, act_lat)

    def conv_fb(i, carry):
        value = None
        for a in range(3):
            at = pl.ds(pl.multiple_of(i * half + band * a, 16), half)
            term = dot(hcf[at, :], wfb[a], NT)
            value = term if value is None else value + term
        sec_fb[rows_at(i, half), :] = value
        return carry[0] + column_sums(value), carry[1] + column_sums(value * value)

    sum_fb, sq_fb = loop(2, conv_fb, zero2(128))

    def narrow_lateral(i):
        at = rows_at(i, half)
        for k in range(3):
            big[at, bs * k : bs * (k + 1)] += dot(jl[at, :], wsa[bs * k : bs * (k + 1), cs_n:], NT)

    loop(2, narrow_lateral)
    prev256, next256 = clip_masks(256)

    def combine_sa(i, carry):
        at = rows_at(i, band)
        value = (
            big[at, bs : 2 * bs]
            + roll_frames(big[at, 0:bs], prev256, 1, False)
            + roll_frames(big[at, 2 * bs : 3 * bs], next256, -1, False)
        )
        sec_sa[at, :] = value
        return carry[0] + column_sums(value), carry[1] + column_sums(value * value)

    sum_sa, sq_sa = loop(bands, combine_sa, zero2(256))
    put(1, 0, squash(sum_fb))
    put(1, 1, squash(sq_fb))
    put(1, 2, squash(sum_sa))
    put(1, 4, squash(sq_sa))
    exchange_start(1)
    exchange_middle(1)
    total = exchange_end(1)

    fb_rows = fold_lanes(total[0:8, :])
    stats_fb = moments(fb_rows[0:1, :], fb_rows[1:2, :], fast_count)
    stats_sa = moments(take(total, 2, 256), take(total, 4, 256), slow_count)

    def act_sa(i):
        normed, pre = before_act(sec_sa[rows_at(i, band), :], stats_sa, "sa")
        spread_columns(hcs, i, pre * sigmoid(pre))

    def act_fb(i):
        at = rows_at(i, band)
        normed, pre = before_act(sec_fb[at, :], stats_fb, "fb")
        hbf[at, :] = (pre * sigmoid(pre)).astype(BF16)

    loop(bands, act_sa)
    loads["wsb"].wait()

    def conv_sb(i, carry):
        value = None
        for a in range(3):
            at = pl.ds(pl.multiple_of(i * half + band * a, 16), half)
            for b in range(3):
                tap = 3 * a + b
                term = dot(hcs[at, bs * b : bs * (b + 1)], wsb[bs * tap : bs * (tap + 1), :], NT)
                value = term if value is None else value + term
        sec_sb[rows_at(i, half), :] = value
        return carry[0] + column_sums(value), carry[1] + column_sums(value * value)

    sum_sb, sq_sb = loop(2, conv_sb, zero2(256))
    loop(bands, act_fb)

    def widen_fast(i, carry):
        at = rows_at(i, half)
        value = dot(hbf[at, :], wfc[...], NT)
        sec_fc[at, :] = value
        return carry[0] + column_sums(value), carry[1] + column_sums(value * value)

    sum_fc, sq_fc = loop(2, widen_fast, zero2(512))

    def fold4(vector):
        return vector[:, 0:128] + vector[:, 128:256] + vector[:, 256:384] + vector[:, 384:512]

    put(2, 0, squash(fold4(sum_fc)))
    put(2, 1, squash(fold4(sq_fc)))
    put(2, 2, squash(sum_sb))
    put(2, 4, squash(sq_sb))
    exchange_start(2)
    exchange_middle(2)
    total = exchange_end(2)

    stats_fc = moments(take(total, 0, 128), take(total, 1, 128), fast_count)
    stats_sb = moments(take(total, 2, 256), take(total, 4, 256), slow_count)

    def act_sb(i):
        at = rows_at(i, band)
        normed, pre = before_act(sec_sb[at, :], stats_sb, "sb")
        hbs[at, :] = (pre * sigmoid(pre)).astype(BF16)

    loop(bands, act_sb)
    loads["wsc"].wait()

    def widen_slow(i, carry):
        at = rows_at(i, half)
        value = dot(hbs[at, :], wsc[...], NT)
        big[at, :] = value
        return carry[0] + column_sums(value), carry[1] + column_sums(value * value)

    sum_sc, sq_sc = loop(2, widen_slow, zero2(cs_n))
    put(3, 0, squash(sum_sc))
    put(3, 8, squash(sq_sc))
    exchange_start(3)

    loads["cf"].wait()

    def finish_fast(i, carry):
        at, fat = rows_at(i, band), rows_at(i, fband)
        bias_sum, gain_sum = carry
        stage_b[...] = cf[fat, :].astype(F32)
        for phase in range(4):
            lanes = slice(128 * phase, 128 * (phase + 1))
            mean, scale = stats_fc
            normed = (sec_fc[at, lanes] - mean) * scale
            total_in = vx[at, 256 + 128 * phase : 384 + 128 * phase].astype(F32)
            value = total_in + normed * gain("fc") + bias("fc")
            gate = sigmoid(value)
            stage_a[pl.ds(phase, band, stride=4), :] = value * gate
            grad = stage_b[pl.ds(phase, band, stride=4), :] * (gate * (1.0 + value * (1.0 - gate)))
            gsf[at, lanes] = grad
            bias_sum = bias_sum + column_sums(grad)
            gain_sum = gain_sum + column_sums(grad * normed)
        xf[fat, :] = stage_a[...].astype(BF16)
        return bias_sum, gain_sum

    bias_fc, gain_fc = loop(bands, finish_fast, zero2(128))
    fast_store = store(xf, fast_h, 11)
    exchange_middle(3)
    loads["cs"].wait()
    total = exchange_end(3)

    stats_sc = moments(take(total, 0, cs_n), take(total, 8, cs_n), slow_count)
    thin = 32

    def finish_slow(i, carry):
        at = rows_at(i, thin)
        normed, shift = before_act(big[at, :], stats_sc, "sc")
        value = xs[at, :].astype(F32) + shift
        gate = sigmoid(value)
        grad = cs[at, :].astype(F32) * (gate * (1.0 + value * (1.0 - gate)))
        cs[at, :] = (value * gate).astype(BF16)
        gsum[at, :] = normed.astype(BF16)
        big[at, :] = grad
        return carry[0] + column_sums(grad), carry[1] + column_sums(grad * normed)

    bias_sc, gain_sc = loop(rows // thin, finish_slow, zero2(cs_n))
    slow_store = store(cs, slow_h, 12)
    put(4, 0, squash(bias_sc))
    put(4, 8, squash(gain_sc))
    put(4, 16, squash(bias_fc))
    put(4, 17, squash(gain_fc))
    exchange_start(4)
    exchange_middle(4)
    total = exchange_end(4)

    bias_sc, gain_sc = take(total, 0, cs_n), take(total, 8, cs_n)
    bias_fc, gain_fc = take(total, 16, 128), take(total, 17, 128)
    report("sc", bias_sc, gain_sc)
    report("fc", bias_fc, gain_fc)
    lead_sc = gain("sc") * stats_sc[1]
    level_sc = lead_sc * bias_sc * (1.0 / slow_count)
    tilt_sc = lead_sc * gain_sc * (1.0 / slow_count)
    slow_store.wait()

    def low_sc(i):
        at = rows_at(i, thin)
        grad = big[at, :]
        cs[at, :] = (grad * lead_sc - level_sc - gsum[at, :].astype(F32) * tilt_sc).astype(BF16)
        gsum[at, :] = grad.astype(BF16)

    loop(rows // thin, low_sc)

    def back_sc(i):
        at = rows_at(i, half)
        dbuf[at, :] = dot(cs[at, :], wsc[...], NN)

    loop(2, back_sc)

    def slope_pass(section, stats, name, buffer):
        def step(i, carry):
            at = rows_at(i, band)
            normed, pre = before_act(section[at, :], stats, name)
            gate = sigmoid(pre)
            grad = buffer[at, :] * (gate * (1.0 + pre * (1.0 - gate)))
            buffer[at, :] = grad
            return carry[0] + column_sums(grad), carry[1] + column_sums(grad * normed)

        return loop(bands, step, zero2(section.shape[1]))

    bias_sb, gain_sb = slope_pass(sec_sb, stats_sb, "sb", dbuf)

    mean_fc, scale_fc = stats_fc
    lead_fc = gain("fc") * scale_fc
    tilt_fc = lead_fc * scale_fc * gain_fc * (1.0 / fast_count)
    level_fc = lead_fc * bias_fc * (1.0 / fast_count) - mean_fc * tilt_fc

    def low_fc(i):
        at = rows_at(i, band)
        for phase in range(4):
            lanes = slice(128 * phase, 128 * (phase + 1))
            value = gsf[at, lanes] * lead_fc - level_fc - sec_fc[at, lanes] * tilt_fc
            cf[pl.ds(pl.multiple_of(rows * phase + i * band, 16), band), :] = value.astype(BF16)

    loop(bands, low_fc)

    def back_fc(i):
        value = None
        for phase in range(4):
            at = pl.ds(pl.multiple_of(rows * phase + i * half, 16), half)
            term = dot(cf[at, :], wfc[128 * phase : 128 * (phase + 1), :], NN)
            value = term if value is None else value + term
        dbuf_f[rows_at(i, half), :] = value

    loop(2, back_fc)
    bias_fb, gain_fb = slope_pass(sec_fb, stats_fb, "fb", dbuf_f)
    put(5, 0, squash(bias_fb))
    put(5, 1, squash(gain_fb))
    put(5, 2, squash(bias_sb))
    put(5, 4, squash(gain_sb))
    exchange_start(5)

    dsc[...] = dot(cs[...], hbs[...], TN)
    exchange_middle(5)
    wide = None
    for phase in range(4):
        term = jnp.where(
            lane_group == phase, dot(cf[rows * phase : rows * (phase + 1), :], hbf[...], TN), 0.0
        )
        wide = term if wide is None else wide + term
    dfc[...] = fold_lanes(wide)
    total = exchange_end(5)

    fold_rows = fold_lanes(total[0:8, :])
    bias_fb, gain_fb = fold_rows[0:1, :], fold_rows[1:2, :]
    bias_sb, gain_sb = take(total, 2, 256), take(total, 4, 256)
    report("fb", bias_fb, gain_fb)
    report("sb", bias_sb, gain_sb)
    vec_sb = back_vectors("sb", stats_sb, bias_sb, gain_sb, slow_count)
    vec_fb = back_vectors("fb", stats_fb, bias_fb, gain_fb, fast_count)

    def norm_grad(buffer, section, at, vectors):
        lead, level, tilt = vectors
        return buffer[at, :] * lead - level - section[at, :] * tilt

    def low_sb(i):
        spread_columns(gcs, i, norm_grad(dbuf, sec_sb, rows_at(i, band), vec_sb))

    loop(bands, low_sb)

    def back_sb(i):
        value = None
        for a in range(3):
            at = pl.ds(pl.multiple_of(i * half + band * (2 - a), 16), half)
            for b in range(3):
                tap = 3 * a + b
                term = dot(gcs[at, bs * (2 - b) : bs * (3 - b)], wsb[bs * tap : bs * (tap + 1), :], NN)
                value = term if value is None else value + term
        dbuf[rows_at(i, half), :] = value

    loop(2, back_sb)
    bias_sa, gain_sa = slope_pass(sec_sa, stats_sa, "sa", dbuf)

    def low_fb(i):
        spread_columns(gcf, i, norm_grad(dbuf_f, sec_fb, rows_at(i, band), vec_fb))

    loop(bands, low_fb)

    def back_fb(i):
        value = None
        for a in range(3):
            at = pl.ds(pl.multiple_of(i * half + band * (2 - a), 16), half)
            term = dot(gcf[at, :], wfbk[a], NN)
            value = term if value is None else value + term
        dbuf_f[rows_at(i, half), :] = value

    loop(2, back_fb)
    bias_fa, gain_fa = slope_pass(sec_fa, stats_fa, "fa", dbuf_f)
    put(6, 0, squash(bias_fa))
    put(6, 1, squash(gain_fa))
    put(6, 2, squash(bias_sa))
    put(6, 4, squash(gain_sa))
    exchange_start(6)

    for a in range(3):
        value = dot(gcs[band : band + rows, bs : 2 * bs], hcs[band * a : band * a + rows, :], TN)
        for b in range(3):
            tap = 3 * a + b
            dsb[bs * tap : bs * (tap + 1), :] = value[:, bs * b : bs * (b + 1)]
    exchange_middle(6)
    for a in range(3):
        value = dot(gcf[band : band + rows, 128:256], hcf[band * a : band * a + rows, :], TN)
        for b in range(3):
            tap = 3 * a + b
            block = value[:, 128 * b : 128 * (b + 1)] * block_mask
            piece = block[0:32] + block[32:64] + block[64:96] + block[96:128]
            dfb[32 * tap : 32 * (tap + 1), :] = fold_lanes(piece)
    total = exchange_end(6)

    fold_rows = fold_lanes(total[0:8, :])
    bias_fa, gain_fa = fold_rows[0:1, :], fold_rows[1:2, :]
    bias_sa, gain_sa = take(total, 2, 256), take(total, 4, 256)
    report("fa", bias_fa, gain_fa)
    report("sa", bias_sa, gain_sa)
    vec_sa = back_vectors("sa", stats_sa, bias_sa, gain_sa, slow_count)
    vec_fa = back_vectors("fa", stats_fa, bias_fa, gain_fa, fast_count)

    def low_sa(i):
        at = rows_at(i, band)
        value = norm_grad(dbuf, sec_sa, at, vec_sa)
        gcs[at, 0:bs] = roll_frames(value, prev256, -1, True).astype(BF16)
        gcs[at, bs : 2 * bs] = value.astype(BF16)
        gcs[at, 2 * bs :] = roll_frames(value, next256, 1, True).astype(BF16)

    loop(bands, low_sa)

    def back_lateral(i):
        at = rows_at(i, half)
        dbuf[at, :] = dot(gcs[at, :], wsa[:, cs_n:], NN)

    loop(2, back_lateral)
    bias_lat, gain_lat = slope_pass(sec_lat, stats_lat, "lat", dbuf)
    put(7, 0, squash(bias_lat))
    put(7, 2, squash(gain_lat))
    exchange_start(7)

    for tile in range(cs_n // 256):
        lanes = slice(256 * tile, 256 * (tile + 1))
        big[0 : 3 * bs, lanes] = dot(gcs[0:rows, :], xs[:, lanes], TN)
    dsa2[...] = dot(gcs[0:rows, :], jl[...], TN)
    sa_store = store(big.at[pl.ds(0, 3 * bs)], dsa_h.at[:, pl.ds(0, cs_n)], 13)
    sa2_store = store(dsa2, dsa_h.at[:, pl.ds(cs_n, bs)], 14)
    exchange_middle(7)

    def slow_back(i):
        at = rows_at(i, half)
        for tile in range(cs_n // 256):
            lanes = slice(256 * tile, 256 * (tile + 1))
            value = gsum[at, lanes].astype(F32) + dot(gcs[at, :], wsa[:, lanes], NN)
            gsum[at, lanes] = value.astype(BF16)

    loop(2, slow_back)
    sgrad_store = store(gsum, sgrad_h, 15)

    def low_fa(i):
        at = rows_at(i, band)
        hbf[at, :] = norm_grad(dbuf_f, sec_fa, at, vec_fa).astype(BF16)

    loop(bands, low_fa)
    value = dot(hbf[...], vx[:, 128:896], TN)
    for k in range(3):
        piece = None
        for phase in range(4):
            term = value[32 * phase : 32 * (phase + 1), 128 * (phase + k) : 128 * (phase + k + 1)]
            piece = term if piece is None else piece + term
        dfa[32 * k : 32 * (k + 1), :] = piece
    total = exchange_end(7)

    bias_lat, gain_lat = take(total, 0, 256), take(total, 2, 256)
    report("lat", bias_lat, gain_lat)
    vec_lat = back_vectors("lat", stats_lat, bias_lat, gain_lat, slow_count)

    def low_lat(i):
        at = rows_at(i, band)
        hbs[at, :] = norm_grad(dbuf, sec_lat, at, vec_lat).astype(BF16)

    loop(bands, low_lat)
    value = dot(hbs[...], vx[:, 0:640], TN)
    for k in range(5):
        dl[bs * k : bs * (k + 1), :] = value[:, 128 * k : 128 * (k + 1)]
    fast_store.wait()

    def fast_back(i):
        at, fat = rows_at(i, 2 * band), rows_at(i, 2 * fband)
        conv = dot(hbf[at, :], wfa[...], NN)
        side_in = dot(hbs[at, :], wlat[...], NN)

        def lane(values, block):
            return values[:, 128 * block : 128 * (block + 1)]

        grads = [gsf[at, 128 * phase : 128 * (phase + 1)] + lane(conv, phase + 1) for phase in range(4)]
        grads[0] = grads[0] + roll_frames(lane(conv, 5), next128, 1, True) + lane(side_in, 2)
        grads[1] = grads[1] + lane(side_in, 3)
        grads[2] = grads[2] + lane(side_in, 4) + roll_frames(lane(side_in, 0), prev128, -1, True)
        grads[3] = grads[3] + roll_frames(lane(side_in, 1) + lane(conv, 0), prev128, -1, True)
        for part in range(2):
            for phase in range(4):
                stage_a[pl.ds(phase, band, stride=4), :] = grads[phase][part * band : (part + 1) * band]
            xf[rows_at(2 * i + part, fband), :] = stage_a[...].astype(BF16)

    loop(bands // 2, fast_back)
    fgrad_store = store(xf, fgrad_h, 16)

    def pack(rows_ref, target):
        lanes = lax.broadcasted_iota(jnp.int32, (24, LANES), 1)
        stacked = rows_ref[...]
        turned = pltpu.roll(stacked, 64, 1)
        moved = jnp.where(lanes >= 64, turned, pltpu.roll(turned, 1, 0))[0:16, :]
        first = jnp.where(lane16[0:1, :] < 32, stacked[16:17, :], stacked[17:18, :])
        first = jnp.where(lane16[0:1, :] < 64, first, moved[0:1, :])
        target[...] = moved * factor
        target[0:1, :] = first * factor

    pack(gain_rows, dgains)
    pack(bias_rows, dbiases)
    sa_store.wait()
    sa2_store.wait()
    sgrad_store.wait()
    fgrad_store.wait()


def body(
    slow_input,
    fast_input,
    clip_ids,
    fast_narrow,
    fast_spatial,
    fast_widen,
    lateral_conv,
    slow_narrow,
    slow_spatial,
    slow_widen,
    norm_gains,
    norm_biases,
    slow_cotangent,
    fast_cotangent,
):
    n_dp, n_rep = lax.axis_size("dp"), lax.axis_size("rep")
    low = 2 if n_dp % 2 == 0 else 1
    high = n_dp // low
    frames, plane, channels = slow_input.shape
    fast_frames, _, fast_channels = fast_input.shape
    side = math.isqrt(plane)
    rows = frames * plane
    slow_count = rows * n_dp * n_rep
    fast_count = slow_count * (fast_frames // frames)

    def flat(values):
        return values.transpose(1, 0, 2).reshape(values.shape[0] * values.shape[1], values.shape[2])

    def unflat(values, count):
        return values.reshape(plane, count, values.shape[1]).transpose(1, 0, 2)

    widths = [
        fast_narrow.shape[1], fast_spatial.shape[1], fast_widen.shape[0], lateral_conv.shape[1],
        slow_narrow.shape[1], slow_spatial.shape[1], slow_widen.shape[0],
    ]

    def lay_out(vector):
        return jnp.pad(vector, (0, 16 * LANES - vector.shape[0])).reshape(16, LANES)

    cf = fast_channels
    bs = slow_spatial.shape[1]
    band = side * frames
    any_spec = pl.BlockSpec(memory_space=pl.ANY)
    vmem_spec = pl.BlockSpec(memory_space=pltpu.VMEM)
    small = sum(1 for size in ROWS if size == 8)
    large = len(ROWS) - small
    pad = rows + 2 * band

    def shape(dims, dtype):
        return jax.ShapeDtypeStruct(dims, dtype)

    out_shape = [
        shape((rows, channels), BF16), shape((4 * rows, cf), BF16),
        shape((rows, channels), BF16), shape((4 * rows, cf), BF16),
        shape((3 * bs, channels + bs), F32), shape((9 * bs, bs), F32), shape((channels, bs), F32),
        shape((5 * bs, cf), F32), shape((96, cf), F32), shape((288, 128), F32), shape((cf, 128), F32),
        shape((16, LANES), F32), shape((16, LANES), F32),
    ]
    scratch = [
        pltpu.VMEM((rows, channels), BF16), pltpu.VMEM((rows, channels), BF16),
        pltpu.VMEM((rows, channels), BF16), pltpu.VMEM((4 * rows, cf), BF16),
        pltpu.VMEM((4 * rows, cf), BF16), pltpu.VMEM((rows, channels), F32),
        pltpu.VMEM((rows, 512), F32), pltpu.VMEM((rows, 512), F32),
        pltpu.VMEM((pad, 3 * bs), BF16), pltpu.VMEM((pad, 3 * bs), BF16),
        pltpu.VMEM((pad, 384), BF16), pltpu.VMEM((pad, 384), BF16),
        pltpu.VMEM((rows, bs), F32), pltpu.VMEM((rows, bs), F32), pltpu.VMEM((rows, bs), F32),
        pltpu.VMEM((rows, bs), F32),
        pltpu.VMEM((rows, 128), F32), pltpu.VMEM((rows, 128), F32), pltpu.VMEM((rows, 128), F32),
        pltpu.VMEM((rows, bs), BF16), pltpu.VMEM((rows, bs), BF16), pltpu.VMEM((rows, 128), BF16),
        pltpu.VMEM((rows, 896), BF16), pltpu.VMEM((3 * bs, bs), F32),
        pltpu.VMEM((3 * bs, channels + bs), BF16), pltpu.VMEM((9 * bs, bs), BF16),
        pltpu.VMEM((channels, bs), BF16), pltpu.VMEM((5 * bs, cf), BF16),
        pltpu.VMEM((96, cf), BF16), pltpu.VMEM((288, 32), BF16), pltpu.VMEM((32, cf), BF16),
        pltpu.VMEM((bs, 640), BF16), pltpu.VMEM((128, 768), BF16),
        pltpu.VMEM((3, 128, 384), BF16), pltpu.VMEM((3, 384, 128), BF16), pltpu.VMEM((512, 128), BF16),
        pltpu.VMEM((4 * band, cf), F32), pltpu.VMEM((4 * band, cf), F32),
        pltpu.VMEM((24, LANES), F32), pltpu.VMEM((24, LANES), F32),
        pltpu.VMEM((small, low * n_rep, 8, LANES), F32), pltpu.VMEM((large, low * n_rep, 24, LANES), F32),
        pltpu.VMEM((small, high, 8, LANES), F32), pltpu.VMEM((large, high, 24, LANES), F32),
        pltpu.SemaphoreType.DMA((len(ROWS),)), pltpu.SemaphoreType.DMA((len(ROWS),)),
        pltpu.SemaphoreType.DMA((len(ROWS),)), pltpu.SemaphoreType.DMA((len(ROWS),)),
        pltpu.SemaphoreType.DMA((17,)),
    ]
    factor = 1.0 / math.sqrt(float(slow_count))
    results = pl.pallas_call(
        functools.partial(kernel, (n_dp, n_rep, low, frames, side, float(slow_count), float(fast_count), factor)),
        out_shape=out_shape,
        in_specs=[any_spec] * 4 + [pl.BlockSpec(memory_space=pltpu.SMEM)] + [any_spec] * 7 + [vmem_spec] * 2,
        out_specs=[any_spec] * 5 + [vmem_spec] * 8,
        scratch_shapes=scratch,
        compiler_params=pltpu.CompilerParams(
            collective_id=0, has_side_effects=True, vmem_limit_bytes=63 * 2**20
        ),
    )(
        flat(slow_input), flat(fast_input), flat(slow_cotangent), flat(fast_cotangent), clip_ids,
        fast_narrow.reshape(-1, cf), fast_spatial.reshape(-1, 32), fast_widen.T,
        lateral_conv.reshape(-1, cf), slow_narrow.reshape(3 * bs, -1), slow_spatial.reshape(9 * bs, bs),
        slow_widen, lay_out(norm_gains), lay_out(norm_biases),
    )
    slow_out, fast_out, slow_grad, fast_grad, dsa, dsb, dsc, dl, dfa, dfb, dfc, dgains, dbiases = results
    dsa, dsb, dsc, dl, dfa, dfb, dfc = lax.psum(
        (dsa, dsb, dsc, dl, dfa, dfb[:, 0:32], dfc[:, 0:32]), ("dp", "rep")
    )

    def gather(packed):
        return packed.reshape(16 * LANES)[0 : sum(widths)]

    return (
        unflat(slow_out, frames),
        unflat(fast_out, fast_frames),
        unflat(slow_grad, frames),
        unflat(fast_grad, fast_frames),
        (dfa * factor).reshape(fast_narrow.shape),
        (dfb * factor).reshape(fast_spatial.shape),
        dfc * factor,
        (dl * factor).reshape(lateral_conv.shape),
        (dsa * factor).reshape(slow_narrow.shape),
        (dsb * factor).reshape(slow_spatial.shape),
        dsc * factor,
        gather(dgains),
        gather(dbiases),
    )


def solution(mesh):
    sharded = P(("dp", "rep"), None, None)
    return jax.shard_map(
        body,
        mesh=mesh,
        in_specs=(sharded, sharded, P(("dp", "rep"), None)) + (P(),) * 9 + (sharded, sharded),
        out_specs=(sharded,) * 4 + (P(),) * 9,
        check_vma=False,
    )
```

time: 838 us -> 444 us (0.53); the launches traced: 823 us -> 444 us
  blocking collectives: 284 us -> 0 us
  other arithmetic: 129 us -> 13.1 us
  Pallas kernels: 0 us -> 103 us
  waiting for transfers between devices: 205 us -> 301 us
  matrix products: 89 us -> 0 us
  local copies, waits for them, and re-layouts: 101 us -> 12.8 us
    psum x7 -> x0, blocking collectives: 284 us -> none  [the longest x4 163 us: moment_sums(): return lax.psum((sums, squares), ('dp', 'rep'))]
    pallas_call x0 -> x1, Pallas kernels: none -> 103 us  [body(): pl.pallas_call(functools.partial(kernel, (n_dp, n_rep, low, frames, side,...]
    psum x2, waiting for transfers between devices: 205 us -> 300 us  [body(): lax.psum((dsa, dsb, dsc, dl, dfa, dfb[:, 0:32], dfc[:, 0:32]), ('dp', 're...]
    dot_general x21 -> x0, matrix products: 89 us -> none  [the longest x5 29.4 us: conv_back(): jnp.einsum('gtpk,gtpo->ko', stacked, grad_out, preferred_element_type=jnp...]
    dot_general x4 -> x0, local copies, waits for them, and re-layouts: 43.8 us -> none  [conv_back(): jnp.einsum('gtpk,gtpo->ko', stacked, grad_out, preferred_element_type=jnp...]
    unnamed x177 -> x23, local copies, waits for them, and re-layouts: 45.8 us -> 11.4 us
    reduce_sum x5 -> x0, other arithmetic: 30 us -> none  [batch_back(): jnp.sum(grad_y, axis=(0, 1, 2))]
    mul x20 -> x7, other arithmetic: 39 us -> 13.1 us  [the longest x1 4.52 us: body(): dsa * factor]
  transfers between devices with their start and end apart: 2 -> 2, of which waited for: 2 -> 2; matrix products, arithmetic and copies ran while one was open for 11% -> 1% of each run, Pallas kernels for 0% -> 0%
where the time goes in v1:
time: 444 us
  waiting for transfers between devices  301 us (68%)
  Pallas kernels  103 us (23%)
  between operations  14.1 us (3%)
  other arithmetic  13.1 us (3%)
  local copies, waits for them, and re-layouts  12.8 us (3%)
    psum x2, waiting for transfers between devices, body(): lax.psum((dsa, dsb, dsc, dl, dfa, dfb[:, 0:32], dfc[:, 0:32]), ('dp', 're...  300 us
    pallas_call x1, Pallas kernels, body(): pl.pallas_call(functools.partial(kernel, (n_dp, n_rep, low, frames, side,...  103 us
    unnamed x23, local copies, waits for them, and re-layouts  11.4 us
  transfers between devices with their start and end apart: 2, of which 2 were waited for; matrix products, arithmetic and copies ran while one was open for 1% of the time, Pallas kernels for 0%

profile of v1, /device:TPU:0, one launch (start us, length us, event | category | flops | bytes accessed | tf_op | source)
XLA Modules:
  0.0 443.7 jit_solution(7312675460038104524)
XLA Ops:
  7.2 0.0 all-reduce.7.cloned.1.call-start
  7.2 1.3 pad_bitcast_fusion
  8.5 102.8 %shard_map.237 = (bf16[1568,1024]{1,0:T(8,128)(2,1)}, bf16[6272,128]{1,0:T(8,128)(2,1)}, bf16[1568,1024]{1,0:T(8,128)(2,1)}, bf16[6272,128]{1,0:T(8,128)(2,1)}, ...) custom-call(bf16[1568,1024]{1,0:T(8,128)(2,1)} %bitcast.46, ...), custom_call_target="tpu_custom_call" | custom-call | tf_op jit(solution)/shard_map/pallas_call | solution.py:842
  111.3 0.0 all-reduce.7.cloned.1.call-update
  111.4 0.0 all-reduce.9.cloned.1.call-start
  111.4 0.7 all-reduce.9.cloned.1.call-update
  112.1 123.7 %all-reduce.7.cloned.1.call-done = (f32[96,128]{1,0:T(8,128)}, f32[288,32]{1,0:T(8,128)}, f32[128,32]{1,0:T(8,128)}) async-done(((f32[96,128]{1,0:T(8,128)}, f32[288,32]{1,0:T(8,128)}, f32[128,32]{1,0:T(8,128)}), (f32[96,128]{1,0:T(8,128)}, f32[288,32]{1,0:T(8,128)}, f32[128,32]{1,0:T(8,128)})) %all-reduce.7.cloned.1.call-update) | async-done | bytes 102416 | tf_op jit(solution)/shard_map/psum | solution.py:858
  235.8 0.8 broadcast_multiply_fusion.5
  236.7 0.7 copy.27
  237.4 1.4 broadcast_multiply_fusion.6
  238.8 1.6 broadcast_multiply_fusion.4
  240.4 176.5 %all-reduce.9.cloned.1.call-done = (f32[1280,128]{1,0:T(8,128)}, f32[768,1280]{1,0:T(8,128)}, f32[2304,256]{1,0:T(8,128)}, f32[1024,256]{1,0:T(8,128)}) async-done(((f32[1280,128]{1,0:T(8,128)}, f32[768,1280]{1,0:T(8,128)}, f32[2304,256]{1,0:T(8,128)}, f32[1024,256]{1,0:T(8,128)}), (f32[1280,128]{1,0:T(8,128)}, f32[768,1280]{1,0:T(8,128)}, f32[2304,256]{1,0:T(8,128)}, ...) | async-done | bytes 7995408 | tf_op jit(solution)/shard_map/psum | solution.py:858
  416.8 2.0 broadcast_multiply_fusion.3
  418.8 0.0 copy-start.2
  418.8 4.5 %broadcast_multiply_fusion = f32[768,1280]{1,0:T(8,128)} fusion(f32[768,1280]{1,0:T(8,128)} %get-tuple-element.56), kind=kLoop, calls=%fused_computation | loop fusion | flops 983040 | bytes 7864320 | tf_op jit(solution)/shard_map/mul | solution.py:874
  423.3 0.0 copy-done.2
  423.4 0.0 copy-start.5
  423.4 1.6 broadcast_multiply_fusion.1
  425.0 0.0 copy-done.5
  425.0 1.1 broadcast_multiply_fusion.2
  426.1 0.7 copy-done.1
  426.8 1.7 copy.41
  428.5 0.9 copy-done.4
  429.4 1.2 copy.42
  430.5 1.3 copy-done
  431.9 1.7 copy.43
  433.6 0.9 copy-done.3
  434.5 1.2 copy.44
  435.6 0.0 copy-done.7
  435.6 0.6 copy.45
  436.2 0.0 copy-done.6
  436.2 0.6 copy.46
  (6 shorter events, 0.0 us)
Async XLA Ops:
  7.2 228.7 %all-reduce.7.cloned.1.call-start = ((), (), s32[]{:S(2)}) async-start(), calls=%async_computation | async-start | bytes 524288 | tf_op jit(solution)/shard_map/psum | solution.py:858
  111.4 305.5 %all-reduce.9.cloned.1.call-start = ((), (), s32[]{:S(2)}) async-start(), calls=%async_computation.1 | async-start | bytes 15990784 | tf_op jit(solution)/shard_map/psum | solution.py:858
  418.8 4.5 %copy-start.2 = (f32[2304,256]{1,0:T(8,128)S(1)}, f32[2304,256]{1,0:T(8,128)}, u32[]{:S(2)}) copy-start(f32[2304,256]{1,0:T(8,128)} %get-tuple-element.57) | copy-start | bytes 7077892
  423.4 1.6 copy-start.5
  423.4 3.5 copy-start.1
  426.8 2.6 copy-start.4
  429.4 2.5 copy-start
  431.9 2.6 copy-start.3
  434.5 1.2 copy-start.7
  434.5 1.8 copy-start.6
Sparse Core Ops, SparseCore 0:
  111.5 124.3 all-reduce.6
  242.1 174.6 all-reduce.8

commit v2 on v1

--- a/solution.py
+++ b/solution.py
@@ -59,11 +59,11 @@
 def kernel(
     dims,
     xs_h, xf_h, cs_h, cf_h, clip, wfa_h, wfb_h, wfc_h, wl_h, wsa_h, wsb_h, wsc_h, gains_in, biases_in,
-    slow_h, fast_h, sgrad_h, fgrad_h, dsa_h, dsb, dsc, dl, dfa, dfb, dfc, dgains, dbiases,
+    slow_h, fast_h, sgrad_h, fgrad_h, dsa_h, dsb_h, dsc_h, dl_h, dfa, dfb, dfc, dgains, dbiases, extra_h,
     xs, cs, gsum, xf, cf, big, sec_fc, gsf, hcs, gcs, hcf, gcf,
-    sec_lat, sec_sa, sec_sb, dbuf, sec_fa, sec_fb, dbuf_f, jl, hbs, hbf, vx, dsa2,
-    wsa, wsb, wsc, wl, wfa_in, wfb_in, wfc_in, wlat, wfa, wfb, wfbk, wfc,
-    stage_a, stage_b, gain_rows, bias_rows, near_s, near_l, far_s, far_l, near_send, near_recv, far_send, far_recv, io_sem,
+    sec_lat, sec_sa, sec_sb, dbuf, sec_fa, sec_fb, dbuf_f, jl, hbs, hbf, vx, slab, slab_sc, summed, gathered,
+    wsa, wsb, wsc, wfa_in, wfb_in, wfc_in, wlat, wfa, wfb, wfbk, wfc,
+    stage_a, stage_b, gain_rows, bias_rows, near_s, near_l, far_s, far_l, near_send, near_recv, far_send, far_recv, io_sem, own_sem, big_send, big_recv,
 ):
     n_dp, n_rep, low, frames, side, slow_count, fast_count, factor = dims
     rows = xs.shape[0]
@@ -87,18 +87,36 @@
     far_rank = dp_hi
     far_peers = [(lax.rem(dp_hi + a, high) * low + dp_lo, rep_i) for a in range(1, high)]
 
+    c, x = lax.rem(rep_i, 2), lax.div(rep_i, 2)
+    y, z = dp_lo, lax.rem(dp_hi, 4)
+    outer, outers = lax.div(dp_hi, 4), high // 4
+    core_peer = (dp_i, 2 * x + 1 - c)
+    x_peer = (dp_i, 2 * (1 - x) + c)
+    y_peer = (dp_hi * low + 1 - y, rep_i)
+    z_peers = [((outer * 4 + lax.rem(z + k, 4)) * low + y, rep_i) for k in range(1, 4)]
+    outer_peers = [((lax.rem(outer + k, outers) * 4 + z) * low + y, rep_i) for k in range(1, outers)]
+
     barrier = pltpu.get_barrier_semaphore()
     for peer in near_peers + far_peers:
         pl.semaphore_signal(barrier, inc=1, device_id=peer, device_id_type=MESH)
 
     loads = {}
     for slot, (name, src, dst) in enumerate([
-        ("xf", xf_h, xf), ("wfa", wfa_h, wfa_in), ("wl", wl_h, wl), ("xs", xs_h, xs),
+        ("xf", xf_h, xf), ("wfa", wfa_h, wfa_in), ("xs", xs_h, xs),
         ("wsa", wsa_h, wsa), ("wfb", wfb_h, wfb_in), ("wfc", wfc_h, wfc_in), ("wsb", wsb_h, wsb),
         ("wsc", wsc_h, wsc), ("cf", cf_h, cf), ("cs", cs_h, cs),
     ]):
         loads[name] = pltpu.make_async_copy(src, dst, io_sem.at[slot])
         loads[name].start()
+        if name == "wfa":
+            taps = [
+                pltpu.make_async_copy(
+                    wl_h.at[pl.ds(bs * k, bs)], wlat.at[:, pl.ds(LANES * k, LANES)], io_sem.at[27 + k]
+                )
+                for k in range(5)
+            ]
+            for tap in taps:
+                tap.start()
     stores = []
 
     def store(src, dst, slot):
@@ -160,6 +178,174 @@
 
     def repeat4(vector):
         return jnp.concatenate([vector] * 4, axis=1)
+
+    pieces = {}
+
+    def add_piece(name, ref, lane, size, index):
+        pieces[name] = {"name": name, "ref": ref, "lane": lane, "size": size, "index": index, "step": 0}
+
+    for k in range(2):
+        add_piece("sb%d" % k, sec_fc, 256 * k, 768, k)
+    for k in range(4):
+        add_piece("sa%d" % k, big, 256 * k, 768, 2 + k)
+    add_piece("sb2", slab.at[0], 0, 768, 6)
+    add_piece("sa4", slab.at[1], 0, 768, 7)
+    add_piece("lt", slab.at[2], 0, 768, 8)
+    add_piece("sc", slab_sc, 0, 1024, 9)
+
+    def span(piece, start, count, lane=0, width=256):
+        return piece["ref"].at[pl.ds(pl.multiple_of(start, 8), count), pl.ds(piece["lane"] + lane, width)]
+
+    def send(piece, step, src, dst, peer):
+        pltpu.make_async_remote_copy(
+            src_ref=src, dst_ref=dst, send_sem=big_send.at[piece["index"], step],
+            recv_sem=big_recv.at[piece["index"], step], device_id=peer, device_id_type=MESH,
+        ).start()
+
+    def result(piece, start, count, lane=0, width=256):
+        name = piece["name"]
+        start = pl.multiple_of(start, 8)
+        if name == "lt":
+            return summed.at[pl.ds(start, count), pl.ds(lane, width)]
+        if name == "sc":
+            return dsc_h.at[pl.ds(start, count), pl.ds(lane, width)]
+        k = int(name[2])
+        if name[1] == "a":
+            return dsa_h.at[pl.ds(start, count), pl.ds(256 * k + lane, width)]
+        return dsb_h.at[pl.ds(768 * k + start, count), pl.ds(lane, width)]
+
+    def own_copies(piece, a, b, t):
+        sem = own_sem.at[piece["index"]]
+        return (
+            pltpu.make_async_copy(span(piece, a, t, 0, 128), result(piece, a, t, 0, 128), sem.at[0]),
+            pltpu.make_async_copy(span(piece, b, t, 128, 128), result(piece, b, t, 128, 128), sem.at[1]),
+        )
+
+    def arrived(piece, step, rows_in):
+        block = span(piece, 0, rows_in) if step < 4 else result(piece, 0, rows_in)
+        copy = pltpu.make_async_remote_copy(
+            src_ref=block, dst_ref=block, send_sem=big_send.at[piece["index"], step],
+            recv_sem=big_recv.at[piece["index"], step], device_id=core_peer, device_id_type=MESH,
+        )
+        copy.wait_recv()
+        copy.wait_send()
+
+    def add_rows(piece, target, source, count, lane, width):
+        lanes = pl.ds(piece["lane"] + lane, width)
+        chunk = piece["size"] // 32
+        ref = piece["ref"]
+
+        def step(i):
+            into = pl.ds(pl.multiple_of(target + i * chunk, 8), chunk)
+            ref[into, lanes] = ref[into, lanes] + ref[pl.ds(pl.multiple_of(source + i * chunk, 8), chunk), lanes]
+
+        loop(count // chunk, step)
+
+    order = ["sc", "sb0", "sb1", "sb2", "sa0", "sa1", "sa2", "sa3", "sa4", "lt"]
+
+    def unpack_small():
+        stores.append(store(summed.at[:, pl.ds(0, 128)], dl_h.at[pl.ds(0, 768)], 16))
+        stores.append(store(summed.at[pl.ds(0, 512), pl.ds(128, 128)], dl_h.at[pl.ds(768, 512)], 17))
+        dfa[...] = summed[512:608, 128:256]
+        for tap in range(9):
+            at = 608 + 32 * (tap // 4)
+            block = summed[at : at + 32, 128:256]
+            dfb[32 * tap : 32 * (tap + 1), :] = block[:, 32 * (tap % 4) : 32 * (tap % 4 + 1)]
+        dfc[...] = summed[704:736, 128:256]
+
+    def advance(name):
+        piece = pieces[name]
+        size, step = piece["size"], piece["step"]
+        piece["step"] = step + 1
+        h, q, o, t = size // 2, size // 4, size // 8, size // 32
+        mine = c * h
+        a1, a1o = mine + x * q, mine + (1 - x) * q
+        b1, b1o = mine + y * q, mine + (1 - y) * q
+        a2, a2o = a1 + y * o, a1 + (1 - y) * o
+        b2, b2o = b1 + x * o, b1 + (1 - x) * o
+        from_core, from_one, from_two = size, size + h, size + h + q
+        from_z = size + h + q + o
+        if step == 0:
+            send(piece, 0, span(piece, (1 - c) * h, h), span(piece, from_core, h), core_peer)
+        elif step == 1:
+            arrived(piece, 0, h)
+            add_rows(piece, mine, from_core, h, 0, 256)
+            send(piece, 1, span(piece, a1o, q, 0, 128), span(piece, from_one, q, 0, 128), x_peer)
+            send(piece, 1, span(piece, b1o, q, 128, 128), span(piece, from_one, q, 128, 128), y_peer)
+        elif step == 2:
+            arrived(piece, 1, q)
+            add_rows(piece, a1, from_one, q, 0, 128)
+            add_rows(piece, b1, from_one, q, 128, 128)
+            send(piece, 2, span(piece, a2o, o, 0, 128), span(piece, from_two, o, 0, 128), y_peer)
+            send(piece, 2, span(piece, b2o, o, 128, 128), span(piece, from_two, o, 128, 128), x_peer)
+        elif step == 3:
+            arrived(piece, 2, o)
+            add_rows(piece, a2, from_two, o, 0, 128)
+            add_rows(piece, b2, from_two, o, 128, 128)
+            for k, peer in enumerate(z_peers):
+                at, into = lax.rem(z + k + 1, 4) * t, from_z + k * t
+                send(piece, 3, span(piece, a2 + at, t, 0, 128), span(piece, into, t, 0, 128), peer)
+                send(piece, 3, span(piece, b2 + at, t, 128, 128), span(piece, into, t, 128, 128), peer)
+        elif step == 4:
+            arrived(piece, 3, 3 * t)
+            ref, lane = piece["ref"], piece["lane"]
+            own_a = (pl.ds(pl.multiple_of(a2 + z * t, 8), t), pl.ds(lane, 128))
+            own_b = (pl.ds(pl.multiple_of(b2 + z * t, 8), t), pl.ds(lane + 128, 128))
+            both = jnp.concatenate([ref[own_a], ref[own_b]], axis=1)
+            for k in range(3):
+                both = both + ref[pl.ds(from_z + k * t, t), pl.ds(lane, 256)]
+            if outers > 1:
+                index = piece["index"]
+                held = span(piece, from_z, t)
+                ref[pl.ds(from_z, t), pl.ds(lane, 256)] = both
+                for peer in outer_peers:
+                    send(piece, 8, held, extra_h.at[index, outer, pl.ds(0, t)], peer)
+                block = extra_h.at[index, pl.ds(0, outers - 1), pl.ds(0, t)]
+                copy = pltpu.make_async_remote_copy(
+                    src_ref=block, dst_ref=block, send_sem=big_send.at[index, 8], recv_sem=big_recv.at[index, 8],
+                    device_id=core_peer, device_id_type=MESH,
+                )
+                copy.wait_recv()
+                copy.wait_send()
+                for src, dst in (
+                    (held, extra_h.at[index, outer, pl.ds(0, t)]),
+                    (extra_h.at[index], gathered),
+                ):
+                    copy = pltpu.make_async_copy(src, dst, own_sem.at[index, 0])
+                    copy.start()
+                    copy.wait()
+                both = jnp.sum(gathered[:, pl.ds(0, t), :], axis=0)
+            both = both * factor
+            ref[own_a] = both[:, 0:128]
+            ref[own_b] = both[:, 128:256]
+            own = (a2 + z * t, 0), (b2 + z * t, 128)
+            for peer in z_peers:
+                for at, half_lanes in own:
+                    send(piece, 4, span(piece, at, t, half_lanes, 128), result(piece, at, t, half_lanes, 128), peer)
+            for copy in own_copies(piece, own[0][0], own[1][0], t):
+                copy.start()
+        elif step == 5:
+            arrived(piece, 4, 3 * t)
+            for copy in own_copies(piece, a2 + z * t, b2 + z * t, t):
+                copy.wait()
+            block = result(piece, a2, o, 0, 128)
+            send(piece, 5, block, block, y_peer)
+            block = result(piece, b2, o, 128, 128)
+            send(piece, 5, block, block, x_peer)
+        elif step == 6:
+            arrived(piece, 5, o)
+            block = result(piece, a1, q, 0, 128)
+            send(piece, 6, block, block, x_peer)
+            block = result(piece, b1, q, 128, 128)
+            send(piece, 6, block, block, y_peer)
+        elif step == 7:
+            arrived(piece, 6, q)
+            block = result(piece, mine, h)
+            send(piece, 7, block, block, core_peer)
+        elif step == 8:
+            arrived(piece, 7, h)
+            if name == "lt":
+                unpack_small()
 
     spots = {"fc": 0, "lat": 1, "sa": 3, "sb": 5, "sc": 7, "fa": 16, "fb": 17}
 
@@ -271,9 +457,8 @@
         vx[at, 768:896] = roll_frames(phases[0], next128, -1, False).astype(BF16)
 
     loop(bands, arrange)
-    loads["wl"].wait()
-    for k in range(5):
-        wlat[:, LANES * k : LANES * (k + 1)] = wl[bs * k : bs * (k + 1), :]
+    for tap in taps:
+        tap.wait()
 
     def zero2(width):
         return (jnp.zeros((8, width), F32), jnp.zeros((8, width), F32))
@@ -470,7 +655,7 @@
         return bias_sum, gain_sum
 
     bias_fc, gain_fc = loop(bands, finish_fast, zero2(128))
-    fast_store = store(xf, fast_h, 11)
+    fast_store = store(xf, fast_h, 10)
     exchange_middle(3)
     loads["cs"].wait()
     total = exchange_end(3)
@@ -490,7 +675,7 @@
         return carry[0] + column_sums(grad), carry[1] + column_sums(grad * normed)
 
     bias_sc, gain_sc = loop(rows // thin, finish_slow, zero2(cs_n))
-    slow_store = store(cs, slow_h, 12)
+    slow_store = store(cs, slow_h, 11)
     put(4, 0, squash(bias_sc))
     put(4, 8, squash(gain_sc))
     put(4, 16, squash(bias_fc))
@@ -565,15 +750,16 @@
     put(5, 4, squash(gain_sb))
     exchange_start(5)
 
-    dsc[...] = dot(cs[...], hbs[...], TN)
+    slab_sc[0:cs_n, :] = dot(cs[...], hbs[...], TN)
+    advance("sc")
     exchange_middle(5)
-    wide = None
+    widening = None
     for phase in range(4):
-        term = jnp.where(
-            lane_group == phase, dot(cf[rows * phase : rows * (phase + 1), :], hbf[...], TN), 0.0
-        )
-        wide = term if wide is None else wide + term
-    dfc[...] = fold_lanes(wide)
+        term = dot(hbf[...], cf[rows * phase : rows * (phase + 1), :], TN)[32 * phase : 32 * (phase + 1), :]
+        widening = term if widening is None else widening + term
+    slab[2, 704:736, 128:256] = widening
+    slab[2, 736:768, 128:256] = jnp.zeros((32, LANES), F32)
+    advance("sc")
     total = exchange_end(5)
 
     fold_rows = fold_lanes(total[0:8, :])
@@ -592,6 +778,7 @@
         spread_columns(gcs, i, norm_grad(dbuf, sec_sb, rows_at(i, band), vec_sb))
 
     loop(bands, low_sb)
+    advance("sc")
 
     def back_sb(i):
         value = None
@@ -604,12 +791,14 @@
         dbuf[rows_at(i, half), :] = value
 
     loop(2, back_sb)
+    advance("sc")
     bias_sa, gain_sa = slope_pass(sec_sa, stats_sa, "sa", dbuf)
 
     def low_fb(i):
         spread_columns(gcf, i, norm_grad(dbuf_f, sec_fb, rows_at(i, band), vec_fb))
 
     loop(bands, low_fb)
+    advance("sc")
 
     def back_fb(i):
         value = None
@@ -629,17 +818,24 @@
 
     for a in range(3):
         value = dot(gcs[band : band + rows, bs : 2 * bs], hcs[band * a : band * a + rows, :], TN)
+        ref, lane = pieces["sb%d" % a]["ref"], pieces["sb%d" % a]["lane"]
         for b in range(3):
-            tap = 3 * a + b
-            dsb[bs * tap : bs * (tap + 1), :] = value[:, bs * b : bs * (b + 1)]
+            ref[bs * b : bs * (b + 1), lane : lane + bs] = value[:, bs * b : bs * (b + 1)]
+        advance("sb%d" % a)
     exchange_middle(6)
+    advance("sc")
+    advance("sb0")
     for a in range(3):
         value = dot(gcf[band : band + rows, 128:256], hcf[band * a : band * a + rows, :], TN)
         for b in range(3):
             tap = 3 * a + b
             block = value[:, 128 * b : 128 * (b + 1)] * block_mask
-            piece = block[0:32] + block[32:64] + block[64:96] + block[96:128]
-            dfb[32 * tap : 32 * (tap + 1), :] = fold_lanes(piece)
+            folded = fold_lanes(block[0:32] + block[32:64] + block[64:96] + block[96:128])
+            folded = jnp.where(lane_group[0:32] == tap % 4, folded, 0.0)
+            at = slice(608 + 32 * (tap // 4), 640 + 32 * (tap // 4))
+            slab[2, at, 128:256] = folded if tap % 4 == 0 else slab[2, at, 128:256] + folded
+    advance("sb1")
+    advance("sb2")
     total = exchange_end(6)
 
     fold_rows = fold_lanes(total[0:8, :])
@@ -659,6 +855,14 @@
 
     loop(bands, low_sa)
 
+    def narrow_gradient(k):
+        ref, lane = pieces["sa%d" % k]["ref"], pieces["sa%d" % k]["lane"]
+        source = xs[:, 256 * k : 256 * (k + 1)] if k < 4 else jl[...]
+        ref[0 : 3 * bs, lane : lane + 256] = dot(gcs[0:rows, :], source, TN)
+        advance("sa%d" % k)
+
+    narrow_gradient(0)
+
     def back_lateral(i):
         at = rows_at(i, half)
         dbuf[at, :] = dot(gcs[at, :], wsa[:, cs_n:], NN)
@@ -669,13 +873,17 @@
     put(7, 2, squash(gain_lat))
     exchange_start(7)
 
-    for tile in range(cs_n // 256):
-        lanes = slice(256 * tile, 256 * (tile + 1))
-        big[0 : 3 * bs, lanes] = dot(gcs[0:rows, :], xs[:, lanes], TN)
-    dsa2[...] = dot(gcs[0:rows, :], jl[...], TN)
-    sa_store = store(big.at[pl.ds(0, 3 * bs)], dsa_h.at[:, pl.ds(0, cs_n)], 13)
-    sa2_store = store(dsa2, dsa_h.at[:, pl.ds(cs_n, bs)], 14)
+    for name in ("sc", "sb0", "sb1", "sb2", "sa0"):
+        advance(name)
+    narrow_gradient(1)
+    narrow_gradient(2)
     exchange_middle(7)
+    for name in ("sb0", "sb1", "sb2", "sa0", "sa1", "sa2"):
+        advance(name)
+    narrow_gradient(3)
+    narrow_gradient(4)
+    for name in ("sc", "sb0", "sb1", "sb2", "sa0", "sa1", "sa2", "sa3", "sa4"):
+        advance(name)
 
     def slow_back(i):
         at = rows_at(i, half)
@@ -685,7 +893,7 @@
             gsum[at, lanes] = value.astype(BF16)
 
     loop(2, slow_back)
-    sgrad_store = store(gsum, sgrad_h, 15)
+    sgrad_store = store(gsum, sgrad_h, 12)
 
     def low_fa(i):
         at = rows_at(i, band)
@@ -698,7 +906,7 @@
         for phase in range(4):
             term = value[32 * phase : 32 * (phase + 1), 128 * (phase + k) : 128 * (phase + k + 1)]
             piece = term if piece is None else piece + term
-        dfa[32 * k : 32 * (k + 1), :] = piece
+        slab[2, 512 + 32 * k : 544 + 32 * k, 128:256] = piece
     total = exchange_end(7)
 
     bias_lat, gain_lat = take(total, 0, 256), take(total, 2, 256)
@@ -712,7 +920,11 @@
     loop(bands, low_lat)
     value = dot(hbs[...], vx[:, 0:640], TN)
     for k in range(5):
-        dl[bs * k : bs * (k + 1), :] = value[:, 128 * k : 128 * (k + 1)]
+        at, lane = 256 * (k % 3), 128 * (k // 3)
+        slab[2, at : at + 256, lane : lane + 128] = value[:, 128 * k : 128 * (k + 1)]
+    advance("lt")
+    for name in ("sb0", "sb1", "sb2", "sa0", "sa1", "sa2", "sa3", "sa4", "lt"):
+        advance(name)
     fast_store.wait()
 
     def fast_back(i):
@@ -734,8 +946,9 @@
             xf[rows_at(2 * i + part, fband), :] = stage_a[...].astype(BF16)
 
     loop(bands // 2, fast_back)
-    fgrad_store = store(xf, fgrad_h, 16)
-
+    fgrad_store = store(xf, fgrad_h, 13)
+    for name in ("sb0", "sb1", "sb2", "sa0", "sa1", "sa2", "sa3", "sa4", "lt"):
+        advance(name)
     def pack(rows_ref, target):
         lanes = lax.broadcasted_iota(jnp.int32, (24, LANES), 1)
         stacked = rows_ref[...]
@@ -748,8 +961,12 @@
 
     pack(gain_rows, dgains)
     pack(bias_rows, dbiases)
-    sa_store.wait()
-    sa2_store.wait()
+    while any(piece["step"] <= 8 for piece in pieces.values()):
+        for name in order:
+            if pieces[name]["step"] <= 8:
+                advance(name)
+    for slot, copy in enumerate(stores):
+        copy.wait()
     sgrad_store.wait()
     fgrad_store.wait()
 
@@ -810,8 +1027,9 @@
         shape((rows, channels), BF16), shape((4 * rows, cf), BF16),
         shape((rows, channels), BF16), shape((4 * rows, cf), BF16),
         shape((3 * bs, channels + bs), F32), shape((9 * bs, bs), F32), shape((channels, bs), F32),
-        shape((5 * bs, cf), F32), shape((96, cf), F32), shape((288, 128), F32), shape((cf, 128), F32),
+        shape((5 * bs, cf), F32), shape((96, cf), F32), shape((288, 32), F32), shape((32, cf), F32),
         shape((16, LANES), F32), shape((16, LANES), F32),
+        shape((10, max(high // 4, 1), 32, 256), F32),
     ]
     scratch = [
         pltpu.VMEM((rows, channels), BF16), pltpu.VMEM((rows, channels), BF16),
@@ -824,9 +1042,10 @@
         pltpu.VMEM((rows, bs), F32),
         pltpu.VMEM((rows, 128), F32), pltpu.VMEM((rows, 128), F32), pltpu.VMEM((rows, 128), F32),
         pltpu.VMEM((rows, bs), BF16), pltpu.VMEM((rows, bs), BF16), pltpu.VMEM((rows, 128), BF16),
-        pltpu.VMEM((rows, 896), BF16), pltpu.VMEM((3 * bs, bs), F32),
+        pltpu.VMEM((rows, 896), BF16), pltpu.VMEM((3, 1512, 256), F32), pltpu.VMEM((2016, 256), F32),
+        pltpu.VMEM((768, 256), F32), pltpu.VMEM((max(high // 4, 1), 32, 256), F32),
         pltpu.VMEM((3 * bs, channels + bs), BF16), pltpu.VMEM((9 * bs, bs), BF16),
-        pltpu.VMEM((channels, bs), BF16), pltpu.VMEM((5 * bs, cf), BF16),
+        pltpu.VMEM((channels, bs), BF16),
         pltpu.VMEM((96, cf), BF16), pltpu.VMEM((288, 32), BF16), pltpu.VMEM((32, cf), BF16),
         pltpu.VMEM((bs, 640), BF16), pltpu.VMEM((128, 768), BF16),
         pltpu.VMEM((3, 128, 384), BF16), pltpu.VMEM((3, 384, 128), BF16), pltpu.VMEM((512, 128), BF16),
@@ -836,17 +1055,18 @@
         pltpu.VMEM((small, high, 8, LANES), F32), pltpu.VMEM((large, high, 24, LANES), F32),
         pltpu.SemaphoreType.DMA((len(ROWS),)), pltpu.SemaphoreType.DMA((len(ROWS),)),
         pltpu.SemaphoreType.DMA((len(ROWS),)), pltpu.SemaphoreType.DMA((len(ROWS),)),
-        pltpu.SemaphoreType.DMA((17,)),
+        pltpu.SemaphoreType.DMA((32,)), pltpu.SemaphoreType.DMA((10, 2)),
+        pltpu.SemaphoreType.DMA((10, 9)), pltpu.SemaphoreType.DMA((10, 9)),
     ]
     factor = 1.0 / math.sqrt(float(slow_count))
     results = pl.pallas_call(
         functools.partial(kernel, (n_dp, n_rep, low, frames, side, float(slow_count), float(fast_count), factor)),
         out_shape=out_shape,
         in_specs=[any_spec] * 4 + [pl.BlockSpec(memory_space=pltpu.SMEM)] + [any_spec] * 7 + [vmem_spec] * 2,
-        out_specs=[any_spec] * 5 + [vmem_spec] * 8,
+        out_specs=[any_spec] * 8 + [vmem_spec] * 5 + [any_spec],
         scratch_shapes=scratch,
         compiler_params=pltpu.CompilerParams(
-            collective_id=0, has_side_effects=True, vmem_limit_bytes=63 * 2**20
+            collective_id=0, has_side_effects=True, vmem_limit_bytes=65000 * 2**10
         ),
     )(
         flat(slow_input), flat(fast_input), flat(slow_cotangent), flat(fast_cotangent), clip_ids,
@@ -854,11 +1074,7 @@
         lateral_conv.reshape(-1, cf), slow_narrow.reshape(3 * bs, -1), slow_spatial.reshape(9 * bs, bs),
         slow_widen, lay_out(norm_gains), lay_out(norm_biases),
     )
-    slow_out, fast_out, slow_grad, fast_grad, dsa, dsb, dsc, dl, dfa, dfb, dfc, dgains, dbiases = results
-    dsa, dsb, dsc, dl, dfa, dfb, dfc = lax.psum(
-        (dsa, dsb, dsc, dl, dfa, dfb[:, 0:32], dfc[:, 0:32]), ("dp", "rep")
-    )
-
+    slow_out, fast_out, slow_grad, fast_grad, dsa, dsb, dsc, dl, dfa, dfb, dfc, dgains, dbiases, _ = results
     def gather(packed):
         return packed.reshape(16 * LANES)[0 : sum(widths)]
 
@@ -867,13 +1083,13 @@
         unflat(fast_out, fast_frames),
         unflat(slow_grad, frames),
         unflat(fast_grad, fast_frames),
-        (dfa * factor).reshape(fast_narrow.shape),
-        (dfb * factor).reshape(fast_spatial.shape),
-        dfc * factor,
-        (dl * factor).reshape(lateral_conv.shape),
-        (dsa * factor).reshape(slow_narrow.shape),
-        (dsb * factor).reshape(slow_spatial.shape),
-        dsc * factor,
+        dfa.reshape(fast_narrow.shape),
+        dfb.reshape(fast_spatial.shape),
+        dfc.T,
+        dl.reshape(lateral_conv.shape),
+        dsa.reshape(slow_narrow.shape),
+        dsb.reshape(slow_spatial.shape),
+        dsc,
         gather(dgains),
         gather(dbiases),
     )

time: 444 us -> 183 us (0.41)
  waiting for transfers between devices: 301 us -> 0 us
  Pallas kernels: 103 us -> 160 us
  between operations: 14.1 us -> 0.69 us
  other arithmetic: 13.1 us -> 0 us
  local copies, waits for them, and re-layouts: 12.8 us -> 21.5 us
    psum x2 -> x0, waiting for transfers between devices: 300 us -> none  [body(): lax.psum((dsa, dsb, dsc, dl, dfa, dfb[:, 0:32], dfc[:, 0:32]), ('dp', 're...]
    pallas_call x1, Pallas kernels: 103 us -> 160 us  [body(): pl.pallas_call(functools.partial(kernel, (n_dp, n_rep, low, frames, side,...]
    mul x7 -> x0, other arithmetic: 13.1 us -> none  [the longest x1 4.52 us: body(): dsa * factor]
    unnamed x23 -> x37, local copies, waits for them, and re-layouts: 11.4 us -> 20.1 us
  transfers between devices with their start and end apart: 2 -> 0, of which waited for: 2 -> 0; matrix products, arithmetic and copies ran while one was open for 1% -> 0% of each run, Pallas kernels for 0% -> 0%
where the time goes in v2:
time: 183 us; the launch traced here: 182 us
  Pallas kernels  160 us (87%)
  local copies, waits for them, and re-layouts  21.5 us (12%)
    pallas_call x1, Pallas kernels, body(): pl.pallas_call(functools.partial(kernel, (n_dp, n_rep, low, frames, side,...  160 us
    unnamed x37, local copies, waits for them, and re-layouts  20.1 us

profile of v2, /device:TPU:0, one launch (start us, length us, event | category | flops | bytes accessed | tf_op | source)
XLA Modules:
  0.0 182.2 jit_solution(11630686721338766843)
XLA Ops:
  0.6 1.3 pad_bitcast_fusion
  2.0 160.0 %shard_map.237 = (bf16[1568,1024]{1,0:T(8,128)(2,1)}, bf16[6272,128]{1,0:T(8,128)(2,1)}, bf16[1568,1024]{1,0:T(8,128)(2,1)}, bf16[6272,128]{1,0:T(8,128)(2,1)}, ...) custom-call(bf16[1568,1024]{1,0:T(8,128)(2,1)} %bitcast.45, ...), custom_call_target="tpu_custom_call" | custom-call | tf_op jit(solution)/shard_map/pallas_call | solution.py:1062
  162.0 0.0 copy-start.4
  162.0 4.0 %copy.40 = bf16[8,196,1024]{2,0,1:T(8,128)(2,1)} copy(bf16[8,196,1024]{2,0,1:T(8,128)(2,1)} %bitcast.48) | data formatting | bytes 6422528
  166.0 0.0 copy-done.4
  166.0 0.0 copy-start.1
  166.0 1.2 copy.41
  167.2 1.3 copy-done.1
  168.5 0.0 copy-start.3
  168.5 0.0 copy-start.8
  168.5 0.0 copy-start.6
  168.5 1.7 copy.42
  170.2 0.8 copy-done.3
  171.0 1.2 copy.43
  172.2 0.0 copy-done.8
  172.2 0.6 copy.44
  172.8 0.0 copy-done.7
  172.8 0.7 copy.45
  173.5 0.0 copy-done.9
  173.5 0.6 copy.46
  174.1 0.0 copy-done.6
  174.1 0.8 copy.47
  174.9 0.0 copy-done
  174.9 2.0 %copy.48 = f32[3,256,1280]{2,1,0:T(8,128)} copy(f32[3,256,1280]{2,1,0:T(8,128)S(1)} %bitcast.44) | data formatting | bytes 7864320
  176.9 1.1 copy-done.2
  178.0 1.4 copy.49
  179.4 0.5 copy-done.5
  180.0 1.0 copy.50
  180.9 0.0 copy-done.11
  181.0 0.6 copy.51
  181.6 0.0 copy-done.10
  181.6 0.6 copy.52
  (7 shorter events, 0.0 us)
Async XLA Ops:
  162.0 4.0 %copy-start.4 = (bf16[6272,128]{1,0:T(8,128)(2,1)S(1)}, bf16[6272,128]{1,0:T(8,128)(2,1)}, u32[]{:S(2)}) copy-start(bf16[6272,128]{1,0:T(8,128)(2,1)} %get-tuple-element.27) | copy-start | bytes 4816900
  166.0 2.5 %copy-start.1 = (bf16[1568,1024]{1,0:T(8,128)(2,1)S(1)}, bf16[1568,1024]{1,0:T(8,128)(2,1)}, u32[]{:S(2)}) copy-start(bf16[1568,1024]{1,0:T(8,128)(2,1)} %get-tuple-element.28) | copy-start | bytes 9633796
  168.5 2.5 %copy-start.3 = (bf16[6272,128]{1,0:T(8,128)(2,1)S(1)}, bf16[6272,128]{1,0:T(8,128)(2,1)}, u32[]{:S(2)}) copy-start(bf16[6272,128]{1,0:T(8,128)(2,1)} %get-tuple-element.29) | copy-start | bytes 4816900
  168.5 3.7 %copy-start.8 = (f32[96,128]{1,0:T(8,128)S(1)}, f32[96,128]{1,0:T(8,128)}, u32[]{:S(2)}) copy-start(f32[96,128]{1,0:T(8,128)} %get-tuple-element.30) | copy-start | bytes 147460
  168.5 4.3 %copy-start.7 = (f32[288,32]{1,0:T(8,128)S(1)}, f32[288,32]{1,0:T(8,128)}, u32[]{:S(2)}) copy-start(f32[288,32]{1,0:T(8,128)} %get-tuple-element.31) | copy-start | bytes 110596
  168.5 5.0 %copy-start.9 = (f32[32,128]{1,0:T(8,128)S(1)}, f32[32,128]{1,0:T(8,128)}, u32[]{:S(2)}) copy-start(f32[32,128]{1,0:T(8,128)} %get-tuple-element.32) | copy-start | bytes 49156
  168.5 5.6 %copy-start.6 = (f32[1280,128]{1,0:T(8,128)S(1)}, f32[1280,128]{1,0:T(8,128)}, u32[]{:S(2)}) copy-start(f32[1280,128]{1,0:T(8,128)} %get-tuple-element.33) | copy-start | bytes 1966084
  171.0 3.9 %copy-start = (f32[768,1280]{1,0:T(8,128)S(1)}, f32[768,1280]{1,0:T(8,128)}, u32[]{:S(2)}) copy-start(f32[768,1280]{1,0:T(8,128)} %get-tuple-element.34) | copy-start | bytes 11796484
  174.9 3.1 %copy-start.2 = (f32[2304,256]{1,0:T(8,128)S(1)}, f32[2304,256]{1,0:T(8,128)}, u32[]{:S(2)}) copy-start(f32[2304,256]{1,0:T(8,128)} %get-tuple-element.35) | copy-start | bytes 7077892
  178.0 2.0 %copy-start.5 = (f32[1024,256]{1,0:T(8,128)S(1)}, f32[1024,256]{1,0:T(8,128)}, u32[]{:S(2)}) copy-start(f32[1024,256]{1,0:T(8,128)} %get-tuple-element.64) | copy-start | bytes 3145732
  178.0 2.9 %copy-start.11 = (f32[16,128]{1,0:T(8,128)S(1)}, f32[16,128]{1,0:T(8,128)}, u32[]{:S(2)}) copy-start(f32[16,128]{1,0:T(8,128)} %get-tuple-element.37) | copy-start | bytes 24580
  178.0 3.5 %copy-start.10 = (f32[16,128]{1,0:T(8,128)S(1)}, f32[16,128]{1,0:T(8,128)}, u32[]{:S(2)}) copy-start(f32[16,128]{1,0:T(8,128)} %get-tuple-element.38) | copy-start | bytes 24580

commit v3 on v2

--- a/solution.py
+++ b/solution.py
@@ -16,7 +16,36 @@
 NT = ((1,), (1,))
 TN = ((0,), (0,))
 LANES = 128
-ROWS = (8, 8, 8, 16, 24, 8, 8, 8)
+TURNS = {
+    "lat": 512, "fa": 128, "sa": 512, "fb": 128, "sb": 512, "fc": 256, "sc0": 768, "sc1": 512,
+    "sc0_back": 1024, "sc1_back": 1024, "fc_back": 256, "sb_back": 512, "fb_back": 128, "sa_back": 512,
+    "fa_back": 128, "lat_back": 512,
+}
+
+
+LINES = ('sb2', )
+POLLS = (
+    '',
+    'sc',
+    '',
+    '',
+    'sb0 sc',
+    'sb1',
+    'sb2',
+    '',
+    '',
+    'sb0 sc sa0',
+    '',
+    'sb2 sb1',
+    'sb0 sa1',
+    'sa0 sc sa2',
+    'sb1 sa3 lt',
+    'sa1',
+    'sa0 sa4 sb2',
+    'sb0 sa2',
+    '',
+    'sa3 sc lt sa1 sa4 sa0 sb1 sa2 sb0 sa3 sa1 sc sa4 lt sa0 sb2 sb0 sb1 sa2 sc sa0 sa3 sb2 sc sa1 sb0 sb1 sb2 sa4 sa1 sa0 lt sb1 sa0 sa2 sa1 sa3 sa2 sb1 sb2 sa1 sa4 lt sa3 sb0 sa4 lt sa2 sb2 sa3 sa3 sa4 sa2 sa4 lt sb2 lt sb2',
+)
 
 
 def dot(left, right, dims):
@@ -63,7 +92,7 @@
     xs, cs, gsum, xf, cf, big, sec_fc, gsf, hcs, gcs, hcf, gcf,
     sec_lat, sec_sa, sec_sb, dbuf, sec_fa, sec_fb, dbuf_f, jl, hbs, hbf, vx, slab, slab_sc, summed, gathered,
     wsa, wsb, wsc, wfa_in, wfb_in, wfc_in, wlat, wfa, wfb, wfbk, wfc,
-    stage_a, stage_b, gain_rows, bias_rows, near_s, near_l, far_s, far_l, near_send, near_recv, far_send, far_recv, io_sem, own_sem, big_send, big_recv,
+    stage_a, stage_b, gain_rows, bias_rows, near, far, sum_send, sum_recv, io_sem, own_sem, big_send, big_recv,
 ):
     n_dp, n_rep, low, frames, side, slow_count, fast_count, factor = dims
     rows = xs.shape[0]
@@ -77,15 +106,20 @@
     dp_i, rep_i = lax.axis_index("dp"), lax.axis_index("rep")
     dp_lo, dp_hi = lax.rem(dp_i, low), lax.div(dp_i, low)
     high = n_dp // low
-    near_rank = dp_lo * n_rep + rep_i
+    direct = n_dp * n_rep <= 32
+    near_low = n_dp if direct else low
+    near_dp, far_dp = lax.rem(dp_i, near_low), lax.div(dp_i, near_low)
     near_peers = [
-        (dp_hi * low + lax.rem(dp_lo + a, low), lax.rem(rep_i + b, n_rep))
-        for a in range(low)
+        (far_dp * near_low + lax.rem(near_dp + a, near_low), lax.rem(rep_i + b, n_rep))
+        for a in range(near_low)
         for b in range(n_rep)
         if a or b
     ]
-    far_rank = dp_hi
-    far_peers = [(lax.rem(dp_hi + a, high) * low + dp_lo, rep_i) for a in range(1, high)]
+    far_count = n_dp // near_low
+    far_peers = [(lax.rem(far_dp + a, far_count) * near_low + near_dp, rep_i) for a in range(1, far_count)]
+    stages = [(near, near_dp * n_rep + rep_i, near_peers)]
+    if far_peers:
+        stages.append((far, far_dp, far_peers))
 
     c, x = lax.rem(rep_i, 2), lax.div(rep_i, 2)
     y, z = dp_lo, lax.rem(dp_hi, 4)
@@ -93,11 +127,15 @@
     core_peer = (dp_i, 2 * x + 1 - c)
     x_peer = (dp_i, 2 * (1 - x) + c)
     y_peer = (dp_hi * low + 1 - y, rep_i)
+    def z_peer(flip):
+        return ((outer * 4 + z + flip - 2 * flip * lax.rem(lax.div(z, flip), 2)) * low + y, rep_i)
+
     z_peers = [((outer * 4 + lax.rem(z + k, 4)) * low + y, rep_i) for k in range(1, 4)]
     outer_peers = [((lax.rem(outer + k, outers) * 4 + z) * low + y, rep_i) for k in range(1, outers)]
 
     barrier = pltpu.get_barrier_semaphore()
-    for peer in near_peers + far_peers:
+    greeted = near_peers + far_peers
+    for peer in greeted:
         pl.semaphore_signal(barrier, inc=1, device_id=peer, device_id_type=MESH)
 
     loads = {}
@@ -124,65 +162,77 @@
         copy.start()
         return copy
 
-    slots, counts = [], {8: 0, 24: 0}
-    for size in ROWS:
-        wide = 8 if size == 8 else 24
-        slots.append((near_s, far_s, counts[wide]) if wide == 8 else (near_l, far_l, counts[wide]))
-        counts[wide] += 1
+    turn_at, turn_index = {}, {}
+    for index, (turn, width) in enumerate(TURNS.items()):
+        turn_at[turn] = sum(list(TURNS.values())[:index])
+        turn_index[turn] = index
 
     def put(turn, at, vector):
-        near, far, slot = slots[turn]
-        for piece in range(vector.shape[1] // LANES):
-            near[slot, near_rank, pl.ds(at + piece, 1), :] = vector[:, piece * LANES : (piece + 1) * LANES]
-
-    def near_copy(turn, first, count, peer):
-        near, far, slot = slots[turn]
-        span = near.at[slot, pl.ds(first, count), pl.ds(0, ROWS[turn])]
+        near[stages[0][1], :, pl.ds(turn_at[turn] + at, vector.shape[1])] = vector
+
+    def sum_copy(turn, stage, first, count, peer):
+        buffer = stages[stage][0]
+        block = buffer.at[pl.ds(first, count), :, pl.ds(turn_at[turn], TURNS[turn])]
         return pltpu.make_async_remote_copy(
-            src_ref=span, dst_ref=span, send_sem=near_send.at[turn], recv_sem=near_recv.at[turn],
-            device_id=peer, device_id_type=MESH,
-        )
-
-    def far_copy(turn, first, count, peer):
-        near, far, slot = slots[turn]
-        span = far.at[slot, pl.ds(first, count), pl.ds(0, ROWS[turn])]
-        return pltpu.make_async_remote_copy(
-            src_ref=span, dst_ref=span, send_sem=far_send.at[turn], recv_sem=far_recv.at[turn],
-            device_id=peer, device_id_type=MESH,
+            src_ref=block, dst_ref=block, send_sem=sum_send.at[turn_index[turn], stage],
+            recv_sem=sum_recv.at[turn_index[turn], stage], device_id=peer, device_id_type=MESH,
         )
 
     def exchange_start(turn):
         for peer in near_peers:
-            near_copy(turn, near_rank, 1, peer).start()
-
-    def exchange_middle(turn):
-        near, far, slot = slots[turn]
-        size = ROWS[turn]
-        near_copy(turn, 0, len(near_peers), near_peers[0]).wait_recv()
-        far[slot, far_rank, pl.ds(0, size), :] = jnp.sum(near[slot, :, pl.ds(0, size), :], axis=0)
-        for peer in far_peers:
-            far_copy(turn, far_rank, 1, peer).start()
+            sum_copy(turn, 0, stages[0][1], 1, peer).start()
 
     def exchange_end(turn):
-        near, far, slot = slots[turn]
-        size = ROWS[turn]
-        far_copy(turn, 0, len(far_peers), far_peers[0]).wait_recv()
-        total = jnp.sum(far[slot, :, pl.ds(0, size), :], axis=0)
-        near_copy(turn, 0, len(near_peers), near_peers[0]).wait_send()
-        far_copy(turn, 0, len(far_peers), far_peers[0]).wait_send()
+        lanes = pl.ds(turn_at[turn], TURNS[turn])
+        for stage, (buffer, rank, peers) in enumerate(stages):
+            if stage:
+                buffer[rank, :, lanes] = total
+                for peer in peers:
+                    sum_copy(turn, stage, rank, 1, peer).start()
+            copy = sum_copy(turn, stage, 0, len(peers), peers[0])
+            copy.wait_recv()
+            total = jnp.sum(buffer[:, :, lanes], axis=0)
+            copy.wait_send()
         return total
 
     def take(total, at, width):
-        pieces = [total[at + piece : at + piece + 1, :] for piece in range(width // LANES)]
-        return pieces[0] if len(pieces) == 1 else jnp.concatenate(pieces, axis=1)
-
-    def repeat4(vector):
-        return jnp.concatenate([vector] * 4, axis=1)
+        return total[:, at : at + width]
+
+    def pair32(first, second):
+        group = lax.broadcasted_iota(jnp.int32, (8, LANES), 1) // 32
+        rows8 = (8, LANES)
+        first = fold_lanes(jnp.broadcast_to(first, rows8))
+        second = fold_lanes(jnp.broadcast_to(second, rows8))
+        return jnp.where(group == 0, first, jnp.where(group == 1, second, 0.0))[0:1, :]
+
+    def unpair32(total):
+        group = lax.broadcasted_iota(jnp.int32, (8, LANES), 1) // 32
+        total = jnp.broadcast_to(total, (8, LANES))
+        first = fold_lanes(jnp.where(group == 0, total, 0.0))
+        second = fold_lanes(jnp.where(group == 1, total, 0.0))
+        return first[0:1, :], second[0:1, :]
 
     pieces = {}
 
+    bits = {"c": (c, core_peer), "x": (x, x_peer), "y": (y, y_peer),
+            "z0": (lax.rem(z, 2), z_peer(1)), "z1": (lax.div(z, 2), z_peer(2))}
+    PLANE_FIRST = (("c", "x", "y", "z"), ("c", "y", "x", "z"))
+    LINE_FIRST = (("c", "z0", "z1", "x", "y"), ("c", "z0", "z1", "y", "x"))
+
     def add_piece(name, ref, lane, size, index):
-        pieces[name] = {"name": name, "ref": ref, "lane": lane, "size": size, "index": index, "step": 0}
+        axes = LINE_FIRST if name in LINES else PLANE_FIRST
+        piece = {"name": name, "ref": ref, "lane": lane, "size": size, "index": index, "step": 0, "axes": axes}
+        starts, counts, arriving = [[0], [0]], [size], [size]
+        for step, pair in enumerate(zip(*axes)):
+            for side, axis in enumerate(pair):
+                if axis == "z":
+                    starts[side].append(starts[side][-1] + z * (counts[-1] // 4))
+                else:
+                    starts[side].append(starts[side][-1] + bits[axis][0] * (counts[-1] // 2))
+            counts.append(counts[-1] // (4 if pair[0] == "z" else 2))
+            arriving.append(arriving[-1] + (3 if pair[0] == "z" else 1) * counts[-1])
+        piece.update(starts=starts, counts=counts, arriving=arriving, steps=len(axes[0]))
+        pieces[name] = piece
 
     for k in range(2):
         add_piece("sb%d" % k, sec_fc, 256 * k, 768, k)
@@ -214,15 +264,19 @@
             return dsa_h.at[pl.ds(start, count), pl.ds(256 * k + lane, width)]
         return dsb_h.at[pl.ds(768 * k + start, count), pl.ds(lane, width)]
 
-    def own_copies(piece, a, b, t):
-        sem = own_sem.at[piece["index"]]
-        return (
-            pltpu.make_async_copy(span(piece, a, t, 0, 128), result(piece, a, t, 0, 128), sem.at[0]),
-            pltpu.make_async_copy(span(piece, b, t, 128, 128), result(piece, b, t, 128, 128), sem.at[1]),
-        )
+    def own_copies(piece):
+        count, sem = piece["counts"][-1], own_sem.at[piece["index"]]
+        return [
+            pltpu.make_async_copy(
+                span(piece, start[-1], count, 128 * side, 128),
+                result(piece, start[-1], count, 128 * side, 128),
+                sem.at[side],
+            )
+            for side, start in enumerate(piece["starts"])
+        ]
 
     def arrived(piece, step, rows_in):
-        block = span(piece, 0, rows_in) if step < 4 else result(piece, 0, rows_in)
+        block = span(piece, 0, rows_in) if step < piece["steps"] else result(piece, 0, rows_in)
         copy = pltpu.make_async_remote_copy(
             src_ref=block, dst_ref=block, send_sem=big_send.at[piece["index"], step],
             recv_sem=big_recv.at[piece["index"], step], device_id=core_peer, device_id_type=MESH,
@@ -253,99 +307,112 @@
             dfb[32 * tap : 32 * (tap + 1), :] = block[:, 32 * (tap % 4) : 32 * (tap % 4 + 1)]
         dfc[...] = summed[704:736, 128:256]
 
+    def poll(turn):
+        for name in POLLS[turn].split():
+            advance(name)
+
+    def done(name):
+        return pieces[name]["step"] > 2 * pieces[name]["steps"]
+
     def advance(name):
         piece = pieces[name]
-        size, step = piece["size"], piece["step"]
+        step, steps, index = piece["step"], piece["steps"], piece["index"]
         piece["step"] = step + 1
-        h, q, o, t = size // 2, size // 4, size // 8, size // 32
-        mine = c * h
-        a1, a1o = mine + x * q, mine + (1 - x) * q
-        b1, b1o = mine + y * q, mine + (1 - y) * q
-        a2, a2o = a1 + y * o, a1 + (1 - y) * o
-        b2, b2o = b1 + x * o, b1 + (1 - x) * o
-        from_core, from_one, from_two = size, size + h, size + h + q
-        from_z = size + h + q + o
-        if step == 0:
-            send(piece, 0, span(piece, (1 - c) * h, h), span(piece, from_core, h), core_peer)
-        elif step == 1:
-            arrived(piece, 0, h)
-            add_rows(piece, mine, from_core, h, 0, 256)
-            send(piece, 1, span(piece, a1o, q, 0, 128), span(piece, from_one, q, 0, 128), x_peer)
-            send(piece, 1, span(piece, b1o, q, 128, 128), span(piece, from_one, q, 128, 128), y_peer)
-        elif step == 2:
-            arrived(piece, 1, q)
-            add_rows(piece, a1, from_one, q, 0, 128)
-            add_rows(piece, b1, from_one, q, 128, 128)
-            send(piece, 2, span(piece, a2o, o, 0, 128), span(piece, from_two, o, 0, 128), y_peer)
-            send(piece, 2, span(piece, b2o, o, 128, 128), span(piece, from_two, o, 128, 128), x_peer)
-        elif step == 3:
-            arrived(piece, 2, o)
-            add_rows(piece, a2, from_two, o, 0, 128)
-            add_rows(piece, b2, from_two, o, 128, 128)
-            for k, peer in enumerate(z_peers):
-                at, into = lax.rem(z + k + 1, 4) * t, from_z + k * t
-                send(piece, 3, span(piece, a2 + at, t, 0, 128), span(piece, into, t, 0, 128), peer)
-                send(piece, 3, span(piece, b2 + at, t, 128, 128), span(piece, into, t, 128, 128), peer)
-        elif step == 4:
-            arrived(piece, 3, 3 * t)
-            ref, lane = piece["ref"], piece["lane"]
-            own_a = (pl.ds(pl.multiple_of(a2 + z * t, 8), t), pl.ds(lane, 128))
-            own_b = (pl.ds(pl.multiple_of(b2 + z * t, 8), t), pl.ds(lane + 128, 128))
-            both = jnp.concatenate([ref[own_a], ref[own_b]], axis=1)
-            for k in range(3):
-                both = both + ref[pl.ds(from_z + k * t, t), pl.ds(lane, 256)]
+        starts, counts, arriving, axes = piece["starts"], piece["counts"], piece["arriving"], piece["axes"]
+        ref, lane = piece["ref"], piece["lane"]
+
+        def received(last):
+            fan = 3 if axes[0][last] == "z" else 1
+            return fan * counts[last + 1]
+
+        if 0 < step < steps or (step == steps and axes[0][-1] != "z"):
+            arrived(piece, step - 1, received(step - 1))
+            if step == 1:
+                add_rows(piece, starts[0][1], arriving[0], counts[1], 0, 256)
+            else:
+                for side in range(2):
+                    add_rows(piece, starts[side][step], arriving[step - 1], counts[step], 128 * side, 128)
+        elif step == steps:
+            arrived(piece, step - 1, received(step - 1))
+        elif step > steps:
+            arrived(piece, step - 1, received(2 * steps - step))
+
+        if step < steps:
+            held, keep = counts[step], counts[step + 1]
+            if step == 0:
+                at = starts[0][0] + (1 - c) * keep
+                send(piece, 0, span(piece, at, keep), span(piece, arriving[0], keep), core_peer)
+                return
+            for side in range(2):
+                axis, start = axes[side][step], starts[side][step]
+                if axis == "z":
+                    for k, peer in enumerate(z_peers):
+                        at, into = start + lax.rem(z + k + 1, 4) * keep, arriving[step] + k * keep
+                        send(
+                            piece, step, span(piece, at, keep, 128 * side, 128),
+                            span(piece, into, keep, 128 * side, 128), peer,
+                        )
+                else:
+                    bit, peer = bits[axis]
+                    at = start + (1 - bit) * keep
+                    send(
+                        piece, step, span(piece, at, keep, 128 * side, 128),
+                        span(piece, arriving[step], keep, 128 * side, 128), peer,
+                    )
+        elif step == steps:
+            last = counts[-1]
+            own = [
+                (pl.ds(pl.multiple_of(starts[side][-1], 8), last), pl.ds(lane + 128 * side, 128))
+                for side in range(2)
+            ]
+            both = jnp.concatenate([ref[own[0]], ref[own[1]]], axis=1)
+            if axes[0][-1] == "z":
+                for k in range(3):
+                    both = both + ref[pl.ds(arriving[steps - 1] + k * last, last), pl.ds(lane, 256)]
             if outers > 1:
-                index = piece["index"]
-                held = span(piece, from_z, t)
-                ref[pl.ds(from_z, t), pl.ds(lane, 256)] = both
+                held = span(piece, arriving[steps - 1], last)
+                ref[pl.ds(arriving[steps - 1], last), pl.ds(lane, 256)] = both
                 for peer in outer_peers:
-                    send(piece, 8, held, extra_h.at[index, outer, pl.ds(0, t)], peer)
-                block = extra_h.at[index, pl.ds(0, outers - 1), pl.ds(0, t)]
+                    send(piece, 10, held, extra_h.at[index, outer, pl.ds(0, last)], peer)
+                block = extra_h.at[index, pl.ds(0, outers - 1), pl.ds(0, last)]
                 copy = pltpu.make_async_remote_copy(
-                    src_ref=block, dst_ref=block, send_sem=big_send.at[index, 8], recv_sem=big_recv.at[index, 8],
+                    src_ref=block, dst_ref=block, send_sem=big_send.at[index, 10], recv_sem=big_recv.at[index, 10],
                     device_id=core_peer, device_id_type=MESH,
                 )
                 copy.wait_recv()
                 copy.wait_send()
                 for src, dst in (
-                    (held, extra_h.at[index, outer, pl.ds(0, t)]),
+                    (held, extra_h.at[index, outer, pl.ds(0, last)]),
                     (extra_h.at[index], gathered),
                 ):
                     copy = pltpu.make_async_copy(src, dst, own_sem.at[index, 0])
                     copy.start()
                     copy.wait()
-                both = jnp.sum(gathered[:, pl.ds(0, t), :], axis=0)
+                both = jnp.sum(gathered[:, pl.ds(0, last), :], axis=0)
             both = both * factor
-            ref[own_a] = both[:, 0:128]
-            ref[own_b] = both[:, 128:256]
-            own = (a2 + z * t, 0), (b2 + z * t, 128)
-            for peer in z_peers:
-                for at, half_lanes in own:
-                    send(piece, 4, span(piece, at, t, half_lanes, 128), result(piece, at, t, half_lanes, 128), peer)
-            for copy in own_copies(piece, own[0][0], own[1][0], t):
-                copy.start()
-        elif step == 5:
-            arrived(piece, 4, 3 * t)
-            for copy in own_copies(piece, a2 + z * t, b2 + z * t, t):
-                copy.wait()
-            block = result(piece, a2, o, 0, 128)
-            send(piece, 5, block, block, y_peer)
-            block = result(piece, b2, o, 128, 128)
-            send(piece, 5, block, block, x_peer)
-        elif step == 6:
-            arrived(piece, 5, o)
-            block = result(piece, a1, q, 0, 128)
-            send(piece, 6, block, block, x_peer)
-            block = result(piece, b1, q, 128, 128)
-            send(piece, 6, block, block, y_peer)
-        elif step == 7:
-            arrived(piece, 6, q)
-            block = result(piece, mine, h)
-            send(piece, 7, block, block, core_peer)
-        elif step == 8:
-            arrived(piece, 7, h)
-            if name == "lt":
-                unpack_small()
+            for side in range(2):
+                ref[own[side]] = both[:, 128 * side : 128 * (side + 1)]
+        if steps <= step < 2 * steps:
+            back = 2 * steps - 1 - step
+            count = counts[back + 1]
+            if step == steps + 1:
+                for copy in own_copies(piece):
+                    copy.wait()
+            if back == 0:
+                block = result(piece, starts[0][1], count)
+                send(piece, step, block, block, core_peer)
+                return
+            for side in range(2):
+                axis, start = axes[side][back], starts[side][back + 1]
+                block = result(piece, start, count, 128 * side, 128)
+                source = span(piece, start, count, 128 * side, 128) if step == steps else block
+                for peer in z_peers if axis == "z" else [bits[axis][1]]:
+                    send(piece, step, source, block, peer)
+            if step == steps:
+                for copy in own_copies(piece):
+                    copy.start()
+        elif step == 2 * steps and name == "lt":
+            unpack_small()
 
     spots = {"fc": 0, "lat": 1, "sa": 3, "sb": 5, "sc": 7, "fa": 16, "fb": 17}
 
@@ -359,7 +426,7 @@
         vectors = {"fa": fa, "fb": fb}
         at = 0
         for name, count in (("fc", 1), ("lat", 2), ("sa", 2), ("sb", 2), ("sc", 8)):
-            vectors[name] = take(moved, at, count * LANES)
+            vectors[name] = jnp.concatenate([moved[at + k : at + k + 1, :] for k in range(count)], axis=1)
             at += count
         return vectors
 
@@ -475,14 +542,15 @@
         sec_lat[at, :] = value
         return carry[0] + column_sums(value), carry[1] + column_sums(value * value)
 
+    sum_lat, sq_lat = loop(2, conv_lat, zero2(256))
+    put("lat", 0, squash(sum_lat))
+    put("lat", 256, squash(sq_lat))
+    pl.semaphore_wait(barrier, len(greeted))
+    exchange_start("lat")
+
     sum_fa, sq_fa = loop(2, conv_fa, zero2(128))
-    sum_lat, sq_lat = loop(2, conv_lat, zero2(256))
-    put(0, 0, squash(sum_fa))
-    put(0, 1, squash(sq_fa))
-    put(0, 2, squash(sum_lat))
-    put(0, 4, squash(sq_lat))
-    pl.semaphore_wait(barrier, len(near_peers) + len(far_peers))
-    exchange_start(0)
+    put("fa", 0, pair32(squash(sum_fa), squash(sq_fa)))
+    exchange_start("fa")
 
     loads["xs"].wait()
     loads["wsa"].wait()
@@ -493,7 +561,6 @@
             big[at, bs * k : bs * (k + 1)] = dot(xs[at, :], wsa[bs * k : bs * (k + 1), 0:cs_n], NT)
 
     loop(2, narrow_main)
-    exchange_middle(0)
     loads["wfb"].wait()
     loads["wfc"].wait()
     spread = dot(wfb_in[...], repeat_lanes, NN)
@@ -506,11 +573,9 @@
     widen = dot(wfc_in[...], repeat_lanes, TN)
     for phase in range(4):
         wfc[LANES * phase : LANES * (phase + 1), :] = jnp.where(lane_group == phase, widen, 0.0).astype(BF16)
-    total = exchange_end(0)
-
-    fa_rows = fold_lanes(total[0:8, :])
-    stats_fa = moments(fa_rows[0:1, :], fa_rows[1:2, :], fast_count)
-    stats_lat = moments(take(total, 2, 256), take(total, 4, 256), slow_count)
+    total = exchange_end("lat")
+
+    stats_lat = moments(take(total, 0, 256), take(total, 256, 256), slow_count)
 
     def act_fa(i):
         normed, pre = before_act(sec_fa[rows_at(i, band), :], stats_fa, "fa")
@@ -521,7 +586,6 @@
         normed, pre = before_act(sec_lat[at, :], stats_lat, "lat")
         jl[at, :] = (pre * sigmoid(pre)).astype(BF16)
 
-    loop(bands, act_fa)
     loop(bands, act_lat)
 
     def conv_fb(i, carry):
@@ -532,8 +596,6 @@
             value = term if value is None else value + term
         sec_fb[rows_at(i, half), :] = value
         return carry[0] + column_sums(value), carry[1] + column_sums(value * value)
-
-    sum_fb, sq_fb = loop(2, conv_fb, zero2(128))
 
     def narrow_lateral(i):
         at = rows_at(i, half)
@@ -554,17 +616,19 @@
         return carry[0] + column_sums(value), carry[1] + column_sums(value * value)
 
     sum_sa, sq_sa = loop(bands, combine_sa, zero2(256))
-    put(1, 0, squash(sum_fb))
-    put(1, 1, squash(sq_fb))
-    put(1, 2, squash(sum_sa))
-    put(1, 4, squash(sq_sa))
-    exchange_start(1)
-    exchange_middle(1)
-    total = exchange_end(1)
-
-    fb_rows = fold_lanes(total[0:8, :])
-    stats_fb = moments(fb_rows[0:1, :], fb_rows[1:2, :], fast_count)
-    stats_sa = moments(take(total, 2, 256), take(total, 4, 256), slow_count)
+    put("sa", 0, squash(sum_sa))
+    put("sa", 256, squash(sq_sa))
+    exchange_start("sa")
+
+    total = exchange_end("fa")
+    stats_fa = moments(*unpair32(total), fast_count)
+    loop(bands, act_fa)
+    sum_fb, sq_fb = loop(2, conv_fb, zero2(128))
+    put("fb", 0, pair32(squash(sum_fb), squash(sq_fb)))
+    exchange_start("fb")
+    total = exchange_end("sa")
+
+    stats_sa = moments(take(total, 0, 256), take(total, 256, 256), slow_count)
 
     def act_sa(i):
         normed, pre = before_act(sec_sa[rows_at(i, band), :], stats_sa, "sa")
@@ -590,6 +654,12 @@
         return carry[0] + column_sums(value), carry[1] + column_sums(value * value)
 
     sum_sb, sq_sb = loop(2, conv_sb, zero2(256))
+    put("sb", 0, squash(sum_sb))
+    put("sb", 256, squash(sq_sb))
+    exchange_start("sb")
+
+    total = exchange_end("fb")
+    stats_fb = moments(*unpair32(total), fast_count)
     loop(bands, act_fb)
 
     def widen_fast(i, carry):
@@ -603,35 +673,42 @@
     def fold4(vector):
         return vector[:, 0:128] + vector[:, 128:256] + vector[:, 256:384] + vector[:, 384:512]
 
-    put(2, 0, squash(fold4(sum_fc)))
-    put(2, 1, squash(fold4(sq_fc)))
-    put(2, 2, squash(sum_sb))
-    put(2, 4, squash(sq_sb))
-    exchange_start(2)
-    exchange_middle(2)
-    total = exchange_end(2)
-
-    stats_fc = moments(take(total, 0, 128), take(total, 1, 128), fast_count)
-    stats_sb = moments(take(total, 2, 256), take(total, 4, 256), slow_count)
-
-    def act_sb(i):
+    put("fc", 0, squash(fold4(sum_fc)))
+    put("fc", 128, squash(fold4(sq_fc)))
+    exchange_start("fc")
+    total = exchange_end("sb")
+
+    stats_sb = moments(take(total, 0, 256), take(total, 256, 256), slow_count)
+
+    def act_sb(i, carry):
         at = rows_at(i, band)
         normed, pre = before_act(sec_sb[at, :], stats_sb, "sb")
-        hbs[at, :] = (pre * sigmoid(pre)).astype(BF16)
-
-    loop(bands, act_sb)
+        value = (pre * sigmoid(pre)).astype(BF16)
+        hbs[at, :] = value
+        return carry + column_sums(value.astype(F32))
+
+    sum_hbs = loop(bands, act_sb, jnp.zeros((8, bs), F32))
     loads["wsc"].wait()
-
-    def widen_slow(i, carry):
-        at = rows_at(i, half)
-        value = dot(hbs[at, :], wsc[...], NT)
-        big[at, :] = value
-        return carry[0] + column_sums(value), carry[1] + column_sums(value * value)
-
-    sum_sc, sq_sc = loop(2, widen_slow, zero2(cs_n))
-    put(3, 0, squash(sum_sc))
-    put(3, 8, squash(sq_sc))
-    exchange_start(3)
+    mid = cs_n // 2
+
+    def widen_slow(part):
+        lanes = slice(part * mid, (part + 1) * mid)
+
+        def step(i, carry):
+            at = rows_at(i, half)
+            value = dot(hbs[at, :], wsc[lanes, :], NT)
+            big[at, lanes] = value
+            return carry + column_sums(value * value)
+
+        return loop(2, step, jnp.zeros((8, mid), F32))
+
+    put("sc0", 0, squash(sum_hbs))
+    put("sc0", 256, squash(widen_slow(0)))
+    exchange_start("sc0")
+    put("sc1", 0, squash(widen_slow(1)))
+    exchange_start("sc1")
+    total = exchange_end("fc")
+    stats_fc = moments(take(total, 0, 128), take(total, 128, 128), fast_count)
 
     loads["cf"].wait()
 
@@ -656,57 +733,54 @@
 
     bias_fc, gain_fc = loop(bands, finish_fast, zero2(128))
     fast_store = store(xf, fast_h, 10)
-    exchange_middle(3)
+    put("fc_back", 0, squash(bias_fc))
+    put("fc_back", 128, squash(gain_fc))
+    exchange_start("fc_back")
     loads["cs"].wait()
-    total = exchange_end(3)
-
-    stats_sc = moments(take(total, 0, cs_n), take(total, 8, cs_n), slow_count)
+    total = exchange_end("sc0")
+    squares = jnp.concatenate([take(total, 256, mid), exchange_end("sc1")], axis=1)
+    whole = lax.dot_general(
+        jnp.broadcast_to(take(total, 0, 256), (8, bs)), wsc[...].astype(F32), (NT, ((), ())),
+        precision=lax.Precision.HIGHEST, preferred_element_type=F32,
+    )[0:1, :]
+
+    stats_sc = moments(whole, squares, slow_count)
     thin = 32
-
-    def finish_slow(i, carry):
-        at = rows_at(i, thin)
-        normed, shift = before_act(big[at, :], stats_sc, "sc")
-        value = xs[at, :].astype(F32) + shift
-        gate = sigmoid(value)
-        grad = cs[at, :].astype(F32) * (gate * (1.0 + value * (1.0 - gate)))
-        cs[at, :] = (value * gate).astype(BF16)
-        gsum[at, :] = normed.astype(BF16)
-        big[at, :] = grad
-        return carry[0] + column_sums(grad), carry[1] + column_sums(grad * normed)
-
-    bias_sc, gain_sc = loop(rows // thin, finish_slow, zero2(cs_n))
+    mean_sc, scale_sc = stats_sc
+    half_lead = 0.5 * gain("sc") * scale_sc
+    half_level = 0.5 * bias("sc") - mean_sc * half_lead
+
+    def finish_slow(part):
+        lanes = slice(part * mid, (part + 1) * mid)
+        lead, level = half_lead[:, lanes], half_level[:, lanes]
+        mean, scale = mean_sc[:, lanes], scale_sc[:, lanes]
+
+        def step(i, carry):
+            at = rows_at(i, thin)
+            section = big[at, lanes]
+            h = 0.5 * xs[at, lanes].astype(F32) + (section * lead + level)
+            t = jnp.tanh(h)
+            out = h + h * t
+            gate = 0.5 + 0.5 * t
+            grad = cs[at, lanes].astype(F32) * (gate + out * (1.0 - gate))
+            normed = (section - mean) * scale
+            cs[at, lanes] = out.astype(BF16)
+            gsum[at, lanes] = normed.astype(BF16)
+            big[at, lanes] = grad
+            return carry[0] + column_sums(grad), carry[1] + column_sums(grad * normed)
+
+        return loop(rows // thin, step, zero2(mid))
+
+    for part in range(2):
+        bias_part, gain_part = finish_slow(part)
+        put("sc%d_back" % part, 0, squash(bias_part))
+        put("sc%d_back" % part, mid, squash(gain_part))
+        exchange_start("sc%d_back" % part)
     slow_store = store(cs, slow_h, 11)
-    put(4, 0, squash(bias_sc))
-    put(4, 8, squash(gain_sc))
-    put(4, 16, squash(bias_fc))
-    put(4, 17, squash(gain_fc))
-    exchange_start(4)
-    exchange_middle(4)
-    total = exchange_end(4)
-
-    bias_sc, gain_sc = take(total, 0, cs_n), take(total, 8, cs_n)
-    bias_fc, gain_fc = take(total, 16, 128), take(total, 17, 128)
-    report("sc", bias_sc, gain_sc)
+
+    total = exchange_end("fc_back")
+    bias_fc, gain_fc = take(total, 0, 128), take(total, 128, 128)
     report("fc", bias_fc, gain_fc)
-    lead_sc = gain("sc") * stats_sc[1]
-    level_sc = lead_sc * bias_sc * (1.0 / slow_count)
-    tilt_sc = lead_sc * gain_sc * (1.0 / slow_count)
-    slow_store.wait()
-
-    def low_sc(i):
-        at = rows_at(i, thin)
-        grad = big[at, :]
-        cs[at, :] = (grad * lead_sc - level_sc - gsum[at, :].astype(F32) * tilt_sc).astype(BF16)
-        gsum[at, :] = grad.astype(BF16)
-
-    loop(rows // thin, low_sc)
-
-    def back_sc(i):
-        at = rows_at(i, half)
-        dbuf[at, :] = dot(cs[at, :], wsc[...], NN)
-
-    loop(2, back_sc)
-
     def slope_pass(section, stats, name, buffer):
         def step(i, carry):
             at = rows_at(i, band)
@@ -718,8 +792,6 @@
 
         return loop(bands, step, zero2(section.shape[1]))
 
-    bias_sb, gain_sb = slope_pass(sec_sb, stats_sb, "sb", dbuf)
-
     mean_fc, scale_fc = stats_fc
     lead_fc = gain("fc") * scale_fc
     tilt_fc = lead_fc * scale_fc * gain_fc * (1.0 / fast_count)
@@ -744,41 +816,84 @@
 
     loop(2, back_fc)
     bias_fb, gain_fb = slope_pass(sec_fb, stats_fb, "fb", dbuf_f)
-    put(5, 0, squash(bias_fb))
-    put(5, 1, squash(gain_fb))
-    put(5, 2, squash(bias_sb))
-    put(5, 4, squash(gain_sb))
-    exchange_start(5)
+    put("fb_back", 0, pair32(squash(bias_fb), squash(gain_fb)))
+    exchange_start("fb_back")
+    slow_store.wait()
+    sums = [exchange_end("sc%d_back" % part) for part in range(2)]
+
+    bias_sc = jnp.concatenate([take(total, 0, mid) for total in sums], axis=1)
+    gain_sc = jnp.concatenate([take(total, mid, mid) for total in sums], axis=1)
+    report("sc", bias_sc, gain_sc)
+    lead_sc = gain("sc") * stats_sc[1]
+    level_sc = lead_sc * bias_sc * (1.0 / slow_count)
+    tilt_sc = lead_sc * gain_sc * (1.0 / slow_count)
+
+    def low_sc(i):
+        at = rows_at(i, thin)
+        grad = big[at, :]
+        cs[at, :] = (grad * lead_sc - level_sc - gsum[at, :].astype(F32) * tilt_sc).astype(BF16)
+        gsum[at, :] = grad.astype(BF16)
+
+    loop(rows // thin, low_sc)
+
+    def back_sc(i):
+        at = rows_at(i, half)
+        dbuf[at, :] = dot(cs[at, :], wsc[...], NN)
+
+    loop(2, back_sc)
+
+    bias_sb, gain_sb = slope_pass(sec_sb, stats_sb, "sb", dbuf)
+
+    put("sb_back", 0, squash(bias_sb))
+    put("sb_back", 256, squash(gain_sb))
+    exchange_start("sb_back")
 
     slab_sc[0:cs_n, :] = dot(cs[...], hbs[...], TN)
     advance("sc")
-    exchange_middle(5)
     widening = None
     for phase in range(4):
         term = dot(hbf[...], cf[rows * phase : rows * (phase + 1), :], TN)[32 * phase : 32 * (phase + 1), :]
         widening = term if widening is None else widening + term
     slab[2, 704:736, 128:256] = widening
     slab[2, 736:768, 128:256] = jnp.zeros((32, LANES), F32)
-    advance("sc")
-    total = exchange_end(5)
-
-    fold_rows = fold_lanes(total[0:8, :])
-    bias_fb, gain_fb = fold_rows[0:1, :], fold_rows[1:2, :]
-    bias_sb, gain_sb = take(total, 2, 256), take(total, 4, 256)
+    poll(0)
+
+    bias_fb, gain_fb = unpair32(exchange_end("fb_back"))
     report("fb", bias_fb, gain_fb)
-    report("sb", bias_sb, gain_sb)
-    vec_sb = back_vectors("sb", stats_sb, bias_sb, gain_sb, slow_count)
     vec_fb = back_vectors("fb", stats_fb, bias_fb, gain_fb, fast_count)
 
     def norm_grad(buffer, section, at, vectors):
         lead, level, tilt = vectors
         return buffer[at, :] * lead - level - section[at, :] * tilt
 
+    def low_fb(i):
+        spread_columns(gcf, i, norm_grad(dbuf_f, sec_fb, rows_at(i, band), vec_fb))
+
+    loop(bands, low_fb)
+
+    def back_fb(i):
+        value = None
+        for a in range(3):
+            at = pl.ds(pl.multiple_of(i * half + band * (2 - a), 16), half)
+            term = dot(gcf[at, :], wfbk[a], NN)
+            value = term if value is None else value + term
+        dbuf_f[rows_at(i, half), :] = value
+
+    loop(2, back_fb)
+    bias_fa, gain_fa = slope_pass(sec_fa, stats_fa, "fa", dbuf_f)
+    put("fa_back", 0, pair32(squash(bias_fa), squash(gain_fa)))
+    exchange_start("fa_back")
+    poll(1)
+    total = exchange_end("sb_back")
+
+    bias_sb, gain_sb = take(total, 0, 256), take(total, 256, 256)
+    report("sb", bias_sb, gain_sb)
+    vec_sb = back_vectors("sb", stats_sb, bias_sb, gain_sb, slow_count)
+
     def low_sb(i):
         spread_columns(gcs, i, norm_grad(dbuf, sec_sb, rows_at(i, band), vec_sb))
 
     loop(bands, low_sb)
-    advance("sc")
 
     def back_sb(i):
         value = None
@@ -791,30 +906,13 @@
         dbuf[rows_at(i, half), :] = value
 
     loop(2, back_sb)
-    advance("sc")
+    poll(2)
     bias_sa, gain_sa = slope_pass(sec_sa, stats_sa, "sa", dbuf)
 
-    def low_fb(i):
-        spread_columns(gcf, i, norm_grad(dbuf_f, sec_fb, rows_at(i, band), vec_fb))
-
-    loop(bands, low_fb)
-    advance("sc")
-
-    def back_fb(i):
-        value = None
-        for a in range(3):
-            at = pl.ds(pl.multiple_of(i * half + band * (2 - a), 16), half)
-            term = dot(gcf[at, :], wfbk[a], NN)
-            value = term if value is None else value + term
-        dbuf_f[rows_at(i, half), :] = value
-
-    loop(2, back_fb)
-    bias_fa, gain_fa = slope_pass(sec_fa, stats_fa, "fa", dbuf_f)
-    put(6, 0, squash(bias_fa))
-    put(6, 1, squash(gain_fa))
-    put(6, 2, squash(bias_sa))
-    put(6, 4, squash(gain_sa))
-    exchange_start(6)
+    put("sa_back", 0, squash(bias_sa))
+    put("sa_back", 256, squash(gain_sa))
+    exchange_start("sa_back")
+    poll(3)
 
     for a in range(3):
         value = dot(gcs[band : band + rows, bs : 2 * bs], hcs[band * a : band * a + rows, :], TN)
@@ -822,9 +920,7 @@
         for b in range(3):
             ref[bs * b : bs * (b + 1), lane : lane + bs] = value[:, bs * b : bs * (b + 1)]
         advance("sb%d" % a)
-    exchange_middle(6)
-    advance("sc")
-    advance("sb0")
+    poll(4)
     for a in range(3):
         value = dot(gcf[band : band + rows, 128:256], hcf[band * a : band * a + rows, :], TN)
         for b in range(3):
@@ -834,66 +930,10 @@
             folded = jnp.where(lane_group[0:32] == tap % 4, folded, 0.0)
             at = slice(608 + 32 * (tap // 4), 640 + 32 * (tap // 4))
             slab[2, at, 128:256] = folded if tap % 4 == 0 else slab[2, at, 128:256] + folded
-    advance("sb1")
-    advance("sb2")
-    total = exchange_end(6)
-
-    fold_rows = fold_lanes(total[0:8, :])
-    bias_fa, gain_fa = fold_rows[0:1, :], fold_rows[1:2, :]
-    bias_sa, gain_sa = take(total, 2, 256), take(total, 4, 256)
+    poll(5)
+    bias_fa, gain_fa = unpair32(exchange_end("fa_back"))
     report("fa", bias_fa, gain_fa)
-    report("sa", bias_sa, gain_sa)
-    vec_sa = back_vectors("sa", stats_sa, bias_sa, gain_sa, slow_count)
     vec_fa = back_vectors("fa", stats_fa, bias_fa, gain_fa, fast_count)
-
-    def low_sa(i):
-        at = rows_at(i, band)
-        value = norm_grad(dbuf, sec_sa, at, vec_sa)
-        gcs[at, 0:bs] = roll_frames(value, prev256, -1, True).astype(BF16)
-        gcs[at, bs : 2 * bs] = value.astype(BF16)
-        gcs[at, 2 * bs :] = roll_frames(value, next256, 1, True).astype(BF16)
-
-    loop(bands, low_sa)
-
-    def narrow_gradient(k):
-        ref, lane = pieces["sa%d" % k]["ref"], pieces["sa%d" % k]["lane"]
-        source = xs[:, 256 * k : 256 * (k + 1)] if k < 4 else jl[...]
-        ref[0 : 3 * bs, lane : lane + 256] = dot(gcs[0:rows, :], source, TN)
-        advance("sa%d" % k)
-
-    narrow_gradient(0)
-
-    def back_lateral(i):
-        at = rows_at(i, half)
-        dbuf[at, :] = dot(gcs[at, :], wsa[:, cs_n:], NN)
-
-    loop(2, back_lateral)
-    bias_lat, gain_lat = slope_pass(sec_lat, stats_lat, "lat", dbuf)
-    put(7, 0, squash(bias_lat))
-    put(7, 2, squash(gain_lat))
-    exchange_start(7)
-
-    for name in ("sc", "sb0", "sb1", "sb2", "sa0"):
-        advance(name)
-    narrow_gradient(1)
-    narrow_gradient(2)
-    exchange_middle(7)
-    for name in ("sb0", "sb1", "sb2", "sa0", "sa1", "sa2"):
-        advance(name)
-    narrow_gradient(3)
-    narrow_gradient(4)
-    for name in ("sc", "sb0", "sb1", "sb2", "sa0", "sa1", "sa2", "sa3", "sa4"):
-        advance(name)
-
-    def slow_back(i):
-        at = rows_at(i, half)
-        for tile in range(cs_n // 256):
-            lanes = slice(256 * tile, 256 * (tile + 1))
-            value = gsum[at, lanes].astype(F32) + dot(gcs[at, :], wsa[:, lanes], NN)
-            gsum[at, lanes] = value.astype(BF16)
-
-    loop(2, slow_back)
-    sgrad_store = store(gsum, sgrad_h, 12)
 
     def low_fa(i):
         at = rows_at(i, band)
@@ -907,9 +947,49 @@
             term = value[32 * phase : 32 * (phase + 1), 128 * (phase + k) : 128 * (phase + k + 1)]
             piece = term if piece is None else piece + term
         slab[2, 512 + 32 * k : 544 + 32 * k, 128:256] = piece
-    total = exchange_end(7)
-
-    bias_lat, gain_lat = take(total, 0, 256), take(total, 2, 256)
+    poll(6)
+    total = exchange_end("sa_back")
+    poll(7)
+
+    bias_sa, gain_sa = take(total, 0, 256), take(total, 256, 256)
+    report("sa", bias_sa, gain_sa)
+    vec_sa = back_vectors("sa", stats_sa, bias_sa, gain_sa, slow_count)
+    def low_sa(i):
+        at = rows_at(i, band)
+        value = norm_grad(dbuf, sec_sa, at, vec_sa)
+        gcs[at, 0:bs] = roll_frames(value, prev256, -1, True).astype(BF16)
+        gcs[at, bs : 2 * bs] = value.astype(BF16)
+        gcs[at, 2 * bs :] = roll_frames(value, next256, 1, True).astype(BF16)
+
+    loop(bands, low_sa)
+
+    def narrow_gradient(k):
+        ref, lane = pieces["sa%d" % k]["ref"], pieces["sa%d" % k]["lane"]
+        source = xs[:, 256 * k : 256 * (k + 1)] if k < 4 else jl[...]
+        ref[0 : 3 * bs, lane : lane + 256] = dot(gcs[0:rows, :], source, TN)
+        advance("sa%d" % k)
+
+    narrow_gradient(0)
+    poll(8)
+
+    def back_lateral(i):
+        at = rows_at(i, half)
+        dbuf[at, :] = dot(gcs[at, :], wsa[:, cs_n:], NN)
+
+    loop(2, back_lateral)
+    bias_lat, gain_lat = slope_pass(sec_lat, stats_lat, "lat", dbuf)
+    put("lat_back", 0, squash(bias_lat))
+    put("lat_back", 256, squash(gain_lat))
+    exchange_start("lat_back")
+
+    poll(9)
+
+    for k in range(1, 4):
+        narrow_gradient(k)
+        poll(9 + k)
+    total = exchange_end("lat_back")
+
+    bias_lat, gain_lat = take(total, 0, 256), take(total, 256, 256)
     report("lat", bias_lat, gain_lat)
     vec_lat = back_vectors("lat", stats_lat, bias_lat, gain_lat, slow_count)
 
@@ -923,8 +1003,22 @@
         at, lane = 256 * (k % 3), 128 * (k // 3)
         slab[2, at : at + 256, lane : lane + 128] = value[:, 128 * k : 128 * (k + 1)]
     advance("lt")
-    for name in ("sb0", "sb1", "sb2", "sa0", "sa1", "sa2", "sa3", "sa4", "lt"):
-        advance(name)
+    poll(13)
+    narrow_gradient(4)
+    poll(14)
+
+    def slow_back(i):
+        at = rows_at(i, half)
+        for tile in range(cs_n // 256):
+            lanes = slice(256 * tile, 256 * (tile + 1))
+            value = gsum[at, lanes].astype(F32) + dot(gcs[at, :], wsa[:, lanes], NN)
+            gsum[at, lanes] = value.astype(BF16)
+
+    for part in range(2):
+        slow_back(part)
+        poll(15 + part)
+    sgrad_store = store(gsum, sgrad_h, 12)
+
     fast_store.wait()
 
     def fast_back(i):
@@ -945,10 +1039,12 @@
                 stage_a[pl.ds(phase, band, stride=4), :] = grads[phase][part * band : (part + 1) * band]
             xf[rows_at(2 * i + part, fband), :] = stage_a[...].astype(BF16)
 
-    loop(bands // 2, fast_back)
+    loop(bands // 4, fast_back)
+    poll(17)
+    loop(bands // 2 - bands // 4, lambda i: fast_back(i + bands // 4))
     fgrad_store = store(xf, fgrad_h, 13)
-    for name in ("sb0", "sb1", "sb2", "sa0", "sa1", "sa2", "sa3", "sa4", "lt"):
-        advance(name)
+    poll(18)
+
     def pack(rows_ref, target):
         lanes = lax.broadcasted_iota(jnp.int32, (24, LANES), 1)
         stacked = rows_ref[...]
@@ -961,14 +1057,30 @@
 
     pack(gain_rows, dgains)
     pack(bias_rows, dbiases)
-    while any(piece["step"] <= 8 for piece in pieces.values()):
+    poll(19)
+    while not all(done(name) for name in order):
         for name in order:
-            if pieces[name]["step"] <= 8:
+            if not done(name):
                 advance(name)
     for slot, copy in enumerate(stores):
         copy.wait()
     sgrad_store.wait()
     fgrad_store.wait()
+
+
+def hand_on(*refs):
+    sources, targets, held, sem = refs[0:13], refs[13:26], refs[26:34], refs[34]
+    loads = [pltpu.make_async_copy(sources[k], held[k], sem.at[k]) for k in range(8)]
+    stores = [pltpu.make_async_copy(held[k], targets[k], sem.at[8 + k]) for k in range(8)]
+    for copy in loads:
+        copy.start()
+    for k in range(8, 13):
+        targets[k][...] = sources[k][...]
+    for load, copy in zip(loads, stores):
+        load.wait()
+        copy.start()
+    for copy in stores:
+        copy.wait()
 
 
 def body(
@@ -1016,8 +1128,7 @@
     band = side * frames
     any_spec = pl.BlockSpec(memory_space=pl.ANY)
     vmem_spec = pl.BlockSpec(memory_space=pltpu.VMEM)
-    small = sum(1 for size in ROWS if size == 8)
-    large = len(ROWS) - small
+    near_low = n_dp if n_dp * n_rep <= 32 else low
     pad = rows + 2 * band
 
     def shape(dims, dtype):
@@ -1051,12 +1162,11 @@
         pltpu.VMEM((3, 128, 384), BF16), pltpu.VMEM((3, 384, 128), BF16), pltpu.VMEM((512, 128), BF16),
         pltpu.VMEM((4 * band, cf), F32), pltpu.VMEM((4 * band, cf), F32),
         pltpu.VMEM((24, LANES), F32), pltpu.VMEM((24, LANES), F32),
-        pltpu.VMEM((small, low * n_rep, 8, LANES), F32), pltpu.VMEM((large, low * n_rep, 24, LANES), F32),
-        pltpu.VMEM((small, high, 8, LANES), F32), pltpu.VMEM((large, high, 24, LANES), F32),
-        pltpu.SemaphoreType.DMA((len(ROWS),)), pltpu.SemaphoreType.DMA((len(ROWS),)),
-        pltpu.SemaphoreType.DMA((len(ROWS),)), pltpu.SemaphoreType.DMA((len(ROWS),)),
+        pltpu.VMEM((near_low * n_rep, 1, sum(TURNS.values())), F32),
+        pltpu.VMEM((max(n_dp // near_low, 1), 1, sum(TURNS.values())), F32),
+        pltpu.SemaphoreType.DMA((len(TURNS), 2)), pltpu.SemaphoreType.DMA((len(TURNS), 2)),
         pltpu.SemaphoreType.DMA((32,)), pltpu.SemaphoreType.DMA((10, 2)),
-        pltpu.SemaphoreType.DMA((10, 9)), pltpu.SemaphoreType.DMA((10, 9)),
+        pltpu.SemaphoreType.DMA((10, 11)), pltpu.SemaphoreType.DMA((10, 11)),
     ]
     factor = 1.0 / math.sqrt(float(slow_count))
     results = pl.pallas_call(
@@ -1074,7 +1184,18 @@
         lateral_conv.reshape(-1, cf), slow_narrow.reshape(3 * bs, -1), slow_spatial.reshape(9 * bs, bs),
         slow_widen, lay_out(norm_gains), lay_out(norm_biases),
     )
-    slow_out, fast_out, slow_grad, fast_grad, dsa, dsb, dsc, dl, dfa, dfb, dfc, dgains, dbiases, _ = results
+    results = list(results[0:13])
+    handed = pl.pallas_call(
+        hand_on,
+        out_shape=out_shape[0:13],
+        in_specs=[any_spec] * 8 + [vmem_spec] * 5,
+        out_specs=[any_spec] * 8 + [vmem_spec] * 5,
+        scratch_shapes=[pltpu.VMEM(item.shape, item.dtype) for item in out_shape[0:8]]
+        + [pltpu.SemaphoreType.DMA((16,))],
+        compiler_params=pltpu.CompilerParams(vmem_limit_bytes=64000 * 2**10),
+    )(*results)
+    slow_out, fast_out, slow_grad, fast_grad, dsa, dsb, dsc, dl, dfa, dfb, dfc, dgains, dbiases = handed
+
     def gather(packed):
         return packed.reshape(16 * LANES)[0 : sum(widths)]
 

time: 183 us -> 152 us (0.83)
  local copies, waits for them, and re-layouts: 21.5 us -> 1.32 us
  Pallas kernels: 160 us -> 150 us
    pallas_call x1, Pallas kernels: 160 us -> 136 us  [body(): pl.pallas_call(functools.partial(kernel, (n_dp, n_rep, low, frames, side,...]
    unnamed x37 -> x0, local copies, waits for them, and re-layouts: 20.1 us -> none
    pallas_call x0 -> x1, Pallas kernels: none -> 13.4 us  [body(): pl.pallas_call(hand_on, out_shape=out_shape[0:13], in_specs=[any_spec] *...]
where the time goes in v3:
time: 152 us
  Pallas kernels  150 us (99%)
    pallas_call x1, Pallas kernels, body(): pl.pallas_call(functools.partial(kernel, (n_dp, n_rep, low, frames, side,...  136 us
    pallas_call x1, Pallas kernels, body(): pl.pallas_call(hand_on, out_shape=out_shape[0:13], in_specs=[any_spec] *...  13.4 us

profile of v3, /device:TPU:0, one launch (start us, length us, event | category | flops | bytes accessed | tf_op | source)
XLA Modules:
  0.0 151.8 jit_solution(14474515353699464636)
XLA Ops:
  0.6 1.3 pad_bitcast_fusion
  2.0 136.2 %shard_map.237 = (bf16[1568,1024]{1,0:T(8,128)(2,1)}, bf16[6272,128]{1,0:T(8,128)(2,1)}, bf16[1568,1024]{1,0:T(8,128)(2,1)}, bf16[6272,128]{1,0:T(8,128)(2,1)}, ...) custom-call(bf16[1568,1024]{1,0:T(8,128)(2,1)} %bitcast.44, ...), custom_call_target="tpu_custom_call" | custom-call | tf_op jit(solution)/shard_map/pallas_call | solution.py:1172
  138.2 13.4 %shard_map.238 = (bf16[1568,1024]{1,0:T(8,128)(2,1)}, bf16[6272,128]{1,0:T(8,128)(2,1)}, bf16[1568,1024]{1,0:T(8,128)(2,1)}, bf16[6272,128]{1,0:T(8,128)(2,1)}, ...) custom-call(bf16[1568,1024]{1,0:T(8,128)(2,1)} %get-tuple-element.39, ...), custom_call_target="tpu_custom_call" | custom-call | tf_op jit(solution)/shard_map/pallas_call | solution.py:1188

commit v4 on v3

--- a/solution.py
+++ b/solution.py
@@ -23,37 +23,57 @@
 }
 
 
-LINES = ('sb2', )
+ORDERS = {
+    "plane": (("c", "x", "y", "z"), ("c", "y", "x", "z")),
+    "halves": (("c", "x", "y", "z0", "z1"), ("c", "y", "x", "z0", "z1")),
+    "between": (("c", "x", "z0", "z1", "y"), ("c", "y", "z0", "z1", "x")),
+    "line": (("c", "z0", "z1", "x", "y"), ("c", "z0", "z1", "y", "x")),
+}
+ORDER_OF = {
+    "sc": "halves",
+    "sb0": "halves",
+    "sb1": "line",
+    "sb2": "plane",
+    "sa0": "halves",
+    "sa1": "between",
+    "sa2": "plane",
+    "sa3": "plane",
+    "sa4": "halves",
+    "lt": "halves",
+}
 POLLS = (
-    '',
-    'sc',
-    '',
-    '',
-    'sb0 sc',
-    'sb1',
-    'sb2',
-    '',
-    '',
-    'sb0 sc sa0',
-    '',
-    'sb2 sb1',
-    'sb0 sa1',
-    'sa0 sc sa2',
-    'sb1 sa3 lt',
-    'sa1',
-    'sa0 sa4 sb2',
-    'sb0 sa2',
-    '',
-    'sa3 sc lt sa1 sa4 sa0 sb1 sa2 sb0 sa3 sa1 sc sa4 lt sa0 sb2 sb0 sb1 sa2 sc sa0 sa3 sb2 sc sa1 sb0 sb1 sb2 sa4 sa1 sa0 lt sb1 sa0 sa2 sa1 sa3 sa2 sb1 sb2 sa1 sa4 lt sa3 sb0 sa4 lt sa2 sb2 sa3 sa3 sa4 sa2 sa4 lt sb2 lt sb2',
+    (),
+    ("sc",),
+    (),
+    (),
+    ("sc", "sb0"),
+    ("sb1",),
+    ("sb2",),
+    (),
+    ("sc",),
+    ("sb0", "sa0"),
+    ("sb2", "sb1"),
+    ("sc",),
+    ("sb0", "sa1"),
+    ("sa0", "sb2", "sa2", "sa3"),
+    ("sb0", "sb1", "lt"),
+    ("sa0", "sc", "sa1", "sa4"),
+    ("sb2", "sa2"),
+    ("sb0",),
+    ("sa0", "sc", "sa3", "sb1"),
+    (
+        "lt", "sa1", "sa4", "sb0", "sa2", "sb2", "sa0", "lt", "sc", "sa4", "sa3", "sa1",
+        "sb0", "sb2", "sa2", "lt", "sa0", "sc", "sa4", "sb1", "sb0", "sa3", "sb2", "sa1",
+        "sa0", "sa2", "lt", "sc", "sb1", "sa4", "sb2", "sa1", "sb0", "sa3", "lt", "sa0",
+        "sa2", "sa4", "sc", "sb1", "sa3", "sa1", "lt", "sb0", "sa0", "sa2", "sa4", "sb1",
+        "sa1", "sa3", "sa2", "lt", "sa0", "sa4", "sa3", "sa1", "sb1", "lt", "sa4", "sb1",
+        "sa1", "lt", "sa4",
+    ),
 )
 
 
 def dot(left, right, dims):
     return lax.dot_general(left, right, (dims, ((), ())), preferred_element_type=F32)
-
-
-def sigmoid(values):
-    return 0.5 * jnp.tanh(0.5 * values) + 0.5
 
 
 def column_sums(values):
@@ -69,16 +89,16 @@
     return half + pltpu.roll(half, 32, 1)
 
 
-def loop(count, body, init=None):
+def loop(count, body, init=None, unroll=1):
     if init is None:
 
         def plain(index, carry):
             body(index)
             return carry
 
-        lax.fori_loop(0, count, plain, 0)
+        lax.fori_loop(0, count, plain, 0, unroll=unroll)
         return None
-    return lax.fori_loop(0, count, body, init)
+    return lax.fori_loop(0, count, body, init, unroll=unroll)
 
 
 def rows_at(index, size):
@@ -87,11 +107,11 @@
 
 def kernel(
     dims,
-    xs_h, xf_h, cs_h, cf_h, clip, wfa_h, wfb_h, wfc_h, wl_h, wsa_h, wsb_h, wsc_h, gains_in, biases_in,
-    slow_h, fast_h, sgrad_h, fgrad_h, dsa_h, dsb_h, dsc_h, dl_h, dfa, dfb, dfc, dgains, dbiases, extra_h,
+    xs_h, xf_h, cs_h, cf_h, clip, wfa_h, wfb_h, wfc_h, wl_h, wsa_h, wsb_h, wsc_h, gains_h, biases_h,
+    slow_h, fast_h, sgrad_h, fgrad_h, dsa_h, dsb_h, dsc_h, dl_h, small_h, dgains_h, dbiases_h, extra_h,
     xs, cs, gsum, xf, cf, big, sec_fc, gsf, hcs, gcs, hcf, gcf,
     sec_lat, sec_sa, sec_sb, dbuf, sec_fa, sec_fb, dbuf_f, jl, hbs, hbf, vx, slab, slab_sc, summed, gathered,
-    wsa, wsb, wsc, wfa_in, wfb_in, wfc_in, wlat, wfa, wfb, wfbk, wfc,
+    wsa, wsb, wsc, gains_in, biases_in, vectors, masks, wfa_in, wfb_in, wfc_in, wlat, wfa, wfb, wfbk, wfc,
     stage_a, stage_b, gain_rows, bias_rows, near, far, sum_send, sum_recv, io_sem, own_sem, big_send, big_recv,
 ):
     n_dp, n_rep, low, frames, side, slow_count, fast_count, factor = dims
@@ -142,7 +162,7 @@
     for slot, (name, src, dst) in enumerate([
         ("xf", xf_h, xf), ("wfa", wfa_h, wfa_in), ("xs", xs_h, xs),
         ("wsa", wsa_h, wsa), ("wfb", wfb_h, wfb_in), ("wfc", wfc_h, wfc_in), ("wsb", wsb_h, wsb),
-        ("wsc", wsc_h, wsc), ("cf", cf_h, cf), ("cs", cs_h, cs),
+        ("wsc", wsc_h, wsc), ("cf", cf_h, cf), ("cs", cs_h, cs), ("gains", gains_h, gains_in), ("biases", biases_h, biases_in),
     ]):
         loads[name] = pltpu.make_async_copy(src, dst, io_sem.at[slot])
         loads[name].start()
@@ -174,8 +194,8 @@
         buffer = stages[stage][0]
         block = buffer.at[pl.ds(first, count), :, pl.ds(turn_at[turn], TURNS[turn])]
         return pltpu.make_async_remote_copy(
-            src_ref=block, dst_ref=block, send_sem=sum_send.at[turn_index[turn], stage],
-            recv_sem=sum_recv.at[turn_index[turn], stage], device_id=peer, device_id_type=MESH,
+            src_ref=block, dst_ref=block, send_sem=sum_send.at[stage, turn_index[turn]],
+            recv_sem=sum_recv.at[stage, turn_index[turn]], device_id=peer, device_id_type=MESH,
         )
 
     def exchange_start(turn):
@@ -216,11 +236,9 @@
 
     bits = {"c": (c, core_peer), "x": (x, x_peer), "y": (y, y_peer),
             "z0": (lax.rem(z, 2), z_peer(1)), "z1": (lax.div(z, 2), z_peer(2))}
-    PLANE_FIRST = (("c", "x", "y", "z"), ("c", "y", "x", "z"))
-    LINE_FIRST = (("c", "z0", "z1", "x", "y"), ("c", "z0", "z1", "y", "x"))
 
     def add_piece(name, ref, lane, size, index):
-        axes = LINE_FIRST if name in LINES else PLANE_FIRST
+        axes = ORDERS[ORDER_OF[name]]
         piece = {"name": name, "ref": ref, "lane": lane, "size": size, "index": index, "step": 0, "axes": axes}
         starts, counts, arriving = [[0], [0]], [size], [size]
         for step, pair in enumerate(zip(*axes)):
@@ -248,7 +266,7 @@
 
     def send(piece, step, src, dst, peer):
         pltpu.make_async_remote_copy(
-            src_ref=src, dst_ref=dst, send_sem=big_send.at[piece["index"], step],
+            src_ref=src, dst_ref=dst, send_sem=big_send.at[piece["index"]],
             recv_sem=big_recv.at[piece["index"], step], device_id=peer, device_id_type=MESH,
         ).start()
 
@@ -278,7 +296,7 @@
     def arrived(piece, step, rows_in):
         block = span(piece, 0, rows_in) if step < piece["steps"] else result(piece, 0, rows_in)
         copy = pltpu.make_async_remote_copy(
-            src_ref=block, dst_ref=block, send_sem=big_send.at[piece["index"], step],
+            src_ref=block, dst_ref=block, send_sem=big_send.at[piece["index"]],
             recv_sem=big_recv.at[piece["index"], step], device_id=core_peer, device_id_type=MESH,
         )
         copy.wait_recv()
@@ -300,15 +318,10 @@
     def unpack_small():
         stores.append(store(summed.at[:, pl.ds(0, 128)], dl_h.at[pl.ds(0, 768)], 16))
         stores.append(store(summed.at[pl.ds(0, 512), pl.ds(128, 128)], dl_h.at[pl.ds(768, 512)], 17))
-        dfa[...] = summed[512:608, 128:256]
-        for tap in range(9):
-            at = 608 + 32 * (tap // 4)
-            block = summed[at : at + 32, 128:256]
-            dfb[32 * tap : 32 * (tap + 1), :] = block[:, 32 * (tap % 4) : 32 * (tap % 4 + 1)]
-        dfc[...] = summed[704:736, 128:256]
+        stores.append(store(summed.at[pl.ds(512, 256), pl.ds(128, 128)], small_h, 18))
 
     def poll(turn):
-        for name in POLLS[turn].split():
+        for name in POLLS[turn]:
             advance(name)
 
     def done(name):
@@ -376,7 +389,7 @@
                     send(piece, 10, held, extra_h.at[index, outer, pl.ds(0, last)], peer)
                 block = extra_h.at[index, pl.ds(0, outers - 1), pl.ds(0, last)]
                 copy = pltpu.make_async_remote_copy(
-                    src_ref=block, dst_ref=block, send_sem=big_send.at[index, 10], recv_sem=big_recv.at[index, 10],
+                    src_ref=block, dst_ref=block, send_sem=big_send.at[index], recv_sem=big_recv.at[index, 10],
                     device_id=core_peer, device_id_type=MESH,
                 )
                 copy.wait_recv()
@@ -423,31 +436,55 @@
         fb = fold_lanes(jnp.where(lane16 // 32 == 1, packed, 0.0))[0:1, :]
         turned = pltpu.roll(packed, 64, 1)
         moved = jnp.where(lane16 < 64, turned, pltpu.roll(turned, 15, 0))
-        vectors = {"fa": fa, "fb": fb}
+        found = {"fa": fa, "fb": fb}
         at = 0
         for name, count in (("fc", 1), ("lat", 2), ("sa", 2), ("sb", 2), ("sc", 8)):
-            vectors[name] = jnp.concatenate([moved[at + k : at + k + 1, :] for k in range(count)], axis=1)
+            found[name] = jnp.concatenate([moved[at + k : at + k + 1, :] for k in range(count)], axis=1)
             at += count
-        return vectors
-
-    gains, biases = unpack(gains_in[...]), unpack(biases_in[...])
+        return found
+
+    held = [0]
+
+    def settle(vector):
+        at, width = held[0], vector.shape[1]
+        held[0] += 1
+        vectors[at, 0:1, 0:width] = vector
+
+        def read(lanes=slice(0, width)):
+            return vectors[at, 0:1, lanes]
+
+        return read
+
+    gains, biases = {}, {}
+
+    def read_parameters():
+        for name, flat_in, target in (("gains", gains_in, gains), ("biases", biases_in, biases)):
+            loads[name].wait()
+            count = flat_in.shape[0]
+            stage_a[0:16, :] = jnp.zeros((16, LANES), F32)
+            for row in range(16):
+                width = min(LANES, count - row * LANES)
+                stage_a[row : row + 1, 0:width] = flat_in[pl.ds(row * LANES, width)].reshape(1, width)
+            for key, vector in unpack(stage_a[0:16, :]).items():
+                target[key] = settle(vector)
 
     def gain(name):
-        return gains[name]
+        return gains[name]()
 
     def bias(name):
-        return biases[name]
-
-    def moments(total, squares, count):
+        return biases[name]()
+
+    def moments(name, total, squares, count):
         mean = total * (1.0 / count)
-        return mean, lax.rsqrt(squares * (1.0 / count) - mean * mean + EPS)
+        scale = lax.rsqrt(squares * (1.0 / count) - mean * mean + EPS)
+        return settle(mean), settle(scale), settle(0.5 * gain(name) * scale), settle(0.5 * bias(name))
 
     def back_vectors(name, stats, bias_total, gain_total, count):
-        mean, scale = stats
+        mean, scale = stats[0](), stats[1]()
         lead = gain(name) * scale
         tilt = lead * scale * gain_total * (1.0 / count)
         level = lead * bias_total * (1.0 / count) - mean * tilt
-        return lead, level, tilt
+        return settle(lead), settle(level), settle(tilt)
 
     def report(name, bias_total, gain_total):
         at = spots[name]
@@ -456,10 +493,14 @@
             gain_rows[at + piece : at + piece + 1, :] = gain_total[:, lanes]
             bias_rows[at + piece : at + piece + 1, :] = bias_total[:, lanes]
 
-    def before_act(values, stats, name):
-        mean, scale = stats
-        normed = (values - mean) * scale
-        return normed, normed * gain(name) + bias(name)
+    def silu_of(values, stats):
+        h = (values - stats[0]()) * stats[2]() + stats[3]()
+        return h + h * jnp.tanh(h)
+
+    def slope_of(h):
+        t = jnp.tanh(h)
+        out, gate = h + h * t, 0.5 + 0.5 * t
+        return out, gate + out * (1.0 - gate)
 
     def clip_masks(width):
         frame = lax.broadcasted_iota(jnp.int32, (1, 8, width), 1)
@@ -471,6 +512,14 @@
             with_next = jnp.where(frame == t - 1, same, with_next)
         return with_prev, with_next
 
+    masks[0:1], masks[1:2] = clip_masks(256)
+
+    def prev(width):
+        return masks[0:1, :, 0:width]
+
+    def following(width):
+        return masks[1:2, :, 0:width]
+
     def roll_frames(values, mask, step, mask_first):
         grouped = values.reshape(values.shape[0] // 8, 8, values.shape[1])
         if mask_first:
@@ -495,9 +544,13 @@
         target[0:band, :] = edge
         target[band + rows : rows + 2 * band, :] = edge
 
-    lane_group = lax.broadcasted_iota(jnp.int32, (LANES, LANES), 1) // 32
-    row_group = lax.broadcasted_iota(jnp.int32, (LANES, LANES), 0) // 32
-    block_mask = jnp.where(lane_group == row_group, 1.0, 0.0)
+    def lane_groups(count=LANES):
+        return lax.broadcasted_iota(jnp.int32, (count, LANES), 1) // 32
+
+    def block_mask():
+        row_group = lax.broadcasted_iota(jnp.int32, (LANES, LANES), 0) // 32
+        return jnp.where(lane_groups() == row_group, 1.0, 0.0)
+
     repeat_lanes = jnp.where(
         lax.broadcasted_iota(jnp.int32, (32, LANES), 1) % 32 == lax.broadcasted_iota(jnp.int32, (32, LANES), 0),
         1.0, 0.0,
@@ -510,20 +563,19 @@
             wfa[32 * phase : 32 * (phase + 1), LANES * (phase + k) : LANES * (phase + k + 1)] = wfa_in[
                 32 * k : 32 * (k + 1), :
             ]
-    prev128, next128 = clip_masks(128)
     loads["xf"].wait()
 
     def arrange(i):
         at = rows_at(i, band)
         stage_a[...] = xf[rows_at(i, fband), :].astype(F32)
         phases = [stage_a[pl.ds(phase, band, stride=4), :] for phase in range(4)]
-        vx[at, 0:128] = roll_frames(phases[2], prev128, 1, False).astype(BF16)
-        vx[at, 128:256] = roll_frames(phases[3], prev128, 1, False).astype(BF16)
+        vx[at, 0:128] = roll_frames(phases[2], prev(128), 1, False).astype(BF16)
+        vx[at, 128:256] = roll_frames(phases[3], prev(128), 1, False).astype(BF16)
         for phase in range(4):
             vx[at, 256 + 128 * phase : 384 + 128 * phase] = phases[phase].astype(BF16)
-        vx[at, 768:896] = roll_frames(phases[0], next128, -1, False).astype(BF16)
-
-    loop(bands, arrange)
+        vx[at, 768:896] = roll_frames(phases[0], following(128), -1, False).astype(BF16)
+
+    loop(bands, arrange, unroll=2)
     for tap in taps:
         tap.wait()
 
@@ -567,26 +619,25 @@
     for a in range(3):
         for b in range(3):
             piece = spread[32 * (3 * a + b) : 32 * (3 * a + b + 1), :]
-            block = (jnp.concatenate([piece] * 4, axis=0) * block_mask).astype(BF16)
+            block = (jnp.concatenate([piece] * 4, axis=0) * block_mask()).astype(BF16)
             wfb[a, :, LANES * b : LANES * (b + 1)] = block
             wfbk[a, LANES * (2 - b) : LANES * (3 - b), :] = block
     widen = dot(wfc_in[...], repeat_lanes, TN)
     for phase in range(4):
-        wfc[LANES * phase : LANES * (phase + 1), :] = jnp.where(lane_group == phase, widen, 0.0).astype(BF16)
+        wfc[LANES * phase : LANES * (phase + 1), :] = jnp.where(lane_groups() == phase, widen, 0.0).astype(BF16)
+    read_parameters()
     total = exchange_end("lat")
 
-    stats_lat = moments(take(total, 0, 256), take(total, 256, 256), slow_count)
+    stats_lat = moments("lat", take(total, 0, 256), take(total, 256, 256), slow_count)
 
     def act_fa(i):
-        normed, pre = before_act(sec_fa[rows_at(i, band), :], stats_fa, "fa")
-        spread_columns(hcf, i, pre * sigmoid(pre))
+        spread_columns(hcf, i, silu_of(sec_fa[rows_at(i, band), :], stats_fa))
 
     def act_lat(i):
-        at = rows_at(i, band)
-        normed, pre = before_act(sec_lat[at, :], stats_lat, "lat")
-        jl[at, :] = (pre * sigmoid(pre)).astype(BF16)
-
-    loop(bands, act_lat)
+        at = rows_at(i, 2 * band)
+        jl[at, :] = silu_of(sec_lat[at, :], stats_lat).astype(BF16)
+
+    loop(bands // 2, act_lat)
 
     def conv_fb(i, carry):
         value = None
@@ -603,14 +654,13 @@
             big[at, bs * k : bs * (k + 1)] += dot(jl[at, :], wsa[bs * k : bs * (k + 1), cs_n:], NT)
 
     loop(2, narrow_lateral)
-    prev256, next256 = clip_masks(256)
 
     def combine_sa(i, carry):
         at = rows_at(i, band)
         value = (
             big[at, bs : 2 * bs]
-            + roll_frames(big[at, 0:bs], prev256, 1, False)
-            + roll_frames(big[at, 2 * bs : 3 * bs], next256, -1, False)
+            + roll_frames(big[at, 0:bs], prev(256), 1, False)
+            + roll_frames(big[at, 2 * bs : 3 * bs], following(256), -1, False)
         )
         sec_sa[at, :] = value
         return carry[0] + column_sums(value), carry[1] + column_sums(value * value)
@@ -621,25 +671,23 @@
     exchange_start("sa")
 
     total = exchange_end("fa")
-    stats_fa = moments(*unpair32(total), fast_count)
-    loop(bands, act_fa)
+    stats_fa = moments("fa", *unpair32(total), fast_count)
+    loop(bands, act_fa, unroll=2)
     sum_fb, sq_fb = loop(2, conv_fb, zero2(128))
     put("fb", 0, pair32(squash(sum_fb), squash(sq_fb)))
     exchange_start("fb")
     total = exchange_end("sa")
 
-    stats_sa = moments(take(total, 0, 256), take(total, 256, 256), slow_count)
+    stats_sa = moments("sa", take(total, 0, 256), take(total, 256, 256), slow_count)
 
     def act_sa(i):
-        normed, pre = before_act(sec_sa[rows_at(i, band), :], stats_sa, "sa")
-        spread_columns(hcs, i, pre * sigmoid(pre))
+        spread_columns(hcs, i, silu_of(sec_sa[rows_at(i, band), :], stats_sa))
 
     def act_fb(i):
-        at = rows_at(i, band)
-        normed, pre = before_act(sec_fb[at, :], stats_fb, "fb")
-        hbf[at, :] = (pre * sigmoid(pre)).astype(BF16)
-
-    loop(bands, act_sa)
+        at = rows_at(i, 2 * band)
+        hbf[at, :] = silu_of(sec_fb[at, :], stats_fb).astype(BF16)
+
+    loop(bands, act_sa, unroll=2)
     loads["wsb"].wait()
 
     def conv_sb(i, carry):
@@ -659,8 +707,8 @@
     exchange_start("sb")
 
     total = exchange_end("fb")
-    stats_fb = moments(*unpair32(total), fast_count)
-    loop(bands, act_fb)
+    stats_fb = moments("fb", *unpair32(total), fast_count)
+    loop(bands // 2, act_fb)
 
     def widen_fast(i, carry):
         at = rows_at(i, half)
@@ -678,16 +726,15 @@
     exchange_start("fc")
     total = exchange_end("sb")
 
-    stats_sb = moments(take(total, 0, 256), take(total, 256, 256), slow_count)
+    stats_sb = moments("sb", take(total, 0, 256), take(total, 256, 256), slow_count)
 
     def act_sb(i, carry):
-        at = rows_at(i, band)
-        normed, pre = before_act(sec_sb[at, :], stats_sb, "sb")
-        value = (pre * sigmoid(pre)).astype(BF16)
+        at = rows_at(i, 2 * band)
+        value = silu_of(sec_sb[at, :], stats_sb).astype(BF16)
         hbs[at, :] = value
         return carry + column_sums(value.astype(F32))
 
-    sum_hbs = loop(bands, act_sb, jnp.zeros((8, bs), F32))
+    sum_hbs = loop(bands // 2, act_sb, jnp.zeros((8, bs), F32))
     loads["wsc"].wait()
     mid = cs_n // 2
 
@@ -708,7 +755,7 @@
     put("sc1", 0, squash(widen_slow(1)))
     exchange_start("sc1")
     total = exchange_end("fc")
-    stats_fc = moments(take(total, 0, 128), take(total, 128, 128), fast_count)
+    stats_fc = moments("fc", take(total, 0, 128), take(total, 128, 128), fast_count)
 
     loads["cf"].wait()
 
@@ -718,93 +765,81 @@
         stage_b[...] = cf[fat, :].astype(F32)
         for phase in range(4):
             lanes = slice(128 * phase, 128 * (phase + 1))
-            mean, scale = stats_fc
-            normed = (sec_fc[at, lanes] - mean) * scale
+            centred = sec_fc[at, lanes] - stats_fc[0]()
             total_in = vx[at, 256 + 128 * phase : 384 + 128 * phase].astype(F32)
-            value = total_in + normed * gain("fc") + bias("fc")
-            gate = sigmoid(value)
-            stage_a[pl.ds(phase, band, stride=4), :] = value * gate
-            grad = stage_b[pl.ds(phase, band, stride=4), :] * (gate * (1.0 + value * (1.0 - gate)))
+            out, slope = slope_of(0.5 * total_in + (centred * stats_fc[2]() + stats_fc[3]()))
+            stage_a[pl.ds(phase, band, stride=4), :] = out
+            grad = stage_b[pl.ds(phase, band, stride=4), :] * slope
             gsf[at, lanes] = grad
             bias_sum = bias_sum + column_sums(grad)
-            gain_sum = gain_sum + column_sums(grad * normed)
+            gain_sum = gain_sum + column_sums(grad * centred)
         xf[fat, :] = stage_a[...].astype(BF16)
         return bias_sum, gain_sum
 
     bias_fc, gain_fc = loop(bands, finish_fast, zero2(128))
     fast_store = store(xf, fast_h, 10)
     put("fc_back", 0, squash(bias_fc))
-    put("fc_back", 128, squash(gain_fc))
+    put("fc_back", 128, squash(gain_fc) * stats_fc[1]())
     exchange_start("fc_back")
     loads["cs"].wait()
     total = exchange_end("sc0")
-    squares = jnp.concatenate([take(total, 256, mid), exchange_end("sc1")], axis=1)
-    whole = lax.dot_general(
-        jnp.broadcast_to(take(total, 0, 256), (8, bs)), wsc[...].astype(F32), (NT, ((), ())),
-        precision=lax.Precision.HIGHEST, preferred_element_type=F32,
-    )[0:1, :]
-
-    stats_sc = moments(whole, squares, slow_count)
-    thin = 32
-    mean_sc, scale_sc = stats_sc
-    half_lead = 0.5 * gain("sc") * scale_sc
-    half_level = 0.5 * bias("sc") - mean_sc * half_lead
+    squares = take(total, 256, mid)
+    whole = settle(
+        lax.dot_general(
+            jnp.broadcast_to(take(total, 0, 256), (8, bs)), wsc[...].astype(F32), (NT, ((), ())),
+            precision=lax.Precision.HIGHEST, preferred_element_type=F32,
+        )[0:1, :]
+    )
+    squares = jnp.concatenate([squares, exchange_end("sc1")], axis=1)
+    stats_sc = moments("sc", whole(), squares, slow_count)
 
     def finish_slow(part):
         lanes = slice(part * mid, (part + 1) * mid)
-        lead, level = half_lead[:, lanes], half_level[:, lanes]
-        mean, scale = mean_sc[:, lanes], scale_sc[:, lanes]
-
         def step(i, carry):
-            at = rows_at(i, thin)
-            section = big[at, lanes]
-            h = 0.5 * xs[at, lanes].astype(F32) + (section * lead + level)
-            t = jnp.tanh(h)
-            out = h + h * t
-            gate = 0.5 + 0.5 * t
-            grad = cs[at, lanes].astype(F32) * (gate + out * (1.0 - gate))
-            normed = (section - mean) * scale
+            at = rows_at(i, band)
+            mean, lead, level = [stats_sc[k](lanes) for k in (0, 2, 3)]
+            centred = big[at, lanes] - mean
+            out, slope = slope_of(0.5 * xs[at, lanes].astype(F32) + (centred * lead + level))
+            grad = cs[at, lanes].astype(F32) * slope
             cs[at, lanes] = out.astype(BF16)
-            gsum[at, lanes] = normed.astype(BF16)
+            gsum[at, lanes] = centred.astype(BF16)
             big[at, lanes] = grad
-            return carry[0] + column_sums(grad), carry[1] + column_sums(grad * normed)
-
-        return loop(rows // thin, step, zero2(mid))
+            return carry[0] + column_sums(grad), carry[1] + column_sums(grad * centred)
+
+        bias_part, gain_part = loop(bands, step, zero2(mid))
+        return squash(bias_part), squash(gain_part) * stats_sc[1](lanes)
 
     for part in range(2):
         bias_part, gain_part = finish_slow(part)
-        put("sc%d_back" % part, 0, squash(bias_part))
-        put("sc%d_back" % part, mid, squash(gain_part))
+        put("sc%d_back" % part, 0, bias_part)
+        put("sc%d_back" % part, mid, gain_part)
         exchange_start("sc%d_back" % part)
     slow_store = store(cs, slow_h, 11)
 
     total = exchange_end("fc_back")
     bias_fc, gain_fc = take(total, 0, 128), take(total, 128, 128)
     report("fc", bias_fc, gain_fc)
-    def slope_pass(section, stats, name, buffer):
+    def slope_pass(section, stats, buffer):
         def step(i, carry):
-            at = rows_at(i, band)
-            normed, pre = before_act(section[at, :], stats, name)
-            gate = sigmoid(pre)
-            grad = buffer[at, :] * (gate * (1.0 + pre * (1.0 - gate)))
+            at = rows_at(i, 2 * band)
+            centred = section[at, :] - stats[0]()
+            grad = buffer[at, :] * slope_of(centred * stats[2]() + stats[3]())[1]
             buffer[at, :] = grad
-            return carry[0] + column_sums(grad), carry[1] + column_sums(grad * normed)
-
-        return loop(bands, step, zero2(section.shape[1]))
-
-    mean_fc, scale_fc = stats_fc
-    lead_fc = gain("fc") * scale_fc
-    tilt_fc = lead_fc * scale_fc * gain_fc * (1.0 / fast_count)
-    level_fc = lead_fc * bias_fc * (1.0 / fast_count) - mean_fc * tilt_fc
+            return carry[0] + column_sums(grad), carry[1] + column_sums(grad * centred)
+
+        bias_sum, gain_sum = loop(bands // 2, step, zero2(section.shape[1]))
+        return squash(bias_sum), squash(gain_sum) * stats[1]()
+
+    lead_fc, level_fc, tilt_fc = back_vectors("fc", stats_fc, bias_fc, gain_fc, fast_count)
 
     def low_fc(i):
         at = rows_at(i, band)
         for phase in range(4):
             lanes = slice(128 * phase, 128 * (phase + 1))
-            value = gsf[at, lanes] * lead_fc - level_fc - sec_fc[at, lanes] * tilt_fc
+            value = gsf[at, lanes] * lead_fc() - level_fc() - sec_fc[at, lanes] * tilt_fc()
             cf[pl.ds(pl.multiple_of(rows * phase + i * band, 16), band), :] = value.astype(BF16)
 
-    loop(bands, low_fc)
+    loop(bands, low_fc, unroll=2)
 
     def back_fc(i):
         value = None
@@ -815,8 +850,8 @@
         dbuf_f[rows_at(i, half), :] = value
 
     loop(2, back_fc)
-    bias_fb, gain_fb = slope_pass(sec_fb, stats_fb, "fb", dbuf_f)
-    put("fb_back", 0, pair32(squash(bias_fb), squash(gain_fb)))
+    bias_fb, gain_fb = slope_pass(sec_fb, stats_fb, dbuf_f)
+    put("fb_back", 0, pair32(bias_fb, gain_fb))
     exchange_start("fb_back")
     slow_store.wait()
     sums = [exchange_end("sc%d_back" % part) for part in range(2)]
@@ -824,17 +859,18 @@
     bias_sc = jnp.concatenate([take(total, 0, mid) for total in sums], axis=1)
     gain_sc = jnp.concatenate([take(total, mid, mid) for total in sums], axis=1)
     report("sc", bias_sc, gain_sc)
-    lead_sc = gain("sc") * stats_sc[1]
-    level_sc = lead_sc * bias_sc * (1.0 / slow_count)
-    tilt_sc = lead_sc * gain_sc * (1.0 / slow_count)
+    lead_sc = gain("sc") * stats_sc[1]()
+    tilt_sc = settle(lead_sc * stats_sc[1]() * gain_sc * (1.0 / slow_count))
+    level_sc = settle(lead_sc * bias_sc * (1.0 / slow_count))
+    lead_sc = settle(lead_sc)
 
     def low_sc(i):
-        at = rows_at(i, thin)
+        at = rows_at(i, 32)
         grad = big[at, :]
-        cs[at, :] = (grad * lead_sc - level_sc - gsum[at, :].astype(F32) * tilt_sc).astype(BF16)
+        cs[at, :] = (grad * lead_sc() - level_sc() - gsum[at, :].astype(F32) * tilt_sc()).astype(BF16)
         gsum[at, :] = grad.astype(BF16)
 
-    loop(rows // thin, low_sc)
+    loop(rows // 32, low_sc, unroll=7)
 
     def back_sc(i):
         at = rows_at(i, half)
@@ -842,10 +878,10 @@
 
     loop(2, back_sc)
 
-    bias_sb, gain_sb = slope_pass(sec_sb, stats_sb, "sb", dbuf)
-
-    put("sb_back", 0, squash(bias_sb))
-    put("sb_back", 256, squash(gain_sb))
+    bias_sb, gain_sb = slope_pass(sec_sb, stats_sb, dbuf)
+
+    put("sb_back", 0, bias_sb)
+    put("sb_back", 256, gain_sb)
     exchange_start("sb_back")
 
     slab_sc[0:cs_n, :] = dot(cs[...], hbs[...], TN)
@@ -864,12 +900,12 @@
 
     def norm_grad(buffer, section, at, vectors):
         lead, level, tilt = vectors
-        return buffer[at, :] * lead - level - section[at, :] * tilt
+        return buffer[at, :] * lead() - level() - section[at, :] * tilt()
 
     def low_fb(i):
         spread_columns(gcf, i, norm_grad(dbuf_f, sec_fb, rows_at(i, band), vec_fb))
 
-    loop(bands, low_fb)
+    loop(bands, low_fb, unroll=2)
 
     def back_fb(i):
         value = None
@@ -880,8 +916,8 @@
         dbuf_f[rows_at(i, half), :] = value
 
     loop(2, back_fb)
-    bias_fa, gain_fa = slope_pass(sec_fa, stats_fa, "fa", dbuf_f)
-    put("fa_back", 0, pair32(squash(bias_fa), squash(gain_fa)))
+    bias_fa, gain_fa = slope_pass(sec_fa, stats_fa, dbuf_f)
+    put("fa_back", 0, pair32(bias_fa, gain_fa))
     exchange_start("fa_back")
     poll(1)
     total = exchange_end("sb_back")
@@ -893,7 +929,7 @@
     def low_sb(i):
         spread_columns(gcs, i, norm_grad(dbuf, sec_sb, rows_at(i, band), vec_sb))
 
-    loop(bands, low_sb)
+    loop(bands, low_sb, unroll=2)
 
     def back_sb(i):
         value = None
@@ -907,10 +943,10 @@
 
     loop(2, back_sb)
     poll(2)
-    bias_sa, gain_sa = slope_pass(sec_sa, stats_sa, "sa", dbuf)
-
-    put("sa_back", 0, squash(bias_sa))
-    put("sa_back", 256, squash(gain_sa))
+    bias_sa, gain_sa = slope_pass(sec_sa, stats_sa, dbuf)
+
+    put("sa_back", 0, bias_sa)
+    put("sa_back", 256, gain_sa)
     exchange_start("sa_back")
     poll(3)
 
@@ -925,9 +961,9 @@
         value = dot(gcf[band : band + rows, 128:256], hcf[band * a : band * a + rows, :], TN)
         for b in range(3):
             tap = 3 * a + b
-            block = value[:, 128 * b : 128 * (b + 1)] * block_mask
+            block = value[:, 128 * b : 128 * (b + 1)] * block_mask()
             folded = fold_lanes(block[0:32] + block[32:64] + block[64:96] + block[96:128])
-            folded = jnp.where(lane_group[0:32] == tap % 4, folded, 0.0)
+            folded = jnp.where(lane_groups(32) == tap % 4, folded, 0.0)
             at = slice(608 + 32 * (tap // 4), 640 + 32 * (tap // 4))
             slab[2, at, 128:256] = folded if tap % 4 == 0 else slab[2, at, 128:256] + folded
     poll(5)
@@ -939,7 +975,7 @@
         at = rows_at(i, band)
         hbf[at, :] = norm_grad(dbuf_f, sec_fa, at, vec_fa).astype(BF16)
 
-    loop(bands, low_fa)
+    loop(bands, low_fa, unroll=2)
     value = dot(hbf[...], vx[:, 128:896], TN)
     for k in range(3):
         piece = None
@@ -957,11 +993,11 @@
     def low_sa(i):
         at = rows_at(i, band)
         value = norm_grad(dbuf, sec_sa, at, vec_sa)
-        gcs[at, 0:bs] = roll_frames(value, prev256, -1, True).astype(BF16)
+        gcs[at, 0:bs] = roll_frames(value, prev(256), -1, True).astype(BF16)
         gcs[at, bs : 2 * bs] = value.astype(BF16)
-        gcs[at, 2 * bs :] = roll_frames(value, next256, 1, True).astype(BF16)
-
-    loop(bands, low_sa)
+        gcs[at, 2 * bs :] = roll_frames(value, following(256), 1, True).astype(BF16)
+
+    loop(bands, low_sa, unroll=2)
 
     def narrow_gradient(k):
         ref, lane = pieces["sa%d" % k]["ref"], pieces["sa%d" % k]["lane"]
@@ -977,9 +1013,9 @@
         dbuf[at, :] = dot(gcs[at, :], wsa[:, cs_n:], NN)
 
     loop(2, back_lateral)
-    bias_lat, gain_lat = slope_pass(sec_lat, stats_lat, "lat", dbuf)
-    put("lat_back", 0, squash(bias_lat))
-    put("lat_back", 256, squash(gain_lat))
+    bias_lat, gain_lat = slope_pass(sec_lat, stats_lat, dbuf)
+    put("lat_back", 0, bias_lat)
+    put("lat_back", 256, gain_lat)
     exchange_start("lat_back")
 
     poll(9)
@@ -991,59 +1027,6 @@
 
     bias_lat, gain_lat = take(total, 0, 256), take(total, 256, 256)
     report("lat", bias_lat, gain_lat)
-    vec_lat = back_vectors("lat", stats_lat, bias_lat, gain_lat, slow_count)
-
-    def low_lat(i):
-        at = rows_at(i, band)
-        hbs[at, :] = norm_grad(dbuf, sec_lat, at, vec_lat).astype(BF16)
-
-    loop(bands, low_lat)
-    value = dot(hbs[...], vx[:, 0:640], TN)
-    for k in range(5):
-        at, lane = 256 * (k % 3), 128 * (k // 3)
-        slab[2, at : at + 256, lane : lane + 128] = value[:, 128 * k : 128 * (k + 1)]
-    advance("lt")
-    poll(13)
-    narrow_gradient(4)
-    poll(14)
-
-    def slow_back(i):
-        at = rows_at(i, half)
-        for tile in range(cs_n // 256):
-            lanes = slice(256 * tile, 256 * (tile + 1))
-            value = gsum[at, lanes].astype(F32) + dot(gcs[at, :], wsa[:, lanes], NN)
-            gsum[at, lanes] = value.astype(BF16)
-
-    for part in range(2):
-        slow_back(part)
-        poll(15 + part)
-    sgrad_store = store(gsum, sgrad_h, 12)
-
-    fast_store.wait()
-
-    def fast_back(i):
-        at, fat = rows_at(i, 2 * band), rows_at(i, 2 * fband)
-        conv = dot(hbf[at, :], wfa[...], NN)
-        side_in = dot(hbs[at, :], wlat[...], NN)
-
-        def lane(values, block):
-            return values[:, 128 * block : 128 * (block + 1)]
-
-        grads = [gsf[at, 128 * phase : 128 * (phase + 1)] + lane(conv, phase + 1) for phase in range(4)]
-        grads[0] = grads[0] + roll_frames(lane(conv, 5), next128, 1, True) + lane(side_in, 2)
-        grads[1] = grads[1] + lane(side_in, 3)
-        grads[2] = grads[2] + lane(side_in, 4) + roll_frames(lane(side_in, 0), prev128, -1, True)
-        grads[3] = grads[3] + roll_frames(lane(side_in, 1) + lane(conv, 0), prev128, -1, True)
-        for part in range(2):
-            for phase in range(4):
-                stage_a[pl.ds(phase, band, stride=4), :] = grads[phase][part * band : (part + 1) * band]
-            xf[rows_at(2 * i + part, fband), :] = stage_a[...].astype(BF16)
-
-    loop(bands // 4, fast_back)
-    poll(17)
-    loop(bands // 2 - bands // 4, lambda i: fast_back(i + bands // 4))
-    fgrad_store = store(xf, fgrad_h, 13)
-    poll(18)
 
     def pack(rows_ref, target):
         lanes = lax.broadcasted_iota(jnp.int32, (24, LANES), 1)
@@ -1055,28 +1038,98 @@
         target[...] = moved * factor
         target[0:1, :] = first * factor
 
-    pack(gain_rows, dgains)
-    pack(bias_rows, dbiases)
+    pack(gain_rows, stage_b.at[pl.ds(0, 16)])
+    pack(bias_rows, stage_b.at[pl.ds(16, 16)])
+    parameter_stores = [
+        store(stage_b.at[pl.ds(0, 16)], dgains_h, 19), store(stage_b.at[pl.ds(16, 16)], dbiases_h, 20)
+    ]
+    vec_lat = back_vectors("lat", stats_lat, bias_lat, gain_lat, slow_count)
+
+    def low_lat(i):
+        at = rows_at(i, band)
+        hbs[at, :] = norm_grad(dbuf, sec_lat, at, vec_lat).astype(BF16)
+
+    loop(bands, low_lat, unroll=2)
+    value = dot(hbs[...], vx[:, 0:640], TN)
+    for k in range(5):
+        at, lane = 256 * (k % 3), 128 * (k // 3)
+        slab[2, at : at + 256, lane : lane + 128] = value[:, 128 * k : 128 * (k + 1)]
+    advance("lt")
+    poll(13)
+    narrow_gradient(4)
+    poll(14)
+
+    def slow_back(i):
+        at = rows_at(i, half)
+        for tile in range(cs_n // 256):
+            lanes = slice(256 * tile, 256 * (tile + 1))
+            value = gsum[at, lanes].astype(F32) + dot(gcs[at, :], wsa[:, lanes], NN)
+            gsum[at, lanes] = value.astype(BF16)
+
+    for part in range(2):
+        slow_back(part)
+        poll(15 + part)
+    sgrad_store = store(gsum, sgrad_h, 12)
+
+    fast_store.wait()
+
+    def fast_back(i):
+        at, fat = rows_at(i, 2 * band), rows_at(i, 2 * fband)
+        conv = dot(hbf[at, :], wfa[...], NN)
+        side_in = dot(hbs[at, :], wlat[...], NN)
+
+        def lane(values, block):
+            return values[:, 128 * block : 128 * (block + 1)]
+
+        grads = [gsf[at, 128 * phase : 128 * (phase + 1)] + lane(conv, phase + 1) for phase in range(4)]
+        grads[0] = grads[0] + roll_frames(lane(conv, 5), following(128), 1, True) + lane(side_in, 2)
+        grads[1] = grads[1] + lane(side_in, 3)
+        grads[2] = grads[2] + lane(side_in, 4) + roll_frames(lane(side_in, 0), prev(128), -1, True)
+        grads[3] = grads[3] + roll_frames(lane(side_in, 1) + lane(conv, 0), prev(128), -1, True)
+        for part in range(2):
+            for phase in range(4):
+                stage_a[pl.ds(phase, band, stride=4), :] = grads[phase][part * band : (part + 1) * band]
+            xf[rows_at(2 * i + part, fband), :] = stage_a[...].astype(BF16)
+
+    loop(bands // 4, fast_back)
+    poll(17)
+    loop(bands // 2 - bands // 4, lambda i: fast_back(i + bands // 4))
+    fgrad_store = store(xf, fgrad_h, 13)
+    poll(18)
+
     poll(19)
     while not all(done(name) for name in order):
         for name in order:
             if not done(name):
                 advance(name)
-    for slot, copy in enumerate(stores):
+    for copy in stores + parameter_stores:
         copy.wait()
     sgrad_store.wait()
     fgrad_store.wait()
 
 
 def hand_on(*refs):
-    sources, targets, held, sem = refs[0:13], refs[13:26], refs[26:34], refs[34]
-    loads = [pltpu.make_async_copy(sources[k], held[k], sem.at[k]) for k in range(8)]
-    stores = [pltpu.make_async_copy(held[k], targets[k], sem.at[8 + k]) for k in range(8)]
-    for copy in loads:
+    sources, targets, held, small, sem = refs[0:11], refs[11:24], refs[24:35], refs[35:40], refs[40]
+    loads = [pltpu.make_async_copy(sources[k], held[k], sem.at[k]) for k in range(11)]
+    stores = [pltpu.make_async_copy(held[k], targets[k], sem.at[11 + k]) for k in range(8)]
+    stores += [pltpu.make_async_copy(small[k], targets[8 + k], sem.at[19 + k]) for k in range(5)]
+    for k in (8, 9, 10, 0, 1, 2, 3, 4, 5, 6, 7):
+        loads[k].start()
+    for k in (8, 9, 10):
+        loads[k].wait()
+    small[0][...] = held[8][0:96, :]
+    for tap in range(9):
+        at = 96 + 32 * (tap // 4)
+        small[1][32 * tap : 32 * (tap + 1), :] = held[8][at : at + 32, 32 * (tap % 4) : 32 * (tap % 4 + 1)]
+    small[2][...] = held[8][192:224, :]
+    for source, target in ((held[9], small[3]), (held[10], small[4])):
+        count = target.shape[0]
+        for row in range(16):
+            width = min(LANES, count - row * LANES)
+            target[pl.ds(row * LANES, width)] = source[row : row + 1, 0:width].reshape(width)
+    for copy in stores[8:13]:
         copy.start()
-    for k in range(8, 13):
-        targets[k][...] = sources[k][...]
-    for load, copy in zip(loads, stores):
+    for load, copy in zip(loads[0:8], stores[0:8]):
         load.wait()
         copy.start()
     for copy in stores:
@@ -1120,15 +1173,13 @@
         slow_narrow.shape[1], slow_spatial.shape[1], slow_widen.shape[0],
     ]
 
-    def lay_out(vector):
-        return jnp.pad(vector, (0, 16 * LANES - vector.shape[0])).reshape(16, LANES)
-
     cf = fast_channels
     bs = slow_spatial.shape[1]
     band = side * frames
     any_spec = pl.BlockSpec(memory_space=pl.ANY)
     vmem_spec = pl.BlockSpec(memory_space=pltpu.VMEM)
     near_low = n_dp if n_dp * n_rep <= 32 else low
+    stages = 1 if near_low == n_dp else 2
     pad = rows + 2 * band
 
     def shape(dims, dtype):
@@ -1138,8 +1189,7 @@
         shape((rows, channels), BF16), shape((4 * rows, cf), BF16),
         shape((rows, channels), BF16), shape((4 * rows, cf), BF16),
         shape((3 * bs, channels + bs), F32), shape((9 * bs, bs), F32), shape((channels, bs), F32),
-        shape((5 * bs, cf), F32), shape((96, cf), F32), shape((288, 32), F32), shape((32, cf), F32),
-        shape((16, LANES), F32), shape((16, LANES), F32),
+        shape((5 * bs, cf), F32), shape((256, cf), F32), shape((16, LANES), F32), shape((16, LANES), F32),
         shape((10, max(high // 4, 1), 32, 256), F32),
     ]
     scratch = [
@@ -1156,7 +1206,8 @@
         pltpu.VMEM((rows, 896), BF16), pltpu.VMEM((3, 1512, 256), F32), pltpu.VMEM((2016, 256), F32),
         pltpu.VMEM((768, 256), F32), pltpu.VMEM((max(high // 4, 1), 32, 256), F32),
         pltpu.VMEM((3 * bs, channels + bs), BF16), pltpu.VMEM((9 * bs, bs), BF16),
-        pltpu.VMEM((channels, bs), BF16),
+        pltpu.VMEM((channels, bs), BF16), pltpu.VMEM(norm_gains.shape, F32), pltpu.VMEM(norm_gains.shape, F32),
+        pltpu.VMEM((72, 8, channels), F32), pltpu.VMEM((2, 8, 256), F32),
         pltpu.VMEM((96, cf), BF16), pltpu.VMEM((288, 32), BF16), pltpu.VMEM((32, cf), BF16),
         pltpu.VMEM((bs, 640), BF16), pltpu.VMEM((128, 768), BF16),
         pltpu.VMEM((3, 128, 384), BF16), pltpu.VMEM((3, 384, 128), BF16), pltpu.VMEM((512, 128), BF16),
@@ -1164,16 +1215,16 @@
         pltpu.VMEM((24, LANES), F32), pltpu.VMEM((24, LANES), F32),
         pltpu.VMEM((near_low * n_rep, 1, sum(TURNS.values())), F32),
         pltpu.VMEM((max(n_dp // near_low, 1), 1, sum(TURNS.values())), F32),
-        pltpu.SemaphoreType.DMA((len(TURNS), 2)), pltpu.SemaphoreType.DMA((len(TURNS), 2)),
+        pltpu.SemaphoreType.DMA((stages, len(TURNS))), pltpu.SemaphoreType.DMA((stages, len(TURNS))),
         pltpu.SemaphoreType.DMA((32,)), pltpu.SemaphoreType.DMA((10, 2)),
-        pltpu.SemaphoreType.DMA((10, 11)), pltpu.SemaphoreType.DMA((10, 11)),
+        pltpu.SemaphoreType.DMA((10,)), pltpu.SemaphoreType.DMA((10, 10 if high == 4 else 11)),
     ]
     factor = 1.0 / math.sqrt(float(slow_count))
     results = pl.pallas_call(
         functools.partial(kernel, (n_dp, n_rep, low, frames, side, float(slow_count), float(fast_count), factor)),
         out_shape=out_shape,
-        in_specs=[any_spec] * 4 + [pl.BlockSpec(memory_space=pltpu.SMEM)] + [any_spec] * 7 + [vmem_spec] * 2,
-        out_specs=[any_spec] * 8 + [vmem_spec] * 5 + [any_spec],
+        in_specs=[any_spec] * 4 + [pl.BlockSpec(memory_space=pltpu.SMEM)] + [any_spec] * 9,
+        out_specs=[any_spec] * 12,
         scratch_shapes=scratch,
         compiler_params=pltpu.CompilerParams(
             collective_id=0, has_side_effects=True, vmem_limit_bytes=65000 * 2**10
@@ -1182,22 +1233,22 @@
         flat(slow_input), flat(fast_input), flat(slow_cotangent), flat(fast_cotangent), clip_ids,
         fast_narrow.reshape(-1, cf), fast_spatial.reshape(-1, 32), fast_widen.T,
         lateral_conv.reshape(-1, cf), slow_narrow.reshape(3 * bs, -1), slow_spatial.reshape(9 * bs, bs),
-        slow_widen, lay_out(norm_gains), lay_out(norm_biases),
+        slow_widen, norm_gains, norm_biases,
     )
-    results = list(results[0:13])
+    final = out_shape[0:8] + [
+        shape((96, cf), F32), shape((288, 32), F32), shape((32, cf), F32),
+        shape(norm_gains.shape, F32), shape(norm_gains.shape, F32),
+    ]
     handed = pl.pallas_call(
         hand_on,
-        out_shape=out_shape[0:13],
-        in_specs=[any_spec] * 8 + [vmem_spec] * 5,
-        out_specs=[any_spec] * 8 + [vmem_spec] * 5,
-        scratch_shapes=[pltpu.VMEM(item.shape, item.dtype) for item in out_shape[0:8]]
-        + [pltpu.SemaphoreType.DMA((16,))],
+        out_shape=final,
+        in_specs=[any_spec] * 11,
+        out_specs=[any_spec] * 13,
+        scratch_shapes=[pltpu.VMEM(item.shape, item.dtype) for item in out_shape[0:11] + final[8:13]]
+        + [pltpu.SemaphoreType.DMA((24,))],
         compiler_params=pltpu.CompilerParams(vmem_limit_bytes=64000 * 2**10),
-    )(*results)
+    )(*results[0:11])
     slow_out, fast_out, slow_grad, fast_grad, dsa, dsb, dsc, dl, dfa, dfb, dfc, dgains, dbiases = handed
-
-    def gather(packed):
-        return packed.reshape(16 * LANES)[0 : sum(widths)]
 
     return (
         unflat(slow_out, frames),
@@ -1211,8 +1262,8 @@
         dsa.reshape(slow_narrow.shape),
         dsb.reshape(slow_spatial.shape),
         dsc,
-        gather(dgains),
-        gather(dbiases),
+        dgains,
+        dbiases,
     )
 
 

time: 152 us -> 141 us (0.928)
  Pallas kernels: 150 us -> 140 us
    pallas_call x1, Pallas kernels: 136 us -> 128 us  [body(): pl.pallas_call(functools.partial(kernel, (n_dp, n_rep, low, frames, side,...]
where the time goes in v4:
time: 141 us
  Pallas kernels  140 us (99%)
    pallas_call x1, Pallas kernels, body(): pl.pallas_call(functools.partial(kernel, (n_dp, n_rep, low, frames, side,...  128 us
    pallas_call x1, Pallas kernels, body(): pl.pallas_call(hand_on, out_shape=final, in_specs=[any_spec] * 11, out_sp...  12.1 us

profile of v4, /device:TPU:0, one launch (start us, length us, event | category | flops | bytes accessed | tf_op | source)
XLA Modules:
  0.0 140.9 jit_solution(17135260542846336137)
XLA Ops:
  0.7 128.0 %shard_map.237 = (bf16[1568,1024]{1,0:T(8,128)(2,1)}, bf16[6272,128]{1,0:T(8,128)(2,1)}, bf16[1568,1024]{1,0:T(8,128)(2,1)}, bf16[6272,128]{1,0:T(8,128)(2,1)}, ...) custom-call(bf16[1568,1024]{1,0:T(8,128)(2,1)} %bitcast.36, ...), custom_call_target="tpu_custom_call" | custom-call | tf_op jit(solution)/shard_map/pallas_call | solution.py:1223
  128.7 12.1 %shard_map.238 = (bf16[1568,1024]{1,0:T(8,128)(2,1)}, bf16[6272,128]{1,0:T(8,128)(2,1)}, bf16[1568,1024]{1,0:T(8,128)(2,1)}, bf16[6272,128]{1,0:T(8,128)(2,1)}, ...) custom-call(bf16[1568,1024]{1,0:T(8,128)(2,1)} %get-tuple-element.37, ...), custom_call_target="tpu_custom_call" | custom-call | tf_op jit(solution)/shard_map/pallas_call | solution.py:1242

commit v5 on v4

--- a/solution.py
+++ b/solution.py
@@ -16,58 +16,56 @@
 NT = ((1,), (1,))
 TN = ((0,), (0,))
 LANES = 128
-TURNS = {
-    "lat": 512, "fa": 128, "sa": 512, "fb": 128, "sb": 512, "fc": 256, "sc0": 768, "sc1": 512,
-    "sc0_back": 1024, "sc1_back": 1024, "fc_back": 256, "sb_back": 512, "fb_back": 128, "sa_back": 512,
-    "fa_back": 128, "lat_back": 512,
-}
-
-
-ORDERS = {
-    "plane": (("c", "x", "y", "z"), ("c", "y", "x", "z")),
-    "halves": (("c", "x", "y", "z0", "z1"), ("c", "y", "x", "z0", "z1")),
-    "between": (("c", "x", "z0", "z1", "y"), ("c", "y", "z0", "z1", "x")),
-    "line": (("c", "z0", "z1", "x", "y"), ("c", "z0", "z1", "y", "x")),
-}
-ORDER_OF = {
-    "sc": "halves",
-    "sb0": "halves",
-    "sb1": "line",
-    "sb2": "plane",
-    "sa0": "halves",
-    "sa1": "between",
-    "sa2": "plane",
-    "sa3": "plane",
-    "sa4": "halves",
-    "lt": "halves",
-}
+FA, FB, FC, LAT, SLOW_A, SLOW_B, SLOW_C = range(7)
+FORWARD = {LAT: 512, FA: 128, SLOW_A: 512, FB: 128, SLOW_B: 512, FC: 256, SLOW_C: 768, SLOW_C + 1: 512}
+BACKWARD = {SLOW_C: 1024, SLOW_C + 1: 1024, FC: 256, SLOW_B: 512, FB: 128, SLOW_A: 512, FA: 128, LAT: 512}
+BACK = 8
+TURNS = {**FORWARD, **{BACK + norm: lanes for norm, lanes in BACKWARD.items()}}
+
+
+class Piece:
+    pass
+
+
+SC, SB, SA, LT = 0, 1, 4, 9
+C, X, Y, Z, Z0, Z1 = range(6)
+PLANE = ((C, X, Y, Z), (C, Y, X, Z))
+HALVES = ((C, X, Y, Z0, Z1), (C, Y, X, Z0, Z1))
+BETWEEN = ((C, X, Z0, Z1, Y), (C, Y, Z0, Z1, X))
+LINE = ((C, Z0, Z1, X, Y), (C, Z0, Z1, Y, X))
+ORDER_OF = (PLANE, HALVES, HALVES, PLANE, LINE, HALVES, HALVES, BETWEEN, PLANE, PLANE)
 POLLS = (
     (),
-    ("sc",),
+    (0,),
     (),
     (),
-    ("sc", "sb0"),
-    ("sb1",),
-    ("sb2",),
     (),
-    ("sc",),
-    ("sb0", "sa0"),
-    ("sb2", "sb1"),
-    ("sc",),
-    ("sb0", "sa1"),
-    ("sa0", "sb2", "sa2", "sa3"),
-    ("sb0", "sb1", "lt"),
-    ("sa0", "sc", "sa1", "sa4"),
-    ("sb2", "sa2"),
-    ("sb0",),
-    ("sa0", "sc", "sa3", "sb1"),
+    (),
+    (),
+    (0,),
+    (),
+    (1,),
+    (2,),
+    (0, 3),
+    (),
+    (),
+    (),
+    (1,),
+    (),
+    (2, 4),
+    (3, 0, 1, 5),
+    (2, 6),
+    (3, 7),
+    (5, 4, 9),
+    (),
+    (6, 2, 0, 1, 8),
+    (7,),
+    (5,),
+    (3,),
     (
-        "lt", "sa1", "sa4", "sb0", "sa2", "sb2", "sa0", "lt", "sc", "sa4", "sa3", "sa1",
-        "sb0", "sb2", "sa2", "lt", "sa0", "sc", "sa4", "sb1", "sb0", "sa3", "sb2", "sa1",
-        "sa0", "sa2", "lt", "sc", "sb1", "sa4", "sb2", "sa1", "sb0", "sa3", "lt", "sa0",
-        "sa2", "sa4", "sc", "sb1", "sa3", "sa1", "lt", "sb0", "sa0", "sa2", "sa4", "sb1",
-        "sa1", "sa3", "sa2", "lt", "sa0", "sa4", "sa3", "sa1", "sb1", "lt", "sa4", "sb1",
-        "sa1", "lt", "sa4",
+        9, 4, 2, 7, 0, 8, 5, 6, 4, 1, 2, 9, 7, 3, 6, 5, 0, 1, 4, 2, 7, 3, 9, 5,
+        4, 6, 0, 1, 7, 8, 2, 9, 6, 3, 5, 4, 1, 9, 7, 8, 6, 3, 2, 5, 2, 4, 9, 1,
+        7, 8, 1, 6, 5, 8, 4, 5, 9, 4, 7, 6, 7, 8, 6, 8,
     ),
 )
 
@@ -108,13 +106,14 @@
 def kernel(
     dims,
     xs_h, xf_h, cs_h, cf_h, clip, wfa_h, wfb_h, wfc_h, wl_h, wsa_h, wsb_h, wsc_h, gains_h, biases_h,
-    slow_h, fast_h, sgrad_h, fgrad_h, dsa_h, dsb_h, dsc_h, dl_h, small_h, dgains_h, dbiases_h, extra_h,
-    xs, cs, gsum, xf, cf, big, sec_fc, gsf, hcs, gcs, hcf, gcf,
-    sec_lat, sec_sa, sec_sb, dbuf, sec_fa, sec_fb, dbuf_f, jl, hbs, hbf, vx, slab, slab_sc, summed, gathered,
+    slow_h, fast_h, gsum, xf, dsa, dsb, dsc_h, dl_h, small_h, dgains_h, dbiases_h, extra_h,
+    xs, cs, cf, big, sec_fc, gsf, hcs, gcs, hcf, gcf,
+    sec_lat, dbuf, sec_fa, sec_fb, dbuf_f, jl, hbs, hbf, vx, slab, slab_sc, summed,
     wsa, wsb, wsc, gains_in, biases_in, vectors, masks, wfa_in, wfb_in, wfc_in, wlat, wfa, wfb, wfbk, wfc,
-    stage_a, stage_b, gain_rows, bias_rows, near, far, sum_send, sum_recv, io_sem, own_sem, big_send, big_recv,
+    stage_a, gain_rows, bias_rows, near, far, sum_send, sum_recv, io_sem, own_sem, big_send, big_recv,
 ):
     n_dp, n_rep, low, frames, side, slow_count, fast_count, factor = dims
+    sec_sa, sec_sb = dsa, dsb
     rows = xs.shape[0]
     half = rows // 2
     band = side * frames
@@ -234,78 +233,79 @@
 
     pieces = {}
 
-    bits = {"c": (c, core_peer), "x": (x, x_peer), "y": (y, y_peer),
-            "z0": (lax.rem(z, 2), z_peer(1)), "z1": (lax.div(z, 2), z_peer(2))}
+    bits = {C: (c, core_peer), X: (x, x_peer), Y: (y, y_peer),
+            Z0: (lax.rem(z, 2), z_peer(1)), Z1: (lax.div(z, 2), z_peer(2))}
 
     def add_piece(name, ref, lane, size, index):
-        axes = ORDERS[ORDER_OF[name]]
-        piece = {"name": name, "ref": ref, "lane": lane, "size": size, "index": index, "step": 0, "axes": axes}
+        axes = ORDER_OF[name]
+        piece = Piece()
+        piece.name, piece.ref, piece.lane, piece.size, piece.index = name, ref, lane, size, index
+        piece.step, piece.axes, piece.steps = 0, axes, len(axes[0])
         starts, counts, arriving = [[0], [0]], [size], [size]
         for step, pair in enumerate(zip(*axes)):
             for side, axis in enumerate(pair):
-                if axis == "z":
+                if axis == Z:
                     starts[side].append(starts[side][-1] + z * (counts[-1] // 4))
                 else:
                     starts[side].append(starts[side][-1] + bits[axis][0] * (counts[-1] // 2))
-            counts.append(counts[-1] // (4 if pair[0] == "z" else 2))
-            arriving.append(arriving[-1] + (3 if pair[0] == "z" else 1) * counts[-1])
-        piece.update(starts=starts, counts=counts, arriving=arriving, steps=len(axes[0]))
+            counts.append(counts[-1] // (4 if pair[0] == Z else 2))
+            arriving.append(arriving[-1] + (3 if pair[0] == Z else 1) * counts[-1])
+        piece.starts, piece.counts, piece.arriving = starts, counts, arriving
         pieces[name] = piece
 
     for k in range(2):
-        add_piece("sb%d" % k, sec_fc, 256 * k, 768, k)
+        add_piece(SB + k, sec_fc, 256 * k, 768, k)
     for k in range(4):
-        add_piece("sa%d" % k, big, 256 * k, 768, 2 + k)
-    add_piece("sb2", slab.at[0], 0, 768, 6)
-    add_piece("sa4", slab.at[1], 0, 768, 7)
-    add_piece("lt", slab.at[2], 0, 768, 8)
-    add_piece("sc", slab_sc, 0, 1024, 9)
+        add_piece(SA + k, big, 256 * k, 768, 2 + k)
+    add_piece(SB + 2, slab.at[0], 0, 768, 6)
+    add_piece(SA + 4, slab.at[1], 0, 768, 7)
+    add_piece(LT, slab.at[2], 0, 768, 8)
+    add_piece(SC, slab_sc, 0, 1024, 9)
 
     def span(piece, start, count, lane=0, width=256):
-        return piece["ref"].at[pl.ds(pl.multiple_of(start, 8), count), pl.ds(piece["lane"] + lane, width)]
+        return piece.ref.at[pl.ds(pl.multiple_of(start, 8), count), pl.ds(piece.lane + lane, width)]
 
     def send(piece, step, src, dst, peer):
         pltpu.make_async_remote_copy(
-            src_ref=src, dst_ref=dst, send_sem=big_send.at[piece["index"]],
-            recv_sem=big_recv.at[piece["index"], step], device_id=peer, device_id_type=MESH,
+            src_ref=src, dst_ref=dst, send_sem=big_send.at[piece.index],
+            recv_sem=big_recv.at[piece.index, step], device_id=peer, device_id_type=MESH,
         ).start()
 
     def result(piece, start, count, lane=0, width=256):
-        name = piece["name"]
+        name = piece.name
         start = pl.multiple_of(start, 8)
-        if name == "lt":
+        if name == LT:
             return summed.at[pl.ds(start, count), pl.ds(lane, width)]
-        if name == "sc":
+        if name == SC:
             return dsc_h.at[pl.ds(start, count), pl.ds(lane, width)]
-        k = int(name[2])
-        if name[1] == "a":
-            return dsa_h.at[pl.ds(start, count), pl.ds(256 * k + lane, width)]
-        return dsb_h.at[pl.ds(768 * k + start, count), pl.ds(lane, width)]
+        if name >= SA:
+            return dsa.at[pl.ds(768 * (name - SA) + start, count), pl.ds(lane, width)]
+        return dsb.at[pl.ds(768 * (name - SB) + start, count), pl.ds(lane, width)]
 
     def own_copies(piece):
-        count, sem = piece["counts"][-1], own_sem.at[piece["index"]]
+        count, sem = piece.counts[-1], own_sem.at[piece.index]
         return [
             pltpu.make_async_copy(
                 span(piece, start[-1], count, 128 * side, 128),
                 result(piece, start[-1], count, 128 * side, 128),
                 sem.at[side],
             )
-            for side, start in enumerate(piece["starts"])
+            for side, start in enumerate(piece.starts)
         ]
 
     def arrived(piece, step, rows_in):
-        block = span(piece, 0, rows_in) if step < piece["steps"] else result(piece, 0, rows_in)
+        block = span(piece, 0, rows_in) if step < piece.steps else result(piece, 0, rows_in)
         copy = pltpu.make_async_remote_copy(
-            src_ref=block, dst_ref=block, send_sem=big_send.at[piece["index"]],
-            recv_sem=big_recv.at[piece["index"], step], device_id=core_peer, device_id_type=MESH,
+            src_ref=block, dst_ref=block, send_sem=big_send.at[piece.index],
+            recv_sem=big_recv.at[piece.index, step], device_id=core_peer, device_id_type=MESH,
         )
         copy.wait_recv()
         copy.wait_send()
 
     def add_rows(piece, target, source, count, lane, width):
-        lanes = pl.ds(piece["lane"] + lane, width)
-        chunk = piece["size"] // 32
-        ref = piece["ref"]
+        lanes = pl.ds(piece.lane + lane, width)
+        chunk = piece.size // 32
+        ref = piece.ref
 
         def step(i):
             into = pl.ds(pl.multiple_of(target + i * chunk, 8), chunk)
@@ -313,32 +313,35 @@
 
         loop(count // chunk, step)
 
-    order = ["sc", "sb0", "sb1", "sb2", "sa0", "sa1", "sa2", "sa3", "sa4", "lt"]
+    order = range(10)
 
     def unpack_small():
         stores.append(store(summed.at[:, pl.ds(0, 128)], dl_h.at[pl.ds(0, 768)], 16))
         stores.append(store(summed.at[pl.ds(0, 512), pl.ds(128, 128)], dl_h.at[pl.ds(768, 512)], 17))
         stores.append(store(summed.at[pl.ds(512, 256), pl.ds(128, 128)], small_h, 18))
 
-    def poll(turn):
-        for name in POLLS[turn]:
+    polled = [0]
+
+    def poll():
+        polled[0] += 1
+        for name in POLLS[polled[0] - 1]:
             advance(name)
 
     def done(name):
-        return pieces[name]["step"] > 2 * pieces[name]["steps"]
+        return pieces[name].step > 2 * pieces[name].steps
 
     def advance(name):
         piece = pieces[name]
-        step, steps, index = piece["step"], piece["steps"], piece["index"]
-        piece["step"] = step + 1
-        starts, counts, arriving, axes = piece["starts"], piece["counts"], piece["arriving"], piece["axes"]
-        ref, lane = piece["ref"], piece["lane"]
+        step, steps, index = piece.step, piece.steps, piece.index
+        piece.step = step + 1
+        starts, counts, arriving, axes = piece.starts, piece.counts, piece.arriving, piece.axes
+        ref, lane = piece.ref, piece.lane
 
         def received(last):
-            fan = 3 if axes[0][last] == "z" else 1
+            fan = 3 if axes[0][last] == Z else 1
             return fan * counts[last + 1]
 
-        if 0 < step < steps or (step == steps and axes[0][-1] != "z"):
+        if 0 < step < steps or (step == steps and axes[0][-1] != Z):
             arrived(piece, step - 1, received(step - 1))
             if step == 1:
                 add_rows(piece, starts[0][1], arriving[0], counts[1], 0, 256)
@@ -358,7 +361,7 @@
                 return
             for side in range(2):
                 axis, start = axes[side][step], starts[side][step]
-                if axis == "z":
+                if axis == Z:
                     for k, peer in enumerate(z_peers):
                         at, into = start + lax.rem(z + k + 1, 4) * keep, arriving[step] + k * keep
                         send(
@@ -379,7 +382,7 @@
                 for side in range(2)
             ]
             both = jnp.concatenate([ref[own[0]], ref[own[1]]], axis=1)
-            if axes[0][-1] == "z":
+            if axes[0][-1] == Z:
                 for k in range(3):
                     both = both + ref[pl.ds(arriving[steps - 1] + k * last, last), pl.ds(lane, 256)]
             if outers > 1:
@@ -394,14 +397,16 @@
                 )
                 copy.wait_recv()
                 copy.wait_send()
-                for src, dst in (
-                    (held, extra_h.at[index, outer, pl.ds(0, last)]),
-                    (extra_h.at[index], gathered),
-                ):
+                local = [(held, extra_h.at[index, outer, pl.ds(0, last)])]
+                for k in range(outers):
+                    local.append((extra_h.at[index, k, pl.ds(0, last)], span(piece, arriving[0] + k * last, last)))
+                for src, dst in local:
                     copy = pltpu.make_async_copy(src, dst, own_sem.at[index, 0])
                     copy.start()
                     copy.wait()
-                both = jnp.sum(gathered[:, pl.ds(0, last), :], axis=0)
+                both = ref[pl.ds(arriving[0], last), pl.ds(lane, 256)]
+                for k in range(1, outers):
+                    both = both + ref[pl.ds(arriving[0] + k * last, last), pl.ds(lane, 256)]
             both = both * factor
             for side in range(2):
                 ref[own[side]] = both[:, 128 * side : 128 * (side + 1)]
@@ -419,15 +424,15 @@
                 axis, start = axes[side][back], starts[side][back + 1]
                 block = result(piece, start, count, 128 * side, 128)
                 source = span(piece, start, count, 128 * side, 128) if step == steps else block
-                for peer in z_peers if axis == "z" else [bits[axis][1]]:
+                for peer in z_peers if axis == Z else [bits[axis][1]]:
                     send(piece, step, source, block, peer)
             if step == steps:
                 for copy in own_copies(piece):
                     copy.start()
-        elif step == 2 * steps and name == "lt":
+        elif step == 2 * steps and name == LT:
             unpack_small()
 
-    spots = {"fc": 0, "lat": 1, "sa": 3, "sb": 5, "sc": 7, "fa": 16, "fb": 17}
+    spots = {FC: 0, LAT: 1, SLOW_A: 3, SLOW_B: 5, SLOW_C: 7, FA: 16, FB: 17}
 
     lane16 = lax.broadcasted_iota(jnp.int32, (16, LANES), 1)
 
@@ -436,9 +441,9 @@
         fb = fold_lanes(jnp.where(lane16 // 32 == 1, packed, 0.0))[0:1, :]
         turned = pltpu.roll(packed, 64, 1)
         moved = jnp.where(lane16 < 64, turned, pltpu.roll(turned, 15, 0))
-        found = {"fa": fa, "fb": fb}
+        found = {FA: fa, FB: fb}
         at = 0
-        for name, count in (("fc", 1), ("lat", 2), ("sa", 2), ("sb", 2), ("sc", 8)):
+        for name, count in ((FC, 1), (LAT, 2), (SLOW_A, 2), (SLOW_B, 2), (SLOW_C, 8)):
             found[name] = jnp.concatenate([moved[at + k : at + k + 1, :] for k in range(count)], axis=1)
             at += count
         return found
@@ -448,10 +453,11 @@
     def settle(vector):
         at, width = held[0], vector.shape[1]
         held[0] += 1
-        vectors[at, 0:1, 0:width] = vector
+        line, row = at // 8, slice(at % 8, at % 8 + 1)
+        vectors[line, row, 0:width] = vector
 
         def read(lanes=slice(0, width)):
-            return vectors[at, 0:1, lanes]
+            return vectors[line, row, lanes]
 
         return read
 
@@ -595,14 +601,14 @@
         return carry[0] + column_sums(value), carry[1] + column_sums(value * value)
 
     sum_lat, sq_lat = loop(2, conv_lat, zero2(256))
-    put("lat", 0, squash(sum_lat))
-    put("lat", 256, squash(sq_lat))
+    put(LAT, 0, squash(sum_lat))
+    put(LAT, 256, squash(sq_lat))
     pl.semaphore_wait(barrier, len(greeted))
-    exchange_start("lat")
+    exchange_start(LAT)
 
     sum_fa, sq_fa = loop(2, conv_fa, zero2(128))
-    put("fa", 0, pair32(squash(sum_fa), squash(sq_fa)))
-    exchange_start("fa")
+    put(FA, 0, pair32(squash(sum_fa), squash(sq_fa)))
+    exchange_start(FA)
 
     loads["xs"].wait()
     loads["wsa"].wait()
@@ -626,9 +632,9 @@
     for phase in range(4):
         wfc[LANES * phase : LANES * (phase + 1), :] = jnp.where(lane_groups() == phase, widen, 0.0).astype(BF16)
     read_parameters()
-    total = exchange_end("lat")
-
-    stats_lat = moments("lat", take(total, 0, 256), take(total, 256, 256), slow_count)
+    total = exchange_end(LAT)
+
+    stats_lat = moments(LAT, take(total, 0, 256), take(total, 256, 256), slow_count)
 
     def act_fa(i):
         spread_columns(hcf, i, silu_of(sec_fa[rows_at(i, band), :], stats_fa))
@@ -666,19 +672,19 @@
         return carry[0] + column_sums(value), carry[1] + column_sums(value * value)
 
     sum_sa, sq_sa = loop(bands, combine_sa, zero2(256))
-    put("sa", 0, squash(sum_sa))
-    put("sa", 256, squash(sq_sa))
-    exchange_start("sa")
-
-    total = exchange_end("fa")
-    stats_fa = moments("fa", *unpair32(total), fast_count)
+    put(SLOW_A, 0, squash(sum_sa))
+    put(SLOW_A, 256, squash(sq_sa))
+    exchange_start(SLOW_A)
+
+    total = exchange_end(FA)
+    stats_fa = moments(FA, *unpair32(total), fast_count)
     loop(bands, act_fa, unroll=2)
     sum_fb, sq_fb = loop(2, conv_fb, zero2(128))
-    put("fb", 0, pair32(squash(sum_fb), squash(sq_fb)))
-    exchange_start("fb")
-    total = exchange_end("sa")
-
-    stats_sa = moments("sa", take(total, 0, 256), take(total, 256, 256), slow_count)
+    put(FB, 0, pair32(squash(sum_fb), squash(sq_fb)))
+    exchange_start(FB)
+    total = exchange_end(SLOW_A)
+
+    stats_sa = moments(SLOW_A, take(total, 0, 256), take(total, 256, 256), slow_count)
 
     def act_sa(i):
         spread_columns(hcs, i, silu_of(sec_sa[rows_at(i, band), :], stats_sa))
@@ -702,12 +708,12 @@
         return carry[0] + column_sums(value), carry[1] + column_sums(value * value)
 
     sum_sb, sq_sb = loop(2, conv_sb, zero2(256))
-    put("sb", 0, squash(sum_sb))
-    put("sb", 256, squash(sq_sb))
-    exchange_start("sb")
-
-    total = exchange_end("fb")
-    stats_fb = moments("fb", *unpair32(total), fast_count)
+    put(SLOW_B, 0, squash(sum_sb))
+    put(SLOW_B, 256, squash(sq_sb))
+    exchange_start(SLOW_B)
+
+    total = exchange_end(FB)
+    stats_fb = moments(FB, *unpair32(total), fast_count)
     loop(bands // 2, act_fb)
 
     def widen_fast(i, carry):
@@ -721,12 +727,12 @@
     def fold4(vector):
         return vector[:, 0:128] + vector[:, 128:256] + vector[:, 256:384] + vector[:, 384:512]
 
-    put("fc", 0, squash(fold4(sum_fc)))
-    put("fc", 128, squash(fold4(sq_fc)))
-    exchange_start("fc")
-    total = exchange_end("sb")
-
-    stats_sb = moments("sb", take(total, 0, 256), take(total, 256, 256), slow_count)
+    put(FC, 0, squash(fold4(sum_fc)))
+    put(FC, 128, squash(fold4(sq_fc)))
+    exchange_start(FC)
+    total = exchange_end(SLOW_B)
+
+    stats_sb = moments(SLOW_B, take(total, 0, 256), take(total, 256, 256), slow_count)
 
     def act_sb(i, carry):
         at = rows_at(i, 2 * band)
@@ -749,27 +755,27 @@
 
         return loop(2, step, jnp.zeros((8, mid), F32))
 
-    put("sc0", 0, squash(sum_hbs))
-    put("sc0", 256, squash(widen_slow(0)))
-    exchange_start("sc0")
-    put("sc1", 0, squash(widen_slow(1)))
-    exchange_start("sc1")
-    total = exchange_end("fc")
-    stats_fc = moments("fc", take(total, 0, 128), take(total, 128, 128), fast_count)
+    put(SLOW_C, 0, squash(sum_hbs))
+    put(SLOW_C, 256, squash(widen_slow(0)))
+    exchange_start(SLOW_C)
+    put(SLOW_C + 1, 0, squash(widen_slow(1)))
+    exchange_start(SLOW_C + 1)
+    total = exchange_end(FC)
+    stats_fc = moments(FC, take(total, 0, 128), take(total, 128, 128), fast_count)
 
     loads["cf"].wait()
 
     def finish_fast(i, carry):
         at, fat = rows_at(i, band), rows_at(i, fband)
         bias_sum, gain_sum = carry
-        stage_b[...] = cf[fat, :].astype(F32)
+        dbuf_f[0:fband, :] = cf[fat, :].astype(F32)
         for phase in range(4):
             lanes = slice(128 * phase, 128 * (phase + 1))
             centred = sec_fc[at, lanes] - stats_fc[0]()
             total_in = vx[at, 256 + 128 * phase : 384 + 128 * phase].astype(F32)
             out, slope = slope_of(0.5 * total_in + (centred * stats_fc[2]() + stats_fc[3]()))
             stage_a[pl.ds(phase, band, stride=4), :] = out
-            grad = stage_b[pl.ds(phase, band, stride=4), :] * slope
+            grad = dbuf_f[pl.ds(phase, band, stride=4), :] * slope
             gsf[at, lanes] = grad
             bias_sum = bias_sum + column_sums(grad)
             gain_sum = gain_sum + column_sums(grad * centred)
@@ -778,11 +784,11 @@
 
     bias_fc, gain_fc = loop(bands, finish_fast, zero2(128))
     fast_store = store(xf, fast_h, 10)
-    put("fc_back", 0, squash(bias_fc))
-    put("fc_back", 128, squash(gain_fc) * stats_fc[1]())
-    exchange_start("fc_back")
+    put(BACK + FC, 0, squash(bias_fc))
+    put(BACK + FC, 128, squash(gain_fc) * stats_fc[1]())
+    exchange_start(BACK + FC)
     loads["cs"].wait()
-    total = exchange_end("sc0")
+    total = exchange_end(SLOW_C)
     squares = take(total, 256, mid)
     whole = settle(
         lax.dot_general(
@@ -790,8 +796,8 @@
             precision=lax.Precision.HIGHEST, preferred_element_type=F32,
         )[0:1, :]
     )
-    squares = jnp.concatenate([squares, exchange_end("sc1")], axis=1)
-    stats_sc = moments("sc", whole(), squares, slow_count)
+    squares = jnp.concatenate([squares, exchange_end(SLOW_C + 1)], axis=1)
+    stats_sc = moments(SLOW_C, whole(), squares, slow_count)
 
     def finish_slow(part):
         lanes = slice(part * mid, (part + 1) * mid)
@@ -811,14 +817,14 @@
 
     for part in range(2):
         bias_part, gain_part = finish_slow(part)
-        put("sc%d_back" % part, 0, bias_part)
-        put("sc%d_back" % part, mid, gain_part)
-        exchange_start("sc%d_back" % part)
+        put(BACK + SLOW_C + part, 0, bias_part)
+        put(BACK + SLOW_C + part, mid, gain_part)
+        exchange_start(BACK + SLOW_C + part)
     slow_store = store(cs, slow_h, 11)
 
-    total = exchange_end("fc_back")
+    total = exchange_end(BACK + FC)
     bias_fc, gain_fc = take(total, 0, 128), take(total, 128, 128)
-    report("fc", bias_fc, gain_fc)
+    report(FC, bias_fc, gain_fc)
     def slope_pass(section, stats, buffer):
         def step(i, carry):
             at = rows_at(i, 2 * band)
@@ -830,7 +836,7 @@
         bias_sum, gain_sum = loop(bands // 2, step, zero2(section.shape[1]))
         return squash(bias_sum), squash(gain_sum) * stats[1]()
 
-    lead_fc, level_fc, tilt_fc = back_vectors("fc", stats_fc, bias_fc, gain_fc, fast_count)
+    lead_fc, level_fc, tilt_fc = back_vectors(FC, stats_fc, bias_fc, gain_fc, fast_count)
 
     def low_fc(i):
         at = rows_at(i, band)
@@ -851,15 +857,15 @@
 
     loop(2, back_fc)
     bias_fb, gain_fb = slope_pass(sec_fb, stats_fb, dbuf_f)
-    put("fb_back", 0, pair32(bias_fb, gain_fb))
-    exchange_start("fb_back")
+    put(BACK + FB, 0, pair32(bias_fb, gain_fb))
+    exchange_start(BACK + FB)
     slow_store.wait()
-    sums = [exchange_end("sc%d_back" % part) for part in range(2)]
+    sums = [exchange_end(BACK + SLOW_C + part) for part in range(2)]
 
     bias_sc = jnp.concatenate([take(total, 0, mid) for total in sums], axis=1)
     gain_sc = jnp.concatenate([take(total, mid, mid) for total in sums], axis=1)
-    report("sc", bias_sc, gain_sc)
-    lead_sc = gain("sc") * stats_sc[1]()
+    report(SLOW_C, bias_sc, gain_sc)
+    lead_sc = gain(SLOW_C) * stats_sc[1]()
     tilt_sc = settle(lead_sc * stats_sc[1]() * gain_sc * (1.0 / slow_count))
     level_sc = settle(lead_sc * bias_sc * (1.0 / slow_count))
     lead_sc = settle(lead_sc)
@@ -880,23 +886,23 @@
 
     bias_sb, gain_sb = slope_pass(sec_sb, stats_sb, dbuf)
 
-    put("sb_back", 0, bias_sb)
-    put("sb_back", 256, gain_sb)
-    exchange_start("sb_back")
+    put(BACK + SLOW_B, 0, bias_sb)
+    put(BACK + SLOW_B, 256, gain_sb)
+    exchange_start(BACK + SLOW_B)
 
     slab_sc[0:cs_n, :] = dot(cs[...], hbs[...], TN)
-    advance("sc")
+    advance(SC)
     widening = None
     for phase in range(4):
         term = dot(hbf[...], cf[rows * phase : rows * (phase + 1), :], TN)[32 * phase : 32 * (phase + 1), :]
         widening = term if widening is None else widening + term
     slab[2, 704:736, 128:256] = widening
     slab[2, 736:768, 128:256] = jnp.zeros((32, LANES), F32)
-    poll(0)
-
-    bias_fb, gain_fb = unpair32(exchange_end("fb_back"))
-    report("fb", bias_fb, gain_fb)
-    vec_fb = back_vectors("fb", stats_fb, bias_fb, gain_fb, fast_count)
+    poll()
+
+    bias_fb, gain_fb = unpair32(exchange_end(BACK + FB))
+    report(FB, bias_fb, gain_fb)
+    vec_fb = back_vectors(FB, stats_fb, bias_fb, gain_fb, fast_count)
 
     def norm_grad(buffer, section, at, vectors):
         lead, level, tilt = vectors
@@ -916,20 +922,22 @@
         dbuf_f[rows_at(i, half), :] = value
 
     loop(2, back_fb)
+    poll()
     bias_fa, gain_fa = slope_pass(sec_fa, stats_fa, dbuf_f)
-    put("fa_back", 0, pair32(bias_fa, gain_fa))
-    exchange_start("fa_back")
-    poll(1)
-    total = exchange_end("sb_back")
+    put(BACK + FA, 0, pair32(bias_fa, gain_fa))
+    exchange_start(BACK + FA)
+    poll()
+    total = exchange_end(BACK + SLOW_B)
 
     bias_sb, gain_sb = take(total, 0, 256), take(total, 256, 256)
-    report("sb", bias_sb, gain_sb)
-    vec_sb = back_vectors("sb", stats_sb, bias_sb, gain_sb, slow_count)
+    report(SLOW_B, bias_sb, gain_sb)
+    vec_sb = back_vectors(SLOW_B, stats_sb, bias_sb, gain_sb, slow_count)
 
     def low_sb(i):
         spread_columns(gcs, i, norm_grad(dbuf, sec_sb, rows_at(i, band), vec_sb))
 
     loop(bands, low_sb, unroll=2)
+    poll()
 
     def back_sb(i):
         value = None
@@ -941,22 +949,23 @@
                 value = term if value is None else value + term
         dbuf[rows_at(i, half), :] = value
 
-    loop(2, back_sb)
-    poll(2)
+    for part in range(2):
+        back_sb(part)
+        poll()
     bias_sa, gain_sa = slope_pass(sec_sa, stats_sa, dbuf)
 
-    put("sa_back", 0, bias_sa)
-    put("sa_back", 256, gain_sa)
-    exchange_start("sa_back")
-    poll(3)
+    put(BACK + SLOW_A, 0, bias_sa)
+    put(BACK + SLOW_A, 256, gain_sa)
+    exchange_start(BACK + SLOW_A)
+    poll()
 
     for a in range(3):
         value = dot(gcs[band : band + rows, bs : 2 * bs], hcs[band * a : band * a + rows, :], TN)
-        ref, lane = pieces["sb%d" % a]["ref"], pieces["sb%d" % a]["lane"]
+        ref, lane = pieces[SB + a].ref, pieces[SB + a].lane
         for b in range(3):
             ref[bs * b : bs * (b + 1), lane : lane + bs] = value[:, bs * b : bs * (b + 1)]
-        advance("sb%d" % a)
-    poll(4)
+        advance(SB + a)
+        poll()
     for a in range(3):
         value = dot(gcf[band : band + rows, 128:256], hcf[band * a : band * a + rows, :], TN)
         for b in range(3):
@@ -966,10 +975,10 @@
             folded = jnp.where(lane_groups(32) == tap % 4, folded, 0.0)
             at = slice(608 + 32 * (tap // 4), 640 + 32 * (tap // 4))
             slab[2, at, 128:256] = folded if tap % 4 == 0 else slab[2, at, 128:256] + folded
-    poll(5)
-    bias_fa, gain_fa = unpair32(exchange_end("fa_back"))
-    report("fa", bias_fa, gain_fa)
-    vec_fa = back_vectors("fa", stats_fa, bias_fa, gain_fa, fast_count)
+    poll()
+    bias_fa, gain_fa = unpair32(exchange_end(BACK + FA))
+    report(FA, bias_fa, gain_fa)
+    vec_fa = back_vectors(FA, stats_fa, bias_fa, gain_fa, fast_count)
 
     def low_fa(i):
         at = rows_at(i, band)
@@ -983,13 +992,13 @@
             term = value[32 * phase : 32 * (phase + 1), 128 * (phase + k) : 128 * (phase + k + 1)]
             piece = term if piece is None else piece + term
         slab[2, 512 + 32 * k : 544 + 32 * k, 128:256] = piece
-    poll(6)
-    total = exchange_end("sa_back")
-    poll(7)
+    poll()
+    total = exchange_end(BACK + SLOW_A)
+    poll()
 
     bias_sa, gain_sa = take(total, 0, 256), take(total, 256, 256)
-    report("sa", bias_sa, gain_sa)
-    vec_sa = back_vectors("sa", stats_sa, bias_sa, gain_sa, slow_count)
+    report(SLOW_A, bias_sa, gain_sa)
+    vec_sa = back_vectors(SLOW_A, stats_sa, bias_sa, gain_sa, slow_count)
     def low_sa(i):
         at = rows_at(i, band)
         value = norm_grad(dbuf, sec_sa, at, vec_sa)
@@ -998,35 +1007,37 @@
         gcs[at, 2 * bs :] = roll_frames(value, following(256), 1, True).astype(BF16)
 
     loop(bands, low_sa, unroll=2)
+    poll()
 
     def narrow_gradient(k):
-        ref, lane = pieces["sa%d" % k]["ref"], pieces["sa%d" % k]["lane"]
+        ref, lane = pieces[SA + k].ref, pieces[SA + k].lane
         source = xs[:, 256 * k : 256 * (k + 1)] if k < 4 else jl[...]
         ref[0 : 3 * bs, lane : lane + 256] = dot(gcs[0:rows, :], source, TN)
-        advance("sa%d" % k)
+        advance(SA + k)
 
     narrow_gradient(0)
-    poll(8)
+    poll()
 
     def back_lateral(i):
         at = rows_at(i, half)
         dbuf[at, :] = dot(gcs[at, :], wsa[:, cs_n:], NN)
 
     loop(2, back_lateral)
+    poll()
     bias_lat, gain_lat = slope_pass(sec_lat, stats_lat, dbuf)
-    put("lat_back", 0, bias_lat)
-    put("lat_back", 256, gain_lat)
-    exchange_start("lat_back")
-
-    poll(9)
+    put(BACK + LAT, 0, bias_lat)
+    put(BACK + LAT, 256, gain_lat)
+    exchange_start(BACK + LAT)
+
+    poll()
 
     for k in range(1, 4):
         narrow_gradient(k)
-        poll(9 + k)
-    total = exchange_end("lat_back")
+        poll()
+    total = exchange_end(BACK + LAT)
 
     bias_lat, gain_lat = take(total, 0, 256), take(total, 256, 256)
-    report("lat", bias_lat, gain_lat)
+    report(LAT, bias_lat, gain_lat)
 
     def pack(rows_ref, target):
         lanes = lax.broadcasted_iota(jnp.int32, (24, LANES), 1)
@@ -1038,12 +1049,12 @@
         target[...] = moved * factor
         target[0:1, :] = first * factor
 
-    pack(gain_rows, stage_b.at[pl.ds(0, 16)])
-    pack(bias_rows, stage_b.at[pl.ds(16, 16)])
+    pack(gain_rows, dbuf_f.at[pl.ds(0, 16)])
+    pack(bias_rows, dbuf_f.at[pl.ds(16, 16)])
     parameter_stores = [
-        store(stage_b.at[pl.ds(0, 16)], dgains_h, 19), store(stage_b.at[pl.ds(16, 16)], dbiases_h, 20)
+        store(dbuf_f.at[pl.ds(0, 16)], dgains_h, 19), store(dbuf_f.at[pl.ds(16, 16)], dbiases_h, 20)
     ]
-    vec_lat = back_vectors("lat", stats_lat, bias_lat, gain_lat, slow_count)
+    vec_lat = back_vectors(LAT, stats_lat, bias_lat, gain_lat, slow_count)
 
     def low_lat(i):
         at = rows_at(i, band)
@@ -1054,10 +1065,10 @@
     for k in range(5):
         at, lane = 256 * (k % 3), 128 * (k // 3)
         slab[2, at : at + 256, lane : lane + 128] = value[:, 128 * k : 128 * (k + 1)]
-    advance("lt")
-    poll(13)
+    advance(LT)
+    poll()
     narrow_gradient(4)
-    poll(14)
+    poll()
 
     def slow_back(i):
         at = rows_at(i, half)
@@ -1068,8 +1079,7 @@
 
     for part in range(2):
         slow_back(part)
-        poll(15 + part)
-    sgrad_store = store(gsum, sgrad_h, 12)
+        poll()
 
     fast_store.wait()
 
@@ -1091,30 +1101,37 @@
                 stage_a[pl.ds(phase, band, stride=4), :] = grads[phase][part * band : (part + 1) * band]
             xf[rows_at(2 * i + part, fband), :] = stage_a[...].astype(BF16)
 
-    loop(bands // 4, fast_back)
-    poll(17)
-    loop(bands // 2 - bands // 4, lambda i: fast_back(i + bands // 4))
-    fgrad_store = store(xf, fgrad_h, 13)
-    poll(18)
-
-    poll(19)
+    third = bands // 6
+    loop(third, fast_back)
+    poll()
+    loop(third, lambda i: fast_back(i + third))
+    poll()
+    loop(bands // 2 - 2 * third, lambda i: fast_back(i + 2 * third))
+    poll()
+
+    poll()
     while not all(done(name) for name in order):
         for name in order:
             if not done(name):
                 advance(name)
     for copy in stores + parameter_stores:
         copy.wait()
-    sgrad_store.wait()
-    fgrad_store.wait()
 
 
 def hand_on(*refs):
-    sources, targets, held, small, sem = refs[0:11], refs[11:24], refs[24:35], refs[35:40], refs[40]
-    loads = [pltpu.make_async_copy(sources[k], held[k], sem.at[k]) for k in range(11)]
-    stores = [pltpu.make_async_copy(held[k], targets[k], sem.at[11 + k]) for k in range(8)]
-    stores += [pltpu.make_async_copy(small[k], targets[8 + k], sem.at[19 + k]) for k in range(5)]
-    for k in (8, 9, 10, 0, 1, 2, 3, 4, 5, 6, 7):
-        loads[k].start()
+    sources, targets, staged, small, sem = refs[0:11], refs[11:24], refs[24:31], refs[31:36], refs[36]
+    held = staged[0:2] + sources[2:6] + staged[2:7]
+    loads = {k: pltpu.make_async_copy(sources[k], held[k], sem.at[k]) for k in (8, 9, 10, 0, 1, 6, 7)}
+    stores = {k: pltpu.make_async_copy(held[k], targets[k], sem.at[11 + k]) for k in (0, 1, 2, 3, 5, 6, 7)}
+    for k in range(5):
+        stores[8 + k] = pltpu.make_async_copy(small[k], targets[8 + k], sem.at[19 + k])
+        stores[13 + k] = pltpu.make_async_copy(
+            held[4].at[pl.ds(768 * k, 768)], targets[4].at[:, pl.ds(256 * k, 256)], sem.at[24 + k]
+        )
+    for copy in loads.values():
+        copy.start()
+    for k in (2, 3, 5, 13, 14, 15, 16, 17):
+        stores[k].start()
     for k in (8, 9, 10):
         loads[k].wait()
     small[0][...] = held[8][0:96, :]
@@ -1127,12 +1144,12 @@
         for row in range(16):
             width = min(LANES, count - row * LANES)
             target[pl.ds(row * LANES, width)] = source[row : row + 1, 0:width].reshape(width)
-    for copy in stores[8:13]:
-        copy.start()
-    for load, copy in zip(loads[0:8], stores[0:8]):
-        load.wait()
-        copy.start()
-    for copy in stores:
+    for k in range(8, 13):
+        stores[k].start()
+    for k in (0, 1, 6, 7):
+        loads[k].wait()
+        stores[k].start()
+    for copy in stores.values():
         copy.wait()
 
 
@@ -1187,31 +1204,29 @@
 
     out_shape = [
         shape((rows, channels), BF16), shape((4 * rows, cf), BF16),
-        shape((rows, channels), BF16), shape((4 * rows, cf), BF16),
-        shape((3 * bs, channels + bs), F32), shape((9 * bs, bs), F32), shape((channels, bs), F32),
+        pltpu.VMEM((rows, channels), BF16), pltpu.VMEM((4 * rows, cf), BF16),
+        pltpu.VMEM((15 * bs, bs), F32), pltpu.VMEM((9 * bs, bs), F32), shape((channels, bs), F32),
         shape((5 * bs, cf), F32), shape((256, cf), F32), shape((16, LANES), F32), shape((16, LANES), F32),
         shape((10, max(high // 4, 1), 32, 256), F32),
     ]
     scratch = [
         pltpu.VMEM((rows, channels), BF16), pltpu.VMEM((rows, channels), BF16),
-        pltpu.VMEM((rows, channels), BF16), pltpu.VMEM((4 * rows, cf), BF16),
         pltpu.VMEM((4 * rows, cf), BF16), pltpu.VMEM((rows, channels), F32),
         pltpu.VMEM((rows, 512), F32), pltpu.VMEM((rows, 512), F32),
         pltpu.VMEM((pad, 3 * bs), BF16), pltpu.VMEM((pad, 3 * bs), BF16),
         pltpu.VMEM((pad, 384), BF16), pltpu.VMEM((pad, 384), BF16),
-        pltpu.VMEM((rows, bs), F32), pltpu.VMEM((rows, bs), F32), pltpu.VMEM((rows, bs), F32),
-        pltpu.VMEM((rows, bs), F32),
+        pltpu.VMEM((rows, bs), F32), pltpu.VMEM((rows, bs), F32),
         pltpu.VMEM((rows, 128), F32), pltpu.VMEM((rows, 128), F32), pltpu.VMEM((rows, 128), F32),
         pltpu.VMEM((rows, bs), BF16), pltpu.VMEM((rows, bs), BF16), pltpu.VMEM((rows, 128), BF16),
         pltpu.VMEM((rows, 896), BF16), pltpu.VMEM((3, 1512, 256), F32), pltpu.VMEM((2016, 256), F32),
-        pltpu.VMEM((768, 256), F32), pltpu.VMEM((max(high // 4, 1), 32, 256), F32),
+        pltpu.VMEM((768, 256), F32),
         pltpu.VMEM((3 * bs, channels + bs), BF16), pltpu.VMEM((9 * bs, bs), BF16),
         pltpu.VMEM((channels, bs), BF16), pltpu.VMEM(norm_gains.shape, F32), pltpu.VMEM(norm_gains.shape, F32),
-        pltpu.VMEM((72, 8, channels), F32), pltpu.VMEM((2, 8, 256), F32),
+        pltpu.VMEM((9, 8, channels), F32), pltpu.VMEM((2, 8, 256), F32),
         pltpu.VMEM((96, cf), BF16), pltpu.VMEM((288, 32), BF16), pltpu.VMEM((32, cf), BF16),
         pltpu.VMEM((bs, 640), BF16), pltpu.VMEM((128, 768), BF16),
         pltpu.VMEM((3, 128, 384), BF16), pltpu.VMEM((3, 384, 128), BF16), pltpu.VMEM((512, 128), BF16),
-        pltpu.VMEM((4 * band, cf), F32), pltpu.VMEM((4 * band, cf), F32),
+        pltpu.VMEM((4 * band, cf), F32),
         pltpu.VMEM((24, LANES), F32), pltpu.VMEM((24, LANES), F32),
         pltpu.VMEM((near_low * n_rep, 1, sum(TURNS.values())), F32),
         pltpu.VMEM((max(n_dp // near_low, 1), 1, sum(TURNS.values())), F32),
@@ -1224,10 +1239,10 @@
         functools.partial(kernel, (n_dp, n_rep, low, frames, side, float(slow_count), float(fast_count), factor)),
         out_shape=out_shape,
         in_specs=[any_spec] * 4 + [pl.BlockSpec(memory_space=pltpu.SMEM)] + [any_spec] * 9,
-        out_specs=[any_spec] * 12,
+        out_specs=[any_spec] * 2 + [vmem_spec] * 4 + [any_spec] * 6,
         scratch_shapes=scratch,
         compiler_params=pltpu.CompilerParams(
-            collective_id=0, has_side_effects=True, vmem_limit_bytes=65000 * 2**10
+            collective_id=0, has_side_effects=True, vmem_limit_bytes=54528 * 2**10
         ),
     )(
         flat(slow_input), flat(fast_input), flat(slow_cotangent), flat(fast_cotangent), clip_ids,
@@ -1235,19 +1250,20 @@
         lateral_conv.reshape(-1, cf), slow_narrow.reshape(3 * bs, -1), slow_spatial.reshape(9 * bs, bs),
         slow_widen, norm_gains, norm_biases,
     )
-    final = out_shape[0:8] + [
+    final = [shape((rows, channels), BF16), shape((4 * rows, cf), BF16)] * 2 + [
+        shape((3 * bs, channels + bs), F32), shape((9 * bs, bs), F32), *out_shape[6:8],
         shape((96, cf), F32), shape((288, 32), F32), shape((32, cf), F32),
         shape(norm_gains.shape, F32), shape(norm_gains.shape, F32),
     ]
     handed = pl.pallas_call(
         hand_on,
         out_shape=final,
-        in_specs=[any_spec] * 11,
+        in_specs=[any_spec] * 2 + [vmem_spec] * 4 + [any_spec] * 5,
         out_specs=[any_spec] * 13,
-        scratch_shapes=[pltpu.VMEM(item.shape, item.dtype) for item in out_shape[0:11] + final[8:13]]
-        + [pltpu.SemaphoreType.DMA((24,))],
-        compiler_params=pltpu.CompilerParams(vmem_limit_bytes=64000 * 2**10),
-    )(*results[0:11])
+        scratch_shapes=[pltpu.VMEM(item.shape, item.dtype) for item in out_shape[0:2] + out_shape[6:11] + final[8:13]]
+        + [pltpu.SemaphoreType.DMA((29,))],
+        compiler_params=pltpu.CompilerParams(vmem_limit_bytes=54528 * 2**10),
+    )(*results[0:2], *[pltpu.with_memory_space_constraint(r, pltpu.VMEM) for r in results[2:6]], *results[6:11])
     slow_out, fast_out, slow_grad, fast_grad, dsa, dsb, dsc, dl, dfa, dfb, dfc, dgains, dbiases = handed
 
     return (

time: 141 us -> 137 us (0.972)
  Pallas kernels: 140 us -> 136 us
    pallas_call x1, Pallas kernels: 12.1 us -> 8.87 us  [body(): pl.pallas_call(hand_on, out_shape=final, in_specs=[any_spec] * 2 + [vmem_...]
where the time goes in v5:
time: 137 us
  Pallas kernels  136 us (99%)
    pallas_call x1, Pallas kernels, body(): pl.pallas_call(functools.partial(kernel, (n_dp, n_rep, low, frames, side,...  128 us
    pallas_call x1, Pallas kernels, body(): pl.pallas_call(hand_on, out_shape=final, in_specs=[any_spec] * 2 + [vmem_...  8.87 us

profile of v5, /device:TPU:0, one launch (start us, length us, event | category | flops | bytes accessed | tf_op | source)
XLA Modules:
  0.0 137.3 jit_solution(1664947775597756572)
XLA Ops:
  0.7 127.6 %shard_map.237 = (bf16[1568,1024]{1,0:T(8,128)(2,1)}, bf16[6272,128]{1,0:T(8,128)(2,1)}, bf16[1568,1024]{1,0:T(8,128)(2,1)S(1)}, bf16[6272,128]{1,0:T(8,128)(2,1...) custom-call(bf16[1568,1024]{1,0:T(8,128)(2,1)} %bitcast.36, ...), custom_call_target="tpu_custom_call" | custom-call | tf_op jit(solution)/shard_map/pallas_call | solution.py:1238
  128.3 8.9 %shard_map.238 = (bf16[1568,1024]{1,0:T(8,128)(2,1)}, bf16[6272,128]{1,0:T(8,128)(2,1)}, bf16[1568,1024]{1,0:T(8,128)(2,1)}, bf16[6272,128]{1,0:T(8,128)(2,1)}, ...) custom-call(bf16[1568,1024]{1,0:T(8,128)(2,1)} %get-tuple-element.37, ...), custom_call_target="tpu_custom_call" | custom-call | tf_op jit(solution)/shard_map/pallas_call | solution.py:1258

commit v6 on v5

--- a/solution.py
+++ b/solution.py
@@ -33,7 +33,7 @@
 HALVES = ((C, X, Y, Z0, Z1), (C, Y, X, Z0, Z1))
 BETWEEN = ((C, X, Z0, Z1, Y), (C, Y, Z0, Z1, X))
 LINE = ((C, Z0, Z1, X, Y), (C, Z0, Z1, Y, X))
-ORDER_OF = (PLANE, HALVES, HALVES, PLANE, LINE, HALVES, HALVES, BETWEEN, PLANE, PLANE)
+ORDER_OF = (PLANE, HALVES, LINE, PLANE, BETWEEN, PLANE, HALVES, HALVES, PLANE, PLANE)
 POLLS = (
     (),
     (0,),
@@ -51,21 +51,21 @@
     (),
     (),
     (1,),
-    (),
-    (2, 4),
-    (3, 0, 1, 5),
-    (2, 6),
-    (3, 7),
-    (5, 4, 9),
-    (),
-    (6, 2, 0, 1, 8),
-    (7,),
-    (5,),
-    (3,),
+    (4,),
+    (3, 2),
+    (1, 5),
+    (4, 0, 6),
+    (3, 7, 1),
+    (5, 2, 9),
+    (6, 4, 8),
+    (7, 0),
+    (5, 3, 2),
+    (1,),
+    (9,),
     (
-        9, 4, 2, 7, 0, 8, 5, 6, 4, 1, 2, 9, 7, 3, 6, 5, 0, 1, 4, 2, 7, 3, 9, 5,
-        4, 6, 0, 1, 7, 8, 2, 9, 6, 3, 5, 4, 1, 9, 7, 8, 6, 3, 2, 5, 2, 4, 9, 1,
-        7, 8, 1, 6, 5, 8, 4, 5, 9, 4, 7, 6, 7, 8, 6, 8,
+        6, 5, 4, 7, 6, 3, 8, 1, 9, 5, 4, 7, 6, 2, 1, 3, 9, 5, 8, 7, 4, 6, 2, 1,
+        3, 9, 5, 0, 8, 7, 6, 4, 1, 2, 9, 3, 5, 8, 0, 7, 6, 4, 1, 9, 2, 8, 0, 7,
+        6, 4, 2, 9, 8, 4, 7, 6, 2, 8, 7,
     ),
 )
 
@@ -106,8 +106,8 @@
 def kernel(
     dims,
     xs_h, xf_h, cs_h, cf_h, clip, wfa_h, wfb_h, wfc_h, wl_h, wsa_h, wsb_h, wsc_h, gains_h, biases_h,
-    slow_h, fast_h, gsum, xf, dsa, dsb, dsc_h, dl_h, small_h, dgains_h, dbiases_h, extra_h,
-    xs, cs, cf, big, sec_fc, gsf, hcs, gcs, hcf, gcf,
+    slow_h, cf, gsum, xf, dsa, dsb, dsc_h, dl_h, small_h, dgains_h, dbiases_h, extra_h,
+    xs, cs, big, sec_fc, gsf, hcs, gcs, hcf, gcf,
     sec_lat, dbuf, sec_fa, sec_fb, dbuf_f, jl, hbs, hbf, vx, slab, slab_sc, summed,
     wsa, wsb, wsc, gains_in, biases_in, vectors, masks, wfa_in, wfb_in, wfc_in, wlat, wfa, wfb, wfbk, wfc,
     stage_a, gain_rows, bias_rows, near, far, sum_send, sum_recv, io_sem, own_sem, big_send, big_recv,
@@ -480,10 +480,10 @@
     def bias(name):
         return biases[name]()
 
-    def moments(name, total, squares, count):
+    def moments(name, total, squares, count, *lanes):
         mean = total * (1.0 / count)
         scale = lax.rsqrt(squares * (1.0 / count) - mean * mean + EPS)
-        return settle(mean), settle(scale), settle(0.5 * gain(name) * scale), settle(0.5 * bias(name))
+        return settle(mean), settle(scale), settle(0.5 * gains[name](*lanes) * scale), settle(0.5 * biases[name](*lanes))
 
     def back_vectors(name, stats, bias_total, gain_total, count):
         mean, scale = stats[0](), stats[1]()
@@ -492,8 +492,8 @@
         level = lead * bias_total * (1.0 / count) - mean * tilt
         return settle(lead), settle(level), settle(tilt)
 
-    def report(name, bias_total, gain_total):
-        at = spots[name]
+    def report(name, bias_total, gain_total, skip=0):
+        at = spots[name] + skip
         for piece in range(bias_total.shape[1] // LANES):
             lanes = slice(piece * LANES, (piece + 1) * LANES)
             gain_rows[at + piece : at + piece + 1, :] = gain_total[:, lanes]
@@ -779,31 +779,29 @@
             gsf[at, lanes] = grad
             bias_sum = bias_sum + column_sums(grad)
             gain_sum = gain_sum + column_sums(grad * centred)
-        xf[fat, :] = stage_a[...].astype(BF16)
+        cf[fat, :] = stage_a[...].astype(BF16)
         return bias_sum, gain_sum
 
     bias_fc, gain_fc = loop(bands, finish_fast, zero2(128))
-    fast_store = store(xf, fast_h, 10)
     put(BACK + FC, 0, squash(bias_fc))
     put(BACK + FC, 128, squash(gain_fc) * stats_fc[1]())
     exchange_start(BACK + FC)
     loads["cs"].wait()
     total = exchange_end(SLOW_C)
-    squares = take(total, 256, mid)
+    squares = [take(total, 256, mid)]
     whole = settle(
         lax.dot_general(
             jnp.broadcast_to(take(total, 0, 256), (8, bs)), wsc[...].astype(F32), (NT, ((), ())),
             precision=lax.Precision.HIGHEST, preferred_element_type=F32,
         )[0:1, :]
     )
-    squares = jnp.concatenate([squares, exchange_end(SLOW_C + 1)], axis=1)
-    stats_sc = moments(SLOW_C, whole(), squares, slow_count)
+    stats_sc = []
 
     def finish_slow(part):
         lanes = slice(part * mid, (part + 1) * mid)
         def step(i, carry):
             at = rows_at(i, band)
-            mean, lead, level = [stats_sc[k](lanes) for k in (0, 2, 3)]
+            mean, lead, level = [stats_sc[part][k]() for k in (0, 2, 3)]
             centred = big[at, lanes] - mean
             out, slope = slope_of(0.5 * xs[at, lanes].astype(F32) + (centred * lead + level))
             grad = cs[at, lanes].astype(F32) * slope
@@ -813,9 +811,13 @@
             return carry[0] + column_sums(grad), carry[1] + column_sums(grad * centred)
 
         bias_part, gain_part = loop(bands, step, zero2(mid))
-        return squash(bias_part), squash(gain_part) * stats_sc[1](lanes)
+        return squash(bias_part), squash(gain_part) * stats_sc[part][1]()
 
     for part in range(2):
+        if part:
+            squares.append(exchange_end(SLOW_C + 1))
+        lanes = slice(part * mid, (part + 1) * mid)
+        stats_sc.append(moments(SLOW_C, whole(lanes), squares[part], slow_count, lanes))
         bias_part, gain_part = finish_slow(part)
         put(BACK + SLOW_C + part, 0, bias_part)
         put(BACK + SLOW_C + part, mid, gain_part)
@@ -843,47 +845,48 @@
         for phase in range(4):
             lanes = slice(128 * phase, 128 * (phase + 1))
             value = gsf[at, lanes] * lead_fc() - level_fc() - sec_fc[at, lanes] * tilt_fc()
-            cf[pl.ds(pl.multiple_of(rows * phase + i * band, 16), band), :] = value.astype(BF16)
+            gcs[at, lanes] = value.astype(BF16)
 
     loop(bands, low_fc, unroll=2)
 
     def back_fc(i):
-        value = None
-        for phase in range(4):
-            at = pl.ds(pl.multiple_of(rows * phase + i * half, 16), half)
-            term = dot(cf[at, :], wfc[128 * phase : 128 * (phase + 1), :], NN)
-            value = term if value is None else value + term
-        dbuf_f[rows_at(i, half), :] = value
+        at = rows_at(i, half)
+        dbuf_f[at, :] = dot(gcs[at, 0:512], wfc[...], NN)
 
     loop(2, back_fc)
     bias_fb, gain_fb = slope_pass(sec_fb, stats_fb, dbuf_f)
     put(BACK + FB, 0, pair32(bias_fb, gain_fb))
     exchange_start(BACK + FB)
     slow_store.wait()
-    sums = [exchange_end(BACK + SLOW_C + part) for part in range(2)]
-
-    bias_sc = jnp.concatenate([take(total, 0, mid) for total in sums], axis=1)
-    gain_sc = jnp.concatenate([take(total, mid, mid) for total in sums], axis=1)
-    report(SLOW_C, bias_sc, gain_sc)
-    lead_sc = gain(SLOW_C) * stats_sc[1]()
-    tilt_sc = settle(lead_sc * stats_sc[1]() * gain_sc * (1.0 / slow_count))
-    level_sc = settle(lead_sc * bias_sc * (1.0 / slow_count))
-    lead_sc = settle(lead_sc)
-
-    def low_sc(i):
-        at = rows_at(i, 32)
-        grad = big[at, :]
-        cs[at, :] = (grad * lead_sc() - level_sc() - gsum[at, :].astype(F32) * tilt_sc()).astype(BF16)
-        gsum[at, :] = grad.astype(BF16)
-
-    loop(rows // 32, low_sc, unroll=7)
-
-    def back_sc(i):
-        at = rows_at(i, half)
-        dbuf[at, :] = dot(cs[at, :], wsc[...], NN)
-
-    loop(2, back_sc)
-
+
+    def back_widen(part):
+        lanes = slice(part * mid, (part + 1) * mid)
+        total = exchange_end(BACK + SLOW_C + part)
+        bias_sc, gain_sc = take(total, 0, mid), take(total, mid, mid)
+        report(SLOW_C, bias_sc, gain_sc, part * (mid // LANES))
+        scale = stats_sc[part][1]()
+        lead = gains[SLOW_C](lanes) * scale
+        tilt_sc = settle(lead * scale * gain_sc * (1.0 / slow_count))
+        level_sc = settle(lead * bias_sc * (1.0 / slow_count))
+        lead_sc = settle(lead)
+
+        def low_sc(i):
+            at = rows_at(i, 32)
+            grad = big[at, lanes]
+            cs[at, lanes] = (grad * lead_sc() - level_sc() - gsum[at, lanes].astype(F32) * tilt_sc()).astype(BF16)
+            gsum[at, lanes] = grad.astype(BF16)
+
+        loop(rows // 32, low_sc, unroll=7)
+
+        def back_sc(i):
+            at = rows_at(i, half)
+            value = dot(cs[at, lanes], wsc[lanes, :], NN)
+            dbuf[at, :] = dbuf[at, :] + value if part else value
+
+        loop(2, back_sc)
+
+    for part in range(2):
+        back_widen(part)
     bias_sb, gain_sb = slope_pass(sec_sb, stats_sb, dbuf)
 
     put(BACK + SLOW_B, 0, bias_sb)
@@ -894,7 +897,7 @@
     advance(SC)
     widening = None
     for phase in range(4):
-        term = dot(hbf[...], cf[rows * phase : rows * (phase + 1), :], TN)[32 * phase : 32 * (phase + 1), :]
+        term = dot(hbf[...], gcs[0:rows, 128 * phase : 128 * (phase + 1)], TN)[32 * phase : 32 * (phase + 1), :]
         widening = term if widening is None else widening + term
     slab[2, 704:736, 128:256] = widening
     slab[2, 736:768, 128:256] = jnp.zeros((32, LANES), F32)
@@ -932,6 +935,8 @@
     bias_sb, gain_sb = take(total, 0, 256), take(total, 256, 256)
     report(SLOW_B, bias_sb, gain_sb)
     vec_sb = back_vectors(SLOW_B, stats_sb, bias_sb, gain_sb, slow_count)
+
+    gcs[0:band, :] = jnp.zeros((band, gcs.shape[1]), BF16)
 
     def low_sb(i):
         spread_columns(gcs, i, norm_grad(dbuf, sec_sb, rows_at(i, band), vec_sb))
@@ -1081,7 +1086,6 @@
         slow_back(part)
         poll()
 
-    fast_store.wait()
 
     def fast_back(i):
         at, fat = rows_at(i, 2 * band), rows_at(i, 2 * fband)
@@ -1119,9 +1123,9 @@
 
 
 def hand_on(*refs):
-    sources, targets, staged, small, sem = refs[0:11], refs[11:24], refs[24:31], refs[31:36], refs[36]
-    held = staged[0:2] + sources[2:6] + staged[2:7]
-    loads = {k: pltpu.make_async_copy(sources[k], held[k], sem.at[k]) for k in (8, 9, 10, 0, 1, 6, 7)}
+    sources, targets, staged, small, sem = refs[0:11], refs[11:24], refs[24:30], refs[30:35], refs[35]
+    held = staged[0:1] + sources[1:6] + staged[1:6]
+    loads = {k: pltpu.make_async_copy(sources[k], held[k], sem.at[k]) for k in (8, 9, 10, 0, 6, 7)}
     stores = {k: pltpu.make_async_copy(held[k], targets[k], sem.at[11 + k]) for k in (0, 1, 2, 3, 5, 6, 7)}
     for k in range(5):
         stores[8 + k] = pltpu.make_async_copy(small[k], targets[8 + k], sem.at[19 + k])
@@ -1130,7 +1134,7 @@
         )
     for copy in loads.values():
         copy.start()
-    for k in (2, 3, 5, 13, 14, 15, 16, 17):
+    for k in (1, 2, 3, 5, 13, 14, 15, 16, 17):
         stores[k].start()
     for k in (8, 9, 10):
         loads[k].wait()
@@ -1146,7 +1150,7 @@
             target[pl.ds(row * LANES, width)] = source[row : row + 1, 0:width].reshape(width)
     for k in range(8, 13):
         stores[k].start()
-    for k in (0, 1, 6, 7):
+    for k in (0, 6, 7):
         loads[k].wait()
         stores[k].start()
     for copy in stores.values():
@@ -1203,7 +1207,7 @@
         return jax.ShapeDtypeStruct(dims, dtype)
 
     out_shape = [
-        shape((rows, channels), BF16), shape((4 * rows, cf), BF16),
+        shape((rows, channels), BF16), pltpu.VMEM((4 * rows, cf), BF16),
         pltpu.VMEM((rows, channels), BF16), pltpu.VMEM((4 * rows, cf), BF16),
         pltpu.VMEM((15 * bs, bs), F32), pltpu.VMEM((9 * bs, bs), F32), shape((channels, bs), F32),
         shape((5 * bs, cf), F32), shape((256, cf), F32), shape((16, LANES), F32), shape((16, LANES), F32),
@@ -1211,7 +1215,7 @@
     ]
     scratch = [
         pltpu.VMEM((rows, channels), BF16), pltpu.VMEM((rows, channels), BF16),
-        pltpu.VMEM((4 * rows, cf), BF16), pltpu.VMEM((rows, channels), F32),
+        pltpu.VMEM((rows, channels), F32),
         pltpu.VMEM((rows, 512), F32), pltpu.VMEM((rows, 512), F32),
         pltpu.VMEM((pad, 3 * bs), BF16), pltpu.VMEM((pad, 3 * bs), BF16),
         pltpu.VMEM((pad, 384), BF16), pltpu.VMEM((pad, 384), BF16),
@@ -1239,10 +1243,10 @@
         functools.partial(kernel, (n_dp, n_rep, low, frames, side, float(slow_count), float(fast_count), factor)),
         out_shape=out_shape,
         in_specs=[any_spec] * 4 + [pl.BlockSpec(memory_space=pltpu.SMEM)] + [any_spec] * 9,
-        out_specs=[any_spec] * 2 + [vmem_spec] * 4 + [any_spec] * 6,
+        out_specs=[any_spec] + [vmem_spec] * 5 + [any_spec] * 6,
         scratch_shapes=scratch,
         compiler_params=pltpu.CompilerParams(
-            collective_id=0, has_side_effects=True, vmem_limit_bytes=54528 * 2**10
+            collective_id=0, has_side_effects=True, vmem_limit_bytes=52960 * 2**10
         ),
     )(
         flat(slow_input), flat(fast_input), flat(slow_cotangent), flat(fast_cotangent), clip_ids,
@@ -1258,12 +1262,12 @@
     handed = pl.pallas_call(
         hand_on,
         out_shape=final,
-        in_specs=[any_spec] * 2 + [vmem_spec] * 4 + [any_spec] * 5,
+        in_specs=[any_spec] + [vmem_spec] * 5 + [any_spec] * 5,
         out_specs=[any_spec] * 13,
-        scratch_shapes=[pltpu.VMEM(item.shape, item.dtype) for item in out_shape[0:2] + out_shape[6:11] + final[8:13]]
+        scratch_shapes=[pltpu.VMEM(item.shape, item.dtype) for item in out_shape[0:1] + out_shape[6:11] + final[8:13]]
         + [pltpu.SemaphoreType.DMA((29,))],
-        compiler_params=pltpu.CompilerParams(vmem_limit_bytes=54528 * 2**10),
-    )(*results[0:2], *[pltpu.with_memory_space_constraint(r, pltpu.VMEM) for r in results[2:6]], *results[6:11])
+        compiler_params=pltpu.CompilerParams(vmem_limit_bytes=52960 * 2**10),
+    )(results[0], *[pltpu.with_memory_space_constraint(r, pltpu.VMEM) for r in results[1:6]], *results[6:11])
     slow_out, fast_out, slow_grad, fast_grad, dsa, dsb, dsc, dl, dfa, dfb, dfc, dgains, dbiases = handed
 
     return (

time: 137 us -> 134 us (0.978)
  Pallas kernels: 136 us -> 133 us
    pallas_call x1, Pallas kernels: 128 us -> 125 us  [body(): pl.pallas_call(functools.partial(kernel, (n_dp, n_rep, low, frames, side,...]
where the time goes in v6:
time: 134 us
  Pallas kernels  133 us (99%)
    pallas_call x1, Pallas kernels, body(): pl.pallas_call(functools.partial(kernel, (n_dp, n_rep, low, frames, side,...  125 us
    pallas_call x1, Pallas kernels, body(): pl.pallas_call(hand_on, out_shape=final, in_specs=[any_spec] + [vmem_spec...  7.71 us

profile of v6, /device:TPU:0, one launch (start us, length us, event | category | flops | bytes accessed | tf_op | source)
XLA Modules:
  0.0 133.9 jit_solution(13034688640601525550)
XLA Ops:
  0.7 125.4 %shard_map.237 = (bf16[1568,1024]{1,0:T(8,128)(2,1)}, bf16[6272,128]{1,0:T(8,128)(2,1)S(1)}, bf16[1568,1024]{1,0:T(8,128)(2,1)S(1)}, bf16[6272,128]{1,0:T(8,128)...) custom-call(bf16[1568,1024]{1,0:T(8,128)(2,1)} %bitcast.36, ...), custom_call_target="tpu_custom_call" | custom-call | tf_op jit(solution)/shard_map/pallas_call | solution.py:1242
  126.0 7.7 %shard_map.238 = (bf16[1568,1024]{1,0:T(8,128)(2,1)}, bf16[6272,128]{1,0:T(8,128)(2,1)}, bf16[1568,1024]{1,0:T(8,128)(2,1)}, bf16[6272,128]{1,0:T(8,128)(2,1)}, ...) custom-call(bf16[1568,1024]{1,0:T(8,128)(2,1)} %get-tuple-element.37, ...), custom_call_target="tpu_custom_call" | custom-call | tf_op jit(solution)/shard_map/pallas_call | solution.py:1262

commit v7 on v6

--- a/solution.py
+++ b/solution.py
@@ -789,12 +789,13 @@
     loads["cs"].wait()
     total = exchange_end(SLOW_C)
     squares = [take(total, 256, mid)]
-    whole = settle(
-        lax.dot_general(
-            jnp.broadcast_to(take(total, 0, 256), (8, bs)), wsc[...].astype(F32), (NT, ((), ())),
-            precision=lax.Precision.HIGHEST, preferred_element_type=F32,
-        )[0:1, :]
-    )
+    rest, row = take(total, 0, 256), lax.broadcasted_iota(jnp.int32, (16, bs), 0)
+    parts = jnp.zeros((16, bs), F32)
+    for k in range(3):
+        part_k = rest.astype(BF16).astype(F32)
+        parts = jnp.where(row == k, part_k, parts)
+        rest = rest - part_k
+    whole = settle(squash(dot(parts.astype(BF16), wsc[...], NT)))
     stats_sc = []
 
     def finish_slow(part):
@@ -981,22 +982,6 @@
             at = slice(608 + 32 * (tap // 4), 640 + 32 * (tap // 4))
             slab[2, at, 128:256] = folded if tap % 4 == 0 else slab[2, at, 128:256] + folded
     poll()
-    bias_fa, gain_fa = unpair32(exchange_end(BACK + FA))
-    report(FA, bias_fa, gain_fa)
-    vec_fa = back_vectors(FA, stats_fa, bias_fa, gain_fa, fast_count)
-
-    def low_fa(i):
-        at = rows_at(i, band)
-        hbf[at, :] = norm_grad(dbuf_f, sec_fa, at, vec_fa).astype(BF16)
-
-    loop(bands, low_fa, unroll=2)
-    value = dot(hbf[...], vx[:, 128:896], TN)
-    for k in range(3):
-        piece = None
-        for phase in range(4):
-            term = value[32 * phase : 32 * (phase + 1), 128 * (phase + k) : 128 * (phase + k + 1)]
-            piece = term if piece is None else piece + term
-        slab[2, 512 + 32 * k : 544 + 32 * k, 128:256] = piece
     poll()
     total = exchange_end(BACK + SLOW_A)
     poll()
@@ -1033,6 +1018,22 @@
     put(BACK + LAT, 0, bias_lat)
     put(BACK + LAT, 256, gain_lat)
     exchange_start(BACK + LAT)
+    bias_fa, gain_fa = unpair32(exchange_end(BACK + FA))
+    report(FA, bias_fa, gain_fa)
+    vec_fa = back_vectors(FA, stats_fa, bias_fa, gain_fa, fast_count)
+
+    def low_fa(i):
+        at = rows_at(i, band)
+        hbf[at, :] = norm_grad(dbuf_f, sec_fa, at, vec_fa).astype(BF16)
+
+    loop(bands, low_fa, unroll=2)
+    value = dot(hbf[...], vx[:, 128:896], TN)
+    for k in range(3):
+        piece = None
+        for phase in range(4):
+            term = value[32 * phase : 32 * (phase + 1), 128 * (phase + k) : 128 * (phase + k + 1)]
+            piece = term if piece is None else piece + term
+        slab[2, 512 + 32 * k : 544 + 32 * k, 128:256] = piece
 
     poll()
 

time: 134 us -> 133 us (level)
  no operation moved by 1% of the time
where the time goes in v7:
time: 133 us
  Pallas kernels  132 us (99%)
    pallas_call x1, Pallas kernels, body(): pl.pallas_call(functools.partial(kernel, (n_dp, n_rep, low, frames, side,...  124 us
    pallas_call x1, Pallas kernels, body(): pl.pallas_call(hand_on, out_shape=final, in_specs=[any_spec] + [vmem_spec...  7.71 us

profile of v7, /device:TPU:0, one launch (start us, length us, event | category | flops | bytes accessed | tf_op | source)
XLA Modules:
  0.0 132.9 jit_solution(5946168181385936692)
XLA Ops:
  0.7 124.4 %shard_map.237 = (bf16[1568,1024]{1,0:T(8,128)(2,1)}, bf16[6272,128]{1,0:T(8,128)(2,1)S(1)}, bf16[1568,1024]{1,0:T(8,128)(2,1)S(1)}, bf16[6272,128]{1,0:T(8,128)...) custom-call(bf16[1568,1024]{1,0:T(8,128)(2,1)} %bitcast.36, ...), custom_call_target="tpu_custom_call" | custom-call | tf_op jit(solution)/shard_map/pallas_call | solution.py:1243
  125.1 7.7 %shard_map.238 = (bf16[1568,1024]{1,0:T(8,128)(2,1)}, bf16[6272,128]{1,0:T(8,128)(2,1)}, bf16[1568,1024]{1,0:T(8,128)(2,1)}, bf16[6272,128]{1,0:T(8,128)(2,1)}, ...) custom-call(bf16[1568,1024]{1,0:T(8,128)(2,1)} %get-tuple-element.37, ...), custom_call_target="tpu_custom_call" | custom-call | tf_op jit(solution)/shard_map/pallas_call | solution.py:1263

commit v8 on v7

--- a/solution.py
+++ b/solution.py
@@ -654,24 +654,20 @@
         sec_fb[rows_at(i, half), :] = value
         return carry[0] + column_sums(value), carry[1] + column_sums(value * value)
 
-    def narrow_lateral(i):
+    def combine_sa(i, carry):
         at = rows_at(i, half)
-        for k in range(3):
-            big[at, bs * k : bs * (k + 1)] += dot(jl[at, :], wsa[bs * k : bs * (k + 1), cs_n:], NT)
-
-    loop(2, narrow_lateral)
-
-    def combine_sa(i, carry):
-        at = rows_at(i, band)
-        value = (
-            big[at, bs : 2 * bs]
-            + roll_frames(big[at, 0:bs], prev(256), 1, False)
-            + roll_frames(big[at, 2 * bs : 3 * bs], following(256), -1, False)
-        )
+
+        def tap(k):
+            lanes = slice(bs * k, bs * (k + 1))
+            return big[at, lanes] + dot(jl[at, :], wsa[lanes, cs_n:], NT)
+
+        value = roll_frames(tap(0), prev(256), 1, False)
+        value = value + tap(1)
+        value = value + roll_frames(tap(2), following(256), -1, False)
         sec_sa[at, :] = value
         return carry[0] + column_sums(value), carry[1] + column_sums(value * value)
 
-    sum_sa, sq_sa = loop(bands, combine_sa, zero2(256))
+    sum_sa, sq_sa = loop(2, combine_sa, zero2(256))
     put(SLOW_A, 0, squash(sum_sa))
     put(SLOW_A, 256, squash(sq_sa))
     exchange_start(SLOW_A)

time: 133 us -> 133 us (level)
  no operation moved by 1% of the time
where the time goes in v8:
time: 133 us
  Pallas kernels  132 us (99%)
    pallas_call x1, Pallas kernels, body(): pl.pallas_call(functools.partial(kernel, (n_dp, n_rep, low, frames, side,...  124 us
    pallas_call x1, Pallas kernels, body(): pl.pallas_call(hand_on, out_shape=final, in_specs=[any_spec] + [vmem_spec...  7.71 us

profile of v8, /device:TPU:0, one launch (start us, length us, event | category | flops | bytes accessed | tf_op | source)
XLA Modules:
  0.0 132.9 jit_solution(17910057457399214100)
XLA Ops:
  0.7 124.4 %shard_map.237 = (bf16[1568,1024]{1,0:T(8,128)(2,1)}, bf16[6272,128]{1,0:T(8,128)(2,1)S(1)}, bf16[1568,1024]{1,0:T(8,128)(2,1)S(1)}, bf16[6272,128]{1,0:T(8,128)...) custom-call(bf16[1568,1024]{1,0:T(8,128)(2,1)} %bitcast.36, ...), custom_call_target="tpu_custom_call" | custom-call | tf_op jit(solution)/shard_map/pallas_call | solution.py:1239
  125.0 7.7 %shard_map.238 = (bf16[1568,1024]{1,0:T(8,128)(2,1)}, bf16[6272,128]{1,0:T(8,128)(2,1)}, bf16[1568,1024]{1,0:T(8,128)(2,1)}, bf16[6272,128]{1,0:T(8,128)(2,1)}, ...) custom-call(bf16[1568,1024]{1,0:T(8,128)(2,1)} %get-tuple-element.37, ...), custom_call_target="tpu_custom_call" | custom-call | tf_op jit(solution)/shard_map/pallas_call | solution.py:1259
